TPU v7x, 128 devices: a whole 4x4x4 slice. The times are simulated.
128 devices in a mesh: sec: 8 (over z_hi, y), dev: 16 (over x, z_lo, core).
Axes of the slice: x: 4, y: 4, z: 4 (z_hi: 2, z_lo: 2; z = z_hi * 2 + z_lo), core: 2. Of those that a mesh axis runs over, the one named last changes fastest.
Arguments:
- child_panel: bfloat16 [8, 6144, 2048], P('sec', 'dev'), may hold values from -0.23925781 to 0.23925781
- child_inverse: bfloat16 [8, 2048, 2048], P('sec'), may hold values from -0.03756505 to 1.5, as said below
- child_map: int32 [8, 48], replicated, may hold values from 0 to 63, as said below
- parent_front: bfloat16 [8192, 8192], P('sec', 'dev'), may hold values from -6 to 6
- parent_inverse: bfloat16 [1024, 1024], replicated, may hold values from -0.00166015625 to 0.046875, as said below
- parent_pivots: int32 [8], replicated, may hold values from 0 to 63, as said below
Outputs:
- parent_update: float32 [8192, 8192], P('sec', 'dev')
- parent_factor: bfloat16 [8192, 1024], P('sec')
Inputs may be any that keep to these rules, and one draw needn't show every extreme that they name: `child_map`: each row names 48 different parent blocks. `parent_pivots`: 8 different parent blocks. `child_inverse`: upper triangular with positive diagonal. `parent_inverse`: upper triangular with positive diagonal.
All inputs are finite; a program needn't handle non-finite values.
Results may differ from a plain program's by a relative error of at most 0.014.
Values may be sent and summed in bfloat16 or wider, within the bound.
No kernel may reach another device: no remote copies, remote signals or barrier semaphores. Data moves between devices by JAX's collectives and lax.ppermute only.
A program may use at most 128 MiB of HBM per device.

v0:
```python
import jax
import jax.numpy as jnp
from jax import lax
from jax.sharding import PartitionSpec as P

BLK = 128
PORD = 8192


def split_up(array, dim, size):
    lengths = array.shape
    tiles = array.reshape(*lengths[:dim], size, lengths[dim] // size, *lengths[dim + 1 :])
    return jnp.moveaxis(tiles, dim, 0)


def sum_at_owner(array, axis, dim):
    tiles = split_up(array, dim, lax.axis_size(axis))
    arrived = lax.all_to_all(tiles, axis, split_axis=0, concat_axis=0, tiled=True)
    return arrived.astype(jnp.float32).sum(axis=0)


def from_everyone(array, axis):
    copies = jnp.broadcast_to(array, (lax.axis_size(axis), *array.shape))
    return lax.all_to_all(copies, axis, split_axis=0, concat_axis=0, tiled=True)


def joined_along(tiles, dim):
    tiles = jnp.moveaxis(tiles, 0, dim)
    lengths = tiles.shape
    return tiles.reshape(*lengths[:dim], lengths[dim] * lengths[dim + 1], *lengths[dim + 2 :])


def collect(array, axis, dim):
    tiles = from_everyone(array, axis)
    return joined_along(tiles, dim)


def spread_2(value, axis, source):
    kept = jnp.where(lax.axis_index(axis) == source, value, 0).astype(value.dtype)
    return lax.psum(kept, axis)


def outer_rows(left_rows, right_rows):
    return lax.dot_general(
        left_rows, right_rows, (((1,), (1,)), ((), ())), preferred_element_type=jnp.float32
    )


def local(child_panel, child_inverse, child_map, parent_front, parent_inverse, parent_pivots):
    dev_count = lax.axis_size("dev")
    sec_count = lax.axis_size("sec")
    sec_index = lax.axis_index("sec")
    dev_index = lax.axis_index("dev")
    block_count = PORD // BLK
    cols_dev = block_count // dev_count
    rows_sec = block_count // sec_count
    col_width = cols_dev * BLK
    my_map = lax.dynamic_index_in_dim(child_map, sec_index, 0, keepdims=False)
    child_blocks = my_map.shape[0]
    place_map = (my_map[:, None] == jnp.arange(block_count, dtype=jnp.int32)[None, :]).astype(
        jnp.bfloat16
    )
    lower_rows = jnp.dot(
        child_panel[0], child_inverse[0], preferred_element_type=jnp.float32
    ).astype(jnp.bfloat16)
    col_targets = dev_index * cols_dev + jnp.arange(cols_dev, dtype=jnp.int32)
    whole_rows = lax.all_gather(lower_rows, "dev", axis=0, tiled=True)
    pick_cols = (my_map[None, :] == col_targets[:, None]).astype(jnp.bfloat16)
    chosen = jnp.einsum(
        "mj,jbp->mbp",
        pick_cols,
        whole_rows.reshape(child_blocks, BLK, -1),
        preferred_element_type=jnp.float32,
    ).astype(jnp.bfloat16)
    by_columns = (-outer_rows(whole_rows, chosen.reshape(col_width, -1))).astype(jnp.bfloat16)
    spread = jnp.einsum(
        "jm,jbc->mbc",
        place_map,
        by_columns.reshape(child_blocks, BLK, col_width),
        preferred_element_type=jnp.float32,
    ).reshape(PORD, col_width)
    summed = lax.psum_scatter(
        spread.astype(jnp.bfloat16), "sec", scatter_dimension=0, tiled=True
    ).astype(jnp.float32)
    assembled = parent_front.astype(jnp.float32) + summed
    panel_values = assembled.astype(jnp.bfloat16)
    pivot_blocks = parent_pivots.shape[0]
    pick_pivots = (parent_pivots[None, :] == col_targets[:, None]).astype(jnp.bfloat16)
    selected = jnp.einsum(
        "mr,rbk->mbk",
        pick_pivots,
        parent_inverse.reshape(pivot_blocks, BLK, -1),
        preferred_element_type=jnp.float32,
    ).astype(jnp.bfloat16)
    partial_sum = jnp.dot(
        panel_values, selected.reshape(col_width, -1), preferred_element_type=jnp.float32
    )
    row_share = sum_at_owner(partial_sum.astype(jnp.bfloat16), "dev", 0).astype(jnp.bfloat16)
    parent_factor = collect(row_share, "dev", 0)
    my_blocks = sec_index * rows_sec + jnp.arange(rows_sec, dtype=jnp.int32)
    is_pivot = jnp.any(parent_pivots[None, :] == my_blocks[:, None], axis=1)
    row_pivot = jnp.repeat(is_pivot, BLK)
    trailing = jnp.where(row_pivot[:, None], jnp.zeros_like(parent_factor), parent_factor)
    offset = dev_index * cols_dev % rows_sec * BLK
    root_sec = dev_index * cols_dev // rows_sec
    column_rows = lax.dynamic_slice_in_dim(trailing, offset, col_width, 0)
    column_factor = spread_2(column_rows, "sec", root_sec)
    parent_update = assembled - outer_rows(trailing, column_factor)
    return (parent_update, parent_factor)


def solution(mesh):
    placed = (P("sec", "dev", None), P("sec", None, None), P(), P("sec", "dev"), P(), P())
    return jax.shard_map(
        local,
        mesh=mesh,
        in_specs=placed,
        out_specs=(P("sec", "dev"), P("sec", None)),
        check_vma=False,
    )
```

profile of v0, /device:TPU:18, one launch (start us, length us, event | category | flops | bytes accessed | tf_op | source)
XLA Modules:
  0.0 530.4 jit_solution(7044709101146843825)
XLA Ops:
  7.2 0.0 all-gather.2.cloned.1.call-start
  7.2 8.5 %fusion.8 = bf16[384,2048]{1,0:T(8,128)(2,1)} fusion(bf16[1,2048,2048]{2,1,0:T(8,128)(2,1)} %param.7, bf16[1,384,2048]{2,1,0:T(8,128)(2,1)} %param.6), kind=kOutput, calls=%fused_computation.8 | convolution fusion | flops 3222011904 | bytes 11534336 | tf_op jit(solution)/shard_map/dot_general | solution.py:63
  15.8 0.0 all-gather.2.cloned.1.call-update
  15.8 0.0 reduce-scatter.2.cloned.1.call-start
  15.9 0.7 dynamic-slice_bitcast_fusion
  16.6 132.4 %all-gather.2.cloned.1.call-done = bf16[6144,2048]{1,0:T(8,128)(2,1)} async-done(((bf16[384,2048]{1,0:T(8,128)(2,1)}), bf16[6144,2048]{1,0:T(8,128)(2,1)}) %all-gather.2.cloned.1.call-update) | async-done | bytes 25165840 | tf_op jit(solution)/shard_map/all_gather | solution.py:67
  148.9 52.3 %fusion.5 = bf16[4,128,2048]{2,0,1:T(4,128)(2,1)S(1)} fusion(bf16[48,128,2048]{2,1,0:T(8,128)(2,1)} %bitcast.37, s32[48]{0:T(128)S(1)} %dynamic-slice_bitcast_fusion, s32[4]{0:T(128)S(1)} %iota_add_fusion.1), kind=kOutput, calls=%fused_computation.7 | convolution fusion | flops 101712064 | bytes 27263184 | tf_op jit(solution)/shard_map/mj,jbp->mbp/dot_general | solution.py:69
  201.3 2.5 copy.18
  203.8 18.9 %negate_convert_fusion = bf16[6144,512]{1,0:T(8,128)(2,1)S(1)} fusion(bf16[6144,2048]{1,0:T(8,128)(2,1)} %all-gather.2.cloned.1.call-done, bf16[512,2048]{1,0:T(8,128)(2,1)} %bitcast.39), kind=kOutput, calls=%fused_computation.2 | convolution fusion | flops 12891193344 | bytes 33554432 | tf_op jit(solution)/shard_map/dot_general | solution.py:44
  222.6 8.4 %convolution_convert_fusion = bf16[64,128,512]{2,0,1:T(8,128)(2,1)} fusion(bf16[48,128,512]{2,1,0:T(8,128)(2,1)S(1)} %bitcast.38, s32[48]{0:T(128)S(1)} %dynamic-slice_bitcast_fusion), kind=kOutput, calls=%fused_computation.5 | convolution fusion | flops 406850560 | bytes 14680256 | tf_op jit(solution)/shard_map/jm,jbc->mbc/dot_general | solution.py:76
  231.0 11.3 %copy.20 = bf16[64,128,512]{2,1,0:T(8,128)(2,1)} copy(bf16[64,128,512]{2,0,1:T(8,128)(2,1)} %convolution_convert_fusion) | data formatting | bytes 16777216 | tf_op jit(solution)/shard_map/convert_element_type | solution.py:83
  242.3 0.0 reduce-scatter.2.cloned.1.call-update
  242.4 0.6 copy-done.2
  243.0 1.4 fusion.16
  244.5 0.3 copy.22
  244.8 111.8 %reduce-scatter.2.cloned.1.call-done = bf16[1024,512]{1,0:T(8,128)(2,1)} async-done(((bf16[8192,512]{1,0:T(8,128)(2,1)}), bf16[1024,512]{1,0:T(8,128)(2,1)}) %reduce-scatter.2.cloned.1.call-update) | async-done | bytes 1048592 | tf_op jit(solution)/shard_map/reduce_scatter | solution.py:82
  356.5 3.0 convolution_convert_fusion.1
  359.6 30.2 %all_to_all.10 = bf16[16,64,1024]{2,1,0:T(8,128)(2,1)} all-to-all(bf16[16,64,1024]{2,1,0:T(8,128)(2,1)S(1)} %bitcast.40), channel_id=1, replica_groups=mesh['sec'=8,'dev'=16] {'dev'}, dimensions={0} | all-to-all | bytes 4194304 | tf_op jit(solution)/shard_map/all_to_all | solution.py:18
  389.7 2.0 reduce_sum.12
  391.7 1.6 broadcast_in_dim.35
  393.3 6.7 %all-to-all-start.1 = ((bf16[16,64,1024]{2,1,0:T(8,128)(2,1)}), bf16[16,64,1024]{2,1,0:T(8,128)(2,1)}, u32[]{:S(2)}, u32[]{:S(2)}) async-start(bf16[16,64,1024]{2,1,0:T(8,128)(2,1)} %broadcast_in_dim.35), calls=%async_computation.2 | async-start | bytes 4194304 | tf_op jit(solution)/shard_map/all_to_all | solution.py:24
  400.0 0.0 all-reduce.2.cloned.1.call-start
  400.0 0.2 compare_reduce_fusion
  400.2 0.1 broadcast_bitcast_fusion
  400.3 25.9 %all-to-all-done.1 = bf16[16,64,1024]{2,1,0:T(8,128)(2,1)} async-done(((bf16[16,64,1024]{2,1,0:T(8,128)(2,1)}), bf16[16,64,1024]{2,1,0:T(8,128)(2,1)}, u32[]{:S(2)}, u32[]{:S(2)}) %all-to-all-start.1) | async-done | bytes 2097184 | tf_op jit(solution)/shard_map/all_to_all | solution.py:24
  426.2 1.8 broadcast_select_fusion
  428.1 1.3 copy-done.1
  429.4 1.2 dynamic-slice_select_fusion
  430.6 0.0 all-reduce.2.cloned.1.call-update
  430.6 85.2 %all-reduce.2.cloned.1.call-done = bf16[512,1024]{1,0:T(8,128)(2,1)} async-done(((bf16[512,1024]{1,0:T(8,128)(2,1)}), bf16[512,1024]{1,0:T(8,128)(2,1)}) %all-reduce.2.cloned.1.call-update) | async-done | bytes 1048592 | tf_op jit(solution)/shard_map/psum | solution.py:40
  515.8 4.8 fusion.13
  520.5 3.1 copy.35
  (8 shorter events, 0.0 us)
Async XLA Ops:
  7.2 235.2 %copy-start = (bf16[1024,1024]{1,0:T(8,128)(2,1)S(1)}, bf16[1024,1024]{1,0:T(8,128)(2,1)}, u32[]{:S(2)}) copy-start(bf16[1024,1024]{1,0:T(8,128)(2,1)} %param.10) | copy-start | bytes 6291460
  7.2 141.8 %all-gather.2.cloned.1.call-start = ((), (), s32[]{:S(2)}) async-start(), calls=%async_computation.3 | async-start | bytes 26738688 | tf_op jit(solution)/shard_map/all_gather | solution.py:67
  15.8 340.7 %reduce-scatter.2.cloned.1.call-start = ((), (), s32[]{:S(2)}) async-start(), calls=%async_computation.4 | async-start | bytes 9437184 | tf_op jit(solution)/shard_map/reduce_scatter | solution.py:82
  242.3 0.7 copy-start.2
  393.3 32.9 %all-to-all-start.1 = ((bf16[16,64,1024]{2,1,0:T(8,128)(2,1)}), bf16[16,64,1024]{2,1,0:T(8,128)(2,1)}, u32[]{:S(2)}, u32[]{:S(2)}) async-start(bf16[16,64,1024]{2,1,0:T(8,128)(2,1)} %broadcast_in_dim.35), calls=%async_computation.2 | async-start | bytes 4194304 | tf_op jit(solution)/shard_map/all_to_all | solution.py:24
  400.0 115.8 %all-reduce.2.cloned.1.call-start = ((), (), s32[]{:S(2)}) async-start(), calls=%async_computation.5 | async-start | bytes 2097152 | tf_op jit(solution)/shard_map/psum | solution.py:40
  428.0 1.3 copy-start.1
  429.4 86.4 %copy-start.3 = (bf16[1024,512]{1,0:T(8,128)(2,1)S(1)}, bf16[1024,512]{1,0:T(8,128)(2,1)}, u32[]{:S(2)}) copy-start(bf16[1024,512]{1,0:T(8,128)(2,1)} %param.9) | copy-start | bytes 3145732
Sparse Core Ops, SparseCore 0:
  15.9 132.9 all-gather.1
  242.5 114.0 reduce-scatter.1
  430.7 85.0 all-reduce.1
where the time goes:
time: 537 us; the launch traced here: 530 us
  waiting for transfers between devices  355 us (66%)
  matrix products  97.4 us (18%)
  blocking collectives  30.2 us (6%)
  local copies, waits for them, and re-layouts  21.5 us (4%)
  between operations  14.1 us (3%)
  starting transfers between devices  6.77 us (1%)
    all_gather x1, waiting for transfers between devices, local(): whole_rows = lax.all_gather(lower_rows, 'dev', axis=0, tiled=True)  132 us
    reduce_scatter x1, waiting for transfers between devices, local(): lax.psum_scatter(spread.astype(jnp.bfloat16), 'sec', scatter_dimension=0,...  112 us
    psum x1, waiting for transfers between devices, spread_2(): return lax.psum(kept, axis)  85.2 us
    dot_general x1, matrix products, local(): jnp.einsum('mj,jbp->mbp', pick_cols, whole_rows.reshape(child_blocks, BLK...  52.3 us
    all_to_all x1, blocking collectives, sum_at_owner(): lax.all_to_all(tiles, axis, split_axis=0, concat_axis=0, tiled=True)  30.2 us
    all_to_all x1, waiting for transfers between devices, from_everyone(): return lax.all_to_all(copies, axis, split_axis=0, concat_axis=0, tiled=True)  25.9 us
    dot_general x2, matrix products, outer_rows(): lax.dot_general(left_rows, right_rows, (((1,), (1,)), ((), ())), preferre...  23.6 us
    convert_element_type x1, local copies, waits for them, and re-layouts, local(): spread.astype(jnp.bfloat16)  11.3 us
  transfers between devices with their start and end apart: 4, of which 4 were waited for; matrix products, arithmetic and copies ran while one was open for 1% of the time, Pallas kernels for 0%

commit v1 on v0

v1 whole, which is shorter than its diff:
```python
import functools

import jax
import jax.numpy as jnp
from jax import lax
from jax.experimental import pallas as pl
from jax.experimental.pallas import tpu as pltpu
from jax.sharding import Mesh
from jax.sharding import PartitionSpec as P

BLK = 128
PORD = 8192
PIV = 2048
KH = PIV // 2
OWN = 384
BF = jnp.bfloat16
F32 = jnp.float32
SIZE = {"h": 2, "y": 4, "x": 4, "z": 2, "c": 2}
AXES = ("h", "y", "x", "z", "c")
KEYS = [(0, 0), (3, 0), (1, 0), (0, 1), (2, 0), (3, 1), (1, 1), (2, 1)]


def shift(array, axis, step):
    size = SIZE[axis]
    return lax.ppermute(array, axis, [(i, (i + step) % size) for i in range(size)])


def gather_rows(s0, s1):
    w0 = shift(s0, "x", 1)
    e0 = shift(s0, "x", -1)
    z0 = shift(s0, "z", 1)
    w1 = shift(s1, "x", 1)
    e1 = shift(s1, "x", -1)
    z1 = shift(s1, "z", 1)
    q0 = shift(w0, "x", 1)
    q1 = shift(e1, "x", -1)
    b0 = shift(z0, "x", 1)
    a1 = shift(z1, "x", -1)
    a0 = shift(e0, "z", 1)
    b1 = shift(w1, "z", 1)
    r0a = shift(b0[:256], "x", 1)
    r0b = shift(q0[256:], "z", 1)
    r1a = shift(a1[:256], "x", -1)
    r1b = shift(q1[256:], "z", 1)
    mine = {
        (0, 0): [[s0], [s1]],
        (3, 0): [[w0], [w1]],
        (1, 0): [[e0], [e1]],
        (0, 1): [[z0], [z1]],
        (2, 0): [[q0], [q1]],
        (3, 1): [[b0], [b1]],
        (1, 1): [[a0], [a1]],
        (2, 1): [[r0a, r0b], [r1a, r1b]],
    }
    other = {k: [[shift(p, "c", 1) for p in half] for half in v] for k, v in mine.items()}
    return mine, other


def piece_list(mine, other):
    out = []
    for place, key in enumerate(KEYS):
        for dc, table in enumerate((mine, other)):
            for half in range(2):
                row = (place * 2 + dc) * OWN
                for array in table[key][half]:
                    out.append((array, row, array.shape[0], half))
                    row += array.shape[0]
    return out


def contribution_kernel(pieces, n_main, dest, chosen, pan_rows, pan_cols, offset, *refs):
    n = len(pieces)
    ins = refs[:n]
    outs = refs[n : n + n_main]
    pans = refs[n + n_main : n + n_main + 8]
    rows, cols, placed, left, right, pan, sem_in, sem_sel, sem_out, sem_pan = refs[n + n_main + 8 :]

    def selection(m, start):
        for i, (first, count, half) in enumerate(pieces):
            for b in range(count // BLK):
                copy = pltpu.make_async_copy(
                    ins[i].at[pl.ds(b * BLK, BLK), :],
                    cols.at[pl.ds(m * BLK, BLK), pl.ds(half * KH, KH)],
                    sem_sel.at[m, half],
                )

                @pl.when(chosen[m] == first // BLK + b)
                def _(copy=copy):
                    copy.start()

    for m in range(4):
        selection(m, True)

    def arrival(i):
        first, count, half = pieces[i]
        return pltpu.make_async_copy(
            ins[i],
            rows.at[pl.ds(first, count), pl.ds(half * KH, KH)],
            sem_in.at[i],
        )

    for i in range(n):
        arrival(i).start()

    @pl.loop(0, PORD // BLK)
    def _(i):
        for half in range(2):
            placed[half, pl.ds(i * BLK, BLK), :] = jnp.zeros((BLK, 256), BF)

    for m in range(4):

        @pl.when(chosen[m] < 0)
        def _(m=m):
            cols[pl.ds(m * BLK, BLK), :] = jnp.zeros((BLK, PIV), BF)

        @pl.when(chosen[m] >= 0)
        def _(m=m):
            for half in range(2):
                pltpu.make_async_copy(
                    ins[0].at[pl.ds(0, BLK), :],
                    cols.at[pl.ds(m * BLK, BLK), pl.ds(half * KH, KH)],
                    sem_sel.at[m, half],
                ).wait()

    done = 0
    for chunk in range(8):
        while done < n and pieces[done][0] < (chunk + 1) * 768:
            arrival(done).wait()
            done += 1

        @pl.loop(0, 2)
        def _(part, chunk=chunk):
            base = chunk * 6 + part * 3
            product = lax.dot_general(
                rows[pl.ds(base * BLK, OWN), :],
                cols[...],
                (((1,), (1,)), ((), ())),
                preferred_element_type=F32,
            )
            for b in range(3):
                block = (-product[b * BLK : (b + 1) * BLK]).astype(BF)
                at = pl.multiple_of(dest[base + b] * BLK, BLK)
                placed[0, pl.ds(at, BLK), :] = block[:, :256]
                placed[1, pl.ds(at, BLK), :] = block[:, 256:]

    def leaving(i):
        return pltpu.make_async_copy(
            placed.at[i % 2, pl.ds((i // 2) * 1024, 1024), :], outs[i], sem_out.at[i]
        )

    for i in range(n_main):
        leaving(i).start()

    for q in range(8):

        @pl.when(pan_rows[q] < 0)
        def _(q=q):
            left[pl.ds(q * 64, 64), :] = jnp.zeros((64, PIV), BF)

        @pl.when(pan_rows[q] >= 0)
        def _(q=q):
            at = pl.multiple_of(pan_rows[q] * BLK + offset[0], 64)
            left[pl.ds(q * 64, 64), :] = rows[pl.ds(at, 64), :]

        @pl.when(pan_cols[q] < 0)
        def _(q=q):
            right[pl.ds(q * BLK, BLK), :] = jnp.zeros((BLK, PIV), BF)

        @pl.when(pan_cols[q] >= 0)
        def _(q=q):
            at = pl.multiple_of(pan_cols[q] * BLK, BLK)
            right[pl.ds(q * BLK, BLK), :] = rows[pl.ds(at, BLK), :]

    @pl.loop(0, 2)
    def _(half):
        pan[half] = (
            -lax.dot_general(
                left[...],
                right[pl.ds(pl.multiple_of(half * 512, 512), 512), :],
                (((1,), (1,)), ((), ())),
                preferred_element_type=F32,
            )
        ).astype(BF)

    def pan_leaving(i):
        return pltpu.make_async_copy(
            pan.at[i % 2, pl.ds((i // 2) * 128, 128), :], pans[i], sem_pan.at[i]
        )

    for i in range(8):
        pan_leaving(i).start()
    for i in range(8):
        pan_leaving(i).wait()
    for i in range(n_main):
        leaving(i).wait()


def contributions(pieces, dest, chosen, pan_rows, pan_cols, offset):
    arrays = [p[0] for p in pieces]
    spec = [p[1:] for p in pieces]
    n = len(arrays)
    any_space = pl.BlockSpec(memory_space=pl.ANY)
    results = pl.pallas_call(
        functools.partial(contribution_kernel, spec, 16),
        out_shape=[jax.ShapeDtypeStruct((1024, 256), BF)] * 16
        + [jax.ShapeDtypeStruct((128, 512), BF)] * 8,
        in_specs=[pl.BlockSpec(memory_space=pltpu.SMEM)] * 5 + [any_space] * n,
        out_specs=[any_space] * 24,
        scratch_shapes=[
            pltpu.VMEM((6144, PIV), BF),
            pltpu.VMEM((512, PIV), BF),
            pltpu.VMEM((2, PORD, 256), BF),
            pltpu.VMEM((512, PIV), BF),
            pltpu.VMEM((1024, PIV), BF),
            pltpu.VMEM((2, 512, 512), BF),
            pltpu.SemaphoreType.DMA((n,)),
            pltpu.SemaphoreType.DMA((4, 2)),
            pltpu.SemaphoreType.DMA((16,)),
            pltpu.SemaphoreType.DMA((8,)),
        ],
        compiler_params=pltpu.CompilerParams(vmem_limit_bytes=60 * 2**20),
        cost_estimate=pl.CostEstimate(
            flops=15_000_000_000, bytes_accessed=36_000_000, transcendentals=0
        ),
    )(dest, chosen, pan_rows, pan_cols, offset, *arrays)
    main, pan = results[:16], results[16:]
    main = [[[main[(dh * 4 + dy) * 2 + half] for half in range(2)] for dy in range(4)] for dh in range(2)]
    pan = [[pan[dy * 2 + half] for half in range(2)] for dy in range(4)]
    return main, pan


def ring_sum(parts):
    a = shift(parts[2][0], "y", 1)
    b = shift(parts[2][1], "y", -1)
    d1 = shift(parts[1][1], "y", 1)
    d0 = shift(parts[3][0], "y", -1)
    e0 = shift(parts[1][0] + a, "y", 1)
    e1 = shift(parts[3][1] + b, "y", -1)
    return [
        parts[0][0].astype(F32) + d0.astype(F32) + e0.astype(F32),
        parts[0][1].astype(F32) + d1.astype(F32) + e1.astype(F32),
    ]


def pick(bit, when_zero, when_one):
    return jnp.where(bit == 0, when_zero, when_one)


def ordered_pair(bit, own, other):
    return jnp.stack([pick(bit, own, other), pick(bit, other, own)])


def ordered_ring(at, parts):
    twice = jnp.stack(list(parts) + list(parts))
    return lax.dynamic_slice_in_dim(twice, (4 - at) % 4, 4, 0)


def front_panel(picked, x, z, c):
    v = picked.reshape(4, 2, 2, 64, 1024)
    v = pick(c, v[:, :, 0], v[:, :, 1]) + shift(pick(c, v[:, :, 1], v[:, :, 0]), "c", 1)
    own = lambda k: lax.dynamic_index_in_dim(v, (x + k) % 4, 0, keepdims=False)
    v = own(0) + shift(own(1), "x", 1) + shift(own(3), "x", -1) + shift(own(2), "x", 2)
    return pick(z, v[0], v[1]) + shift(pick(z, v[1], v[0]), "z", 1)


def local(child_panel, child_inverse, child_map, parent_front, parent_inverse, parent_pivots):
    h, y, x, z, c = (lax.axis_index(a) for a in AXES)
    sec = h * 4 + y
    dev = x * 4 + z * 2 + c

    my_map = lax.dynamic_index_in_dim(child_map, sec, 0, keepdims=False)
    place_of = {key: i for i, key in enumerate(KEYS)}
    place_table = jnp.array([[place_of[(dx, dz)] for dz in range(2)] for dx in range(4)], jnp.int32)
    child = jnp.arange(48, dtype=jnp.int32)
    owner = child // 3
    place = place_table[(owner // 4 - x) % 4, (owner // 2 % 2) ^ z]
    position = (place * 2 + ((owner % 2) ^ c)) * 3 + child % 3
    parent_row = my_map // 8
    slot = (((parent_row // 4) ^ h) * 4 + (parent_row % 4 - y) % 4) * 8 + my_map % 8
    dest = jnp.sum(
        jnp.where(position[None, :] == child[:, None], slot[None, :], 0), axis=1, dtype=jnp.int32
    )

    def find(targets):
        hit = my_map[None, :] == targets[:, None]
        return jnp.sum(jnp.where(hit, position[None, :] + 1, 0), axis=1, dtype=jnp.int32) - 1

    chosen = find(dev * 4 + jnp.arange(4, dtype=jnp.int32))
    slots = jnp.arange(8, dtype=jnp.int32)
    row_sec = ((slots % 2) ^ h) * 4 + (slots // 2 + y) % 4
    pan_rows = find(row_sec * 8 + dev // 2)
    pan_cols = find(parent_pivots)
    offset = (dev % 2 * 64).astype(jnp.int32).reshape(1)

    panel = child_panel[0]
    inverse = child_inverse[0]
    s0 = jnp.dot(panel[:, :KH], inverse[:KH, :KH], preferred_element_type=F32).astype(BF)
    s1 = jnp.dot(panel, inverse[:, KH:], preferred_element_type=F32).astype(BF)
    mine, other = gather_rows(s0, s1)

    main, pan = contributions(piece_list(mine, other), dest, chosen, pan_rows, pan_cols, offset)

    targets = dev * 4 + jnp.arange(4, dtype=jnp.int32)
    hot = (parent_pivots[:, None] == targets[None, :]).astype(BF)
    picked = jnp.einsum(
        "nri,pr->npi", parent_front.reshape(1024, 4, BLK), hot, preferred_element_type=F32
    ).astype(BF)
    front_rows = front_panel(picked.reshape(1024, 1024), x, z, c)

    pan_sum = ring_sum(pan)
    pan_sum = jnp.concatenate(pan_sum, axis=1)
    from_h = shift(pan_sum[64:].astype(BF), "h", 1)
    pan_rows_f = pan_sum[:64] + from_h.astype(F32) + front_rows.astype(F32)
    share = jnp.dot(pan_rows_f.astype(BF), parent_inverse, preferred_element_type=F32).astype(BF)

    row_block = sec * 8 + dev // 2
    masked = jnp.where(jnp.any(parent_pivots == row_block), jnp.zeros_like(share), share)
    pairs = [(s * 16 + d, (d % 8) * 16 + 2 * s + d // 8) for s in range(8) for d in range(16)]
    moved = lax.ppermute(masked, AXES, pairs)
    both = ordered_pair(h, moved, shift(moved, "h", 1))
    ring = ordered_ring(y, [both, shift(both, "y", -1), shift(both, "y", 2), shift(both, "y", 1)])
    column_factor = ring.transpose(1, 0, 2, 3).reshape(512, 1024)

    both = ordered_pair(z, share, shift(share, "z", 1))
    ring = ordered_ring(x, [both, shift(both, "x", -1), shift(both, "x", 2), shift(both, "x", 1)])
    both = ordered_pair(c, ring, shift(ring, "c", 1))
    parent_factor = both.transpose(1, 2, 0, 3, 4).reshape(1024, 1024)

    far = jnp.concatenate(ring_sum(main[1]), axis=1).astype(BF)
    far = shift(far, "h", 1)
    near = jnp.concatenate(ring_sum(main[0]), axis=1)
    assembled = parent_front.astype(F32) + near + far.astype(F32)

    my_blocks = sec * 8 + jnp.arange(8, dtype=jnp.int32)
    is_pivot = jnp.any(parent_pivots[None, :] == my_blocks[:, None], axis=1)
    row_pivot = jnp.repeat(is_pivot, BLK)
    trailing = jnp.where(row_pivot[:, None], jnp.zeros_like(parent_factor), parent_factor)
    update = lax.dot_general(
        trailing, column_factor, (((1,), (1,)), ((), ())), preferred_element_type=F32
    )
    return assembled - update, parent_factor


def solution(mesh):
    fine = Mesh(mesh.devices.reshape(tuple(SIZE[a] for a in AXES)), AXES)
    sec, dev = ("h", "y"), ("x", "z", "c")
    placed = (P(sec, dev, None), P(sec, None, None), P(), P(sec, dev), P(), P())
    return jax.shard_map(
        local,
        mesh=fine,
        in_specs=placed,
        out_specs=(P(sec, dev), P(sec, None)),
        check_vma=False,
    )
```

time: 537 us -> 337 us (0.63)
  waiting for transfers between devices: 355 us -> 157 us
  starting transfers between devices: 6.77 us -> 102 us
  matrix products: 97.4 us -> 14 us
  blocking collectives: 30.2 us -> 0 us
  Pallas kernels: 0 us -> 24.2 us
  between operations: 14.1 us -> 1.84 us
  other arithmetic: 5.18 us -> 17.1 us
  local copies, waits for them, and re-layouts: 21.5 us -> 14.6 us
    ppermute x0 -> x69, waiting for transfers between devices: none -> 157 us  [the longest x68 152 us: shift(): lax.ppermute(array, axis, [(i, (i + step) % size) for i in range(size)])]
    all_gather x1 -> x0, waiting for transfers between devices: 132 us -> none  [local(): whole_rows = lax.all_gather(lower_rows, 'dev', axis=0, tiled=True)]
    reduce_scatter x1 -> x0, waiting for transfers between devices: 112 us -> none  [local(): lax.psum_scatter(spread.astype(jnp.bfloat16), 'sec', scatter_dimension=0,...]
    ppermute x0 -> x69, starting transfers between devices: none -> 102 us  [the longest x68 90.3 us: shift(): lax.ppermute(array, axis, [(i, (i + step) % size) for i in range(size)])]
    psum x1 -> x0, waiting for transfers between devices: 85.2 us -> none  [spread_2(): return lax.psum(kept, axis)]
    dot_general x7 -> x5, matrix products: 97.4 us -> 14 us  [the longest x1 4.87 us: local(): s1 = jnp.dot(panel, inverse[:, KH:], preferred_element_type=F32).astype(BF)]
    all_to_all x1 -> x0, blocking collectives: 30.2 us -> none  [sum_at_owner(): lax.all_to_all(tiles, axis, split_axis=0, concat_axis=0, tiled=True)]
    all_to_all x1 -> x0, waiting for transfers between devices: 25.9 us -> none  [from_everyone(): return lax.all_to_all(copies, axis, split_axis=0, concat_axis=0, tiled=True)]
  transfers between devices with their start and end apart: 4 -> 69, of which waited for: 4 -> 24; matrix products, arithmetic and copies ran while one was open for 1% -> 12% of each run, Pallas kernels for 0% -> 7%
where the time goes in v1:
time: 337 us; the launch traced here: 330 us
  waiting for transfers between devices  157 us (47%)
  starting transfers between devices  102 us (30%)
  Pallas kernels  24.2 us (7%)
  other arithmetic  17.1 us (5%)
  local copies, waits for them, and re-layouts  14.6 us (4%)
  matrix products  14 us (4%)
    ppermute x68, waiting for transfers between devices, shift(): lax.ppermute(array, axis, [(i, (i + step) % size) for i in range(size)])  152 us
    ppermute x68, starting transfers between devices, shift(): lax.ppermute(array, axis, [(i, (i + step) % size) for i in range(size)])  90.3 us
    pallas_call x1, Pallas kernels, contributions(): pl.pallas_call(functools.partial(contribution_kernel, spec, 16), out_shap...  24.2 us
    ppermute x1, starting transfers between devices, local(): moved = lax.ppermute(masked, AXES, pairs)  11.5 us
  transfers between devices with their start and end apart: 69, of which 24 were waited for; matrix products, arithmetic and copies ran while one was open for 12% of the time, Pallas kernels for 7%

profile of v1, /device:TPU:18, one launch (start us, length us, event | category | flops | bytes accessed | tf_op | source)
XLA Modules:
  0.0 330.1 jit_solution(7117430734329979753)
XLA Ops:
  0.7 3.9 %fusion.9.refs_0_ = bf16[384,1024]{1,0:T(8,128)(2,1)} fusion(bf16[2048,2048]{1,0:T(8,128)(2,1)} %bitcast.103, bf16[384,2048]{1,0:T(8,128)(2,1)} %bitcast.105), kind=kOutput, calls=%fused_computation.12 | convolution fusion | flops 805699584 | bytes 3670016 | tf_op jit(solution)/shard_map/dot_general | solution.py:297
  4.5 4.9 %fusion.6.refs_1_ = bf16[384,1024]{1,0:T(8,128)(2,1)} fusion(bf16[2048,2048]{1,0:T(8,128)(2,1)} %bitcast.104, bf16[1,384,2048]{2,1,0:T(8,128)(2,1)S(1)} %copy-done.13), kind=kOutput, calls=%fused_computation.11 | convolution fusion | flops 1611005952 | bytes 6553600 | tf_op jit(solution)/shard_map/dot_general | solution.py:298
  18.7 4.2 %reshape_reshape.3 = bf16[4,2,2,64,1024]{4,3,2,1,0:T(8,128)(2,1)} reshape(bf16[1024,8,128]{2,1,0:T(8,128)(2,1)} %convert_bitcast_fusion) | data formatting | bytes 4194304 | tf_op jit(solution)/shard_map/reshape;reshape | solution.py:259
  24.6 6.0 %collective-permute-done.2.refs_4_ = bf16[384,1024]{1,0:T(8,128)(2,1)} collective-permute-done((bf16[384,1024]{1,0:T(8,128)(2,1)}, bf16[384,1024]{1,0:T(8,128)(2,1)}, u32[]{:S(2)}, u32[]{:S(2)}) %collective-permute-start.2) | collective-permute-done | bytes 786464 | tf_op jit(solution)/shard_map/ppermute | solution.py:25
  32.5 14.0 %collective-permute-done.3.refs_5_ = bf16[384,1024]{1,0:T(8,128)(2,1)} collective-permute-done((bf16[384,1024]{1,0:T(8,128)(2,1)}, bf16[384,1024]{1,0:T(8,128)(2,1)}, u32[]{:S(2)}, u32[]{:S(2)}) %collective-permute-start.3) | collective-permute-done | bytes 786464 | tf_op jit(solution)/shard_map/ppermute | solution.py:25
  49.2 16.4 %collective-permute-done.11.refs_13_ = bf16[384,1024]{1,0:T(8,128)(2,1)} collective-permute-done((bf16[384,1024]{1,0:T(8,128)(2,1)}, bf16[384,1024]{1,0:T(8,128)(2,1)}, u32[]{:S(2)}, u32[]{:S(2)}) %collective-permute-start.11) | collective-permute-done | bytes 786464 | tf_op jit(solution)/shard_map/ppermute | solution.py:25
  71.2 15.4 %collective-permute-done.18.refs_20_ = bf16[384,1024]{1,0:T(8,128)(2,1)} collective-permute-done((bf16[384,1024]{1,0:T(8,128)(2,1)S(1)}, bf16[384,1024]{1,0:T(8,128)(2,1)}, u32[]{:S(2)}, u32[]{:S(2)}) %collective-permute-start.18) | collective-permute-done | bytes 786464 | tf_op jit(solution)/shard_map/ppermute | solution.py:25
  92.4 10.3 %collective-permute-done.14.refs_16_ = bf16[384,1024]{1,0:T(8,128)(2,1)} collective-permute-done((bf16[384,1024]{1,0:T(8,128)(2,1)}, bf16[384,1024]{1,0:T(8,128)(2,1)}, u32[]{:S(2)}, u32[]{:S(2)}) %collective-permute-start.14) | collective-permute-done | bytes 786464 | tf_op jit(solution)/shard_map/ppermute | solution.py:25
  111.1 13.2 %collective-permute-done.22.refs_24_ = bf16[384,1024]{1,0:T(8,128)(2,1)} collective-permute-done((bf16[384,1024]{1,0:T(8,128)(2,1)}, bf16[384,1024]{1,0:T(8,128)(2,1)}, u32[]{:S(2)}, u32[]{:S(2)}) %collective-permute-start.22) | collective-permute-done | bytes 786464 | tf_op jit(solution)/shard_map/ppermute | solution.py:25
  125.6 4.3 %collective-permute-done.27.refs_29_ = bf16[128,1024]{1,0:T(8,128)(2,1)} collective-permute-done((bf16[128,1024]{1,0:T(8,128)(2,1)}, bf16[128,1024]{1,0:T(8,128)(2,1)}, u32[]{:S(2)}, u32[]{:S(2)}) %collective-permute-start.27) | collective-permute-done | bytes 262176 | tf_op jit(solution)/shard_map/ppermute | solution.py:25
  129.9 3.0 collective-permute-done.29.refs_31_
  146.0 24.2 %shard_map.86 = (bf16[1024,256]{1,0:T(8,128)(2,1)}, bf16[1024,256]{1,0:T(8,128)(2,1)}, bf16[1024,256]{1,0:T(8,128)(2,1)}, bf16[1024,256]{1,0:T(8,128)(2,1)}, bf1...) custom-call(s32[48]{0:T(128)} %select_reduce_fusion.dest, ...), custom_call_target="tpu_custom_call" | custom-call | flops 15000000512 | bytes 36000000 | tf_op jit(solution)/shard_map/pallas_call | solution.py:203
  183.2 3.6 %collective-permute-done.50 = bf16[128,512]{1,0:T(8,128)(2,1)S(1)} collective-permute-done((bf16[128,512]{1,0:T(8,128)(2,1)S(1)}, bf16[128,512]{1,0:T(8,128)(2,1)S(1)}, u32[]{:S(2)}, u32[]{:S(2)}) %collective-permute-start.50) | collective-permute-done | bytes 131104 | tf_op jit(solution)/shard_map/ppermute | solution.py:25
  190.5 5.2 %collective-permute-done.53 = bf16[64,1024]{1,0:T(8,128)(2,1)S(1)} collective-permute-done((bf16[64,1024]{1,0:T(8,128)(2,1)S(1)}, bf16[64,1024]{1,0:T(8,128)(2,1)S(1)}, u32[]{:S(2)}, u32[]{:S(2)}) %collective-permute-start.53) | collective-permute-done | bytes 131104 | tf_op jit(solution)/shard_map/ppermute | solution.py:25
  201.4 3.0 collective-permute-start.41
  205.1 3.1 collective-permute-start.60
  208.5 5.9 %collective-permute-done.38 = bf16[1024,256]{1,0:T(8,128)(2,1)} collective-permute-done((bf16[1024,256]{1,0:T(8,128)(2,1)}, bf16[1024,256]{1,0:T(8,128)(2,1)}, u32[]{:S(2)}, u32[]{:S(2)}) %collective-permute-start.38) | collective-permute-done | bytes 524320 | tf_op jit(solution)/shard_map/ppermute | solution.py:25
  214.4 3.1 collective-permute-start.37
  220.4 3.1 collective-permute-done.44
  227.0 4.1 %collective-permute-start.61 = (bf16[2,64,1024]{2,1,0:T(8,128)(2,1)S(1)}, bf16[2,64,1024]{2,1,0:T(8,128)(2,1)S(1)}, u32[]{:S(2)}, u32[]{:S(2)}) collective-permute-start(bf16[2,64,1024]{2,1,0:T(8,128)(2,1)S(1)} %pad_maximum_fusion.2), channel_id=1, source_target_pairs={{0,8},{4,12},{8,0},{12,4},{1,9},{5,13},{9,1},{13,5},{2,10},{6,14},... | collective-permute-start | bytes 786440 | tf_op jit(solution)/shard_map/ppermute | solution.py:25
  235.4 11.5 %collective-permute-start.64 = (bf16[64,1024]{1,0:T(8,128)(2,1)S(1)}, bf16[64,1024]{1,0:T(8,128)(2,1)S(1)}, u32[]{:S(2)}, u32[]{:S(2)}) collective-permute-start(bf16[64,1024]{1,0:T(8,128)(2,1)S(1)} %get-tuple-element.63), channel_id=1, source_target_pairs={{0,0},{1,16},{2,32},{3,48},{4,64},{5,80},{6,96},{7,112},{8,1},{9,1... | collective-permute-start | bytes 393224 | tf_op jit(solution)/shard_map/ppermute | solution.py:319
  247.0 4.3 %collective-permute-done.64 = bf16[64,1024]{1,0:T(8,128)(2,1)S(1)} collective-permute-done((bf16[64,1024]{1,0:T(8,128)(2,1)S(1)}, bf16[64,1024]{1,0:T(8,128)(2,1)S(1)}, u32[]{:S(2)}, u32[]{:S(2)}) %collective-permute-start.64) | collective-permute-done | bytes 131104 | tf_op jit(solution)/shard_map/ppermute | solution.py:319
  254.0 3.7 %collective-permute-done.65 = bf16[64,1024]{1,0:T(8,128)(2,1)S(1)} collective-permute-done((bf16[64,1024]{1,0:T(8,128)(2,1)S(1)}, bf16[64,1024]{1,0:T(8,128)(2,1)S(1)}, u32[]{:S(2)}, u32[]{:S(2)}) %collective-permute-start.65) | collective-permute-done | bytes 131104 | tf_op jit(solution)/shard_map/ppermute | solution.py:25
  257.7 7.9 %collective-permute-start.42 = (bf16[1024,256]{1,0:T(8,128)(2,1)S(1)}, bf16[1024,256]{1,0:T(8,128)(2,1)S(1)}, u32[]{:S(2)}, u32[]{:S(2)}) collective-permute-start(bf16[1024,256]{1,0:T(8,128)(2,1)S(1)} %add.421), channel_id=1, source_target_pairs={{0,16},{16,32},{32,48},{48,0},{1,17},{17,33},{33,49},{49,1},{2,18}... | collective-permute-start | bytes 1572872 | tf_op jit(solution)/shard_map/ppermute | solution.py:25
  265.9 5.9 %collective-permute-done.45 = bf16[1024,256]{1,0:T(8,128)(2,1)S(1)} collective-permute-done((bf16[1024,256]{1,0:T(8,128)(2,1)S(1)}, bf16[1024,256]{1,0:T(8,128)(2,1)S(1)}, u32[]{:S(2)}, u32[]{:S(2)}) %collective-permute-start.45) | collective-permute-done | bytes 524320 | tf_op jit(solution)/shard_map/ppermute | solution.py:25
  272.0 3.6 %collective-permute-start.36 = (bf16[1024,256]{1,0:T(8,128)(2,1)S(1)}, bf16[1024,256]{1,0:T(8,128)(2,1)S(1)}, u32[]{:S(2)}, u32[]{:S(2)}) collective-permute-start(bf16[1024,256]{1,0:T(8,128)(2,1)S(1)} %add.414), channel_id=1, source_target_pairs={{0,16},{16,32},{32,48},{48,0},{1,17},{17,33},{33,49},{49,1},{2,18}... | collective-permute-start | bytes 1572872 | tf_op jit(solution)/shard_map/ppermute | solution.py:25
  275.6 5.0 %collective-permute-start.66 = (bf16[2,64,1024]{2,1,0:T(8,128)(2,1)S(1)}, bf16[2,64,1024]{2,1,0:T(8,128)(2,1)S(1)}, u32[]{:S(2)}, u32[]{:S(2)}) collective-permute-start(bf16[2,64,1024]{2,1,0:T(8,128)(2,1)S(1)} %pad_maximum_fusion.3), channel_id=1, source_target_pairs={{0,48},{16,0},{32,16},{48,32},{1,49},{17,1},{33,17},{49,33},{2,50}... | collective-permute-start | bytes 786440 | tf_op jit(solution)/shard_map/ppermute | solution.py:25
  281.9 11.9 %collective-permute-done.39 = bf16[1024,256]{1,0:T(8,128)(2,1)S(1)} collective-permute-done((bf16[1024,256]{1,0:T(8,128)(2,1)S(1)}, bf16[1024,256]{1,0:T(8,128)(2,1)S(1)}, u32[]{:S(2)}, u32[]{:S(2)}) %collective-permute-start.39) | collective-permute-done | bytes 524320 | tf_op jit(solution)/shard_map/ppermute | solution.py:25
  293.8 5.8 %collective-permute-start.68 = (bf16[2,64,1024]{2,1,0:T(8,128)(2,1)S(1)}, bf16[2,64,1024]{2,1,0:T(8,128)(2,1)S(1)}, u32[]{:S(2)}, u32[]{:S(2)}) collective-permute-start(bf16[2,64,1024]{2,1,0:T(8,128)(2,1)S(1)} %pad_maximum_fusion.3), channel_id=1, source_target_pairs={{0,16},{16,32},{32,48},{48,0},{1,17},{17,33},{33,49},{49,1},{2,18}... | collective-permute-start | bytes 786440 | tf_op jit(solution)/shard_map/ppermute | solution.py:25
  300.2 3.2 collective-permute-done.68
  306.2 20.8 %collective-permute-done.46 = bf16[1024,512]{1,0:T(8,128)(2,1)S(1)} collective-permute-done((bf16[1024,512]{1,0:T(8,128)(2,1)S(1)}, bf16[1024,512]{1,0:T(8,128)(2,1)S(1)}, u32[]{:S(2)}, u32[]{:S(2)}) %collective-permute-start.46) | collective-permute-done | bytes 1048608 | tf_op jit(solution)/shard_map/ppermute | solution.py:25
  326.9 2.7 fusion.5
  (230 shorter events, 91.3 us)
Async XLA Ops:
  9.9 20.7 %collective-permute-start.2 = (bf16[384,1024]{1,0:T(8,128)(2,1)}, bf16[384,1024]{1,0:T(8,128)(2,1)}, u32[]{:S(2)}, u32[]{:S(2)}) collective-permute-start(bf16[384,1024]{1,0:T(8,128)(2,1)} %fusion.9.refs_0_), channel_id=1, source_target_pairs={{0,4},{4,8},{8,12},{12,0},{1,5},{5,9},{9,13},{13,1},{2,6},{6,10},{... | collective-permute-start | bytes 2359304 | tf_op jit(solution)/shard_map/ppermute | solution.py:25
  11.4 35.1 %collective-permute-start.3 = (bf16[384,1024]{1,0:T(8,128)(2,1)}, bf16[384,1024]{1,0:T(8,128)(2,1)}, u32[]{:S(2)}, u32[]{:S(2)}) collective-permute-start(bf16[384,1024]{1,0:T(8,128)(2,1)} %fusion.6.refs_1_), channel_id=1, source_target_pairs={{0,4},{4,8},{8,12},{12,0},{1,5},{5,9},{9,13},{13,1},{2,6},{6,10},{... | collective-permute-start | bytes 2359304 | tf_op jit(solution)/shard_map/ppermute | solution.py:25
  12.6 35.8 %collective-permute-start.6 = (bf16[384,1024]{1,0:T(8,128)(2,1)}, bf16[384,1024]{1,0:T(8,128)(2,1)}, u32[]{:S(2)}, u32[]{:S(2)}) collective-permute-start(bf16[384,1024]{1,0:T(8,128)(2,1)} %fusion.9.refs_0_), channel_id=1, source_target_pairs={{0,12},{4,0},{8,4},{12,8},{1,13},{5,1},{9,5},{13,9},{2,14},{6,2},{... | collective-permute-start | bytes 2359304 | tf_op jit(solution)/shard_map/ppermute | solution.py:25
  14.8 33.9 %collective-permute-start.7 = (bf16[384,1024]{1,0:T(8,128)(2,1)}, bf16[384,1024]{1,0:T(8,128)(2,1)}, u32[]{:S(2)}, u32[]{:S(2)}) collective-permute-start(bf16[384,1024]{1,0:T(8,128)(2,1)} %fusion.6.refs_1_), channel_id=1, source_target_pairs={{0,12},{4,0},{8,4},{12,8},{1,13},{5,1},{9,5},{13,9},{2,14},{6,2},{... | collective-permute-start | bytes 2359304 | tf_op jit(solution)/shard_map/ppermute | solution.py:25
  24.6 41.1 %collective-permute-start.54 = (bf16[4,2,64,1024]{3,2,1,0:T(8,128)(2,1)S(1)}, bf16[4,2,64,1024]{3,2,1,0:T(8,128)(2,1)}, u32[]{:S(2)}, u32[]{:S(2)}) collective-permute-start(bf16[4,2,64,1024]{3,2,1,0:T(8,128)(2,1)S(1)} %select_bitcast_fusion.2), channel_id=1, source_target_pairs={{0,1},{1,0},{2,3},{3,2},{4,5},{5,4},{6,7},{7,6},{8,9},{9,8},{10,11... | collective-permute-start | bytes 3145736 | tf_op jit(solution)/shard_map/ppermute | solution.py:25
  66.1 20.5 %collective-permute-start.18 = (bf16[384,1024]{1,0:T(8,128)(2,1)S(1)}, bf16[384,1024]{1,0:T(8,128)(2,1)}, u32[]{:S(2)}, u32[]{:S(2)}) collective-permute-start(bf16[384,1024]{1,0:T(8,128)(2,1)S(1)} %collective-permute-done.10.refs_12_), channel_id=1, source_target_pairs={{0,4},{4,8},{8,12},{12,0},{1,5},{5,9},{9,13},{13,1},{2,6},{6,10},{... | collective-permute-start | bytes 2359304 | tf_op jit(solution)/shard_map/ppermute | solution.py:25
  67.6 20.8 %collective-permute-start.23 = (bf16[384,1024]{1,0:T(8,128)(2,1)}, bf16[384,1024]{1,0:T(8,128)(2,1)}, u32[]{:S(2)}, u32[]{:S(2)}) collective-permute-start(bf16[384,1024]{1,0:T(8,128)(2,1)} %collective-permute-done.11.refs_13_), channel_id=1, source_target_pairs={{0,12},{4,0},{8,4},{12,8},{1,13},{5,1},{9,5},{13,9},{2,14},{6,2},{... | collective-permute-start | bytes 2359304 | tf_op jit(solution)/shard_map/ppermute | solution.py:25
  68.2 34.5 %collective-permute-start.14 = (bf16[384,1024]{1,0:T(8,128)(2,1)}, bf16[384,1024]{1,0:T(8,128)(2,1)}, u32[]{:S(2)}, u32[]{:S(2)}) collective-permute-start(bf16[384,1024]{1,0:T(8,128)(2,1)} %collective-permute-done.2.refs_4_), channel_id=1, source_target_pairs={{0,4},{4,8},{8,12},{12,0},{1,5},{5,9},{9,13},{13,1},{2,6},{6,10},{... | collective-permute-start | bytes 2359304 | tf_op jit(solution)/shard_map/ppermute | solution.py:25
  69.7 34.4 %collective-permute-start.15 = (bf16[384,1024]{1,0:T(8,128)(2,1)}, bf16[384,1024]{1,0:T(8,128)(2,1)}, u32[]{:S(2)}, u32[]{:S(2)}) collective-permute-start(bf16[384,1024]{1,0:T(8,128)(2,1)} %collective-permute-done.7.refs_9_), channel_id=1, source_target_pairs={{0,12},{4,0},{8,4},{12,8},{1,13},{5,1},{9,5},{13,9},{2,14},{6,2},{... | collective-permute-start | bytes 2359304 | tf_op jit(solution)/shard_map/ppermute | solution.py:25
  71.2 37.7 %collective-permute-start.13 = (bf16[384,1024]{1,0:T(8,128)(2,1)}, bf16[384,1024]{1,0:T(8,128)(2,1)}, u32[]{:S(2)}, u32[]{:S(2)}) collective-permute-start(bf16[384,1024]{1,0:T(8,128)(2,1)} %collective-permute-done.11.refs_13_), channel_id=1, source_target_pairs={{0,1},{1,0},{2,3},{3,2},{4,5},{5,4},{6,7},{7,6},{8,9},{9,8},{10,11... | collective-permute-start | bytes 2359304 | tf_op jit(solution)/shard_map/ppermute | solution.py:25
  86.6 24.2 %collective-permute-start.19 = (bf16[384,1024]{1,0:T(8,128)(2,1)}, bf16[384,1024]{1,0:T(8,128)(2,1)}, u32[]{:S(2)}, u32[]{:S(2)}) collective-permute-start(bf16[384,1024]{1,0:T(8,128)(2,1)} %collective-permute-done.3.refs_5_), channel_id=1, source_target_pairs={{0,2},{2,0},{1,3},{3,1},{4,6},{6,4},{5,7},{7,5},{8,10},{10,8},{9,1... | collective-permute-start | bytes 2359304 | tf_op jit(solution)/shard_map/ppermute | solution.py:25
  88.4 35.9 %collective-permute-start.22 = (bf16[384,1024]{1,0:T(8,128)(2,1)}, bf16[384,1024]{1,0:T(8,128)(2,1)}, u32[]{:S(2)}, u32[]{:S(2)}) collective-permute-start(bf16[384,1024]{1,0:T(8,128)(2,1)} %collective-permute-done.6.refs_8_), channel_id=1, source_target_pairs={{0,2},{2,0},{1,3},{3,1},{4,6},{6,4},{5,7},{7,5},{8,10},{10,8},{9,1... | collective-permute-start | bytes 2359304 | tf_op jit(solution)/shard_map/ppermute | solution.py:25
  102.6 30.4 %collective-permute-start.26 = (bf16[256,1024]{1,0:T(8,128)(2,1)S(1)}, bf16[256,1024]{1,0:T(8,128)(2,1)}, u32[]{:S(2)}, u32[]{:S(2)}) collective-permute-start(bf16[256,1024]{1,0:T(8,128)(2,1)S(1)} %slice.62), channel_id=1, source_target_pairs={{0,4},{4,8},{8,12},{12,0},{1,5},{5,9},{9,13},{13,1},{2,6},{6,10},{... | collective-permute-start | bytes 1572872 | tf_op jit(solution)/shard_map/ppermute | solution.py:25
  104.1 29.6 %collective-permute-start.28 = (bf16[256,1024]{1,0:T(8,128)(2,1)S(1)}, bf16[256,1024]{1,0:T(8,128)(2,1)}, u32[]{:S(2)}, u32[]{:S(2)}) collective-permute-start(bf16[256,1024]{1,0:T(8,128)(2,1)S(1)} %slice.64), channel_id=1, source_target_pairs={{0,12},{4,0},{8,4},{12,8},{1,13},{5,1},{9,5},{13,9},{2,14},{6,2},{... | collective-permute-start | bytes 1572872 | tf_op jit(solution)/shard_map/ppermute | solution.py:25
  109.0 20.9 %collective-permute-start.27 = (bf16[128,1024]{1,0:T(8,128)(2,1)}, bf16[128,1024]{1,0:T(8,128)(2,1)}, u32[]{:S(2)}, u32[]{:S(2)}) collective-permute-start(bf16[128,1024]{1,0:T(8,128)(2,1)} %slice.63), channel_id=1, source_target_pairs={{0,2},{2,0},{1,3},{3,1},{4,6},{6,4},{5,7},{7,5},{8,10},{10,8},{9,1... | collective-permute-start | bytes 786440 | tf_op jit(solution)/shard_map/ppermute | solution.py:25
  110.8 22.1 %collective-permute-start.29 = (bf16[128,1024]{1,0:T(8,128)(2,1)S(1)}, bf16[128,1024]{1,0:T(8,128)(2,1)}, u32[]{:S(2)}, u32[]{:S(2)}) collective-permute-start(bf16[128,1024]{1,0:T(8,128)(2,1)S(1)} %slice.65), channel_id=1, source_target_pairs={{0,2},{2,0},{1,3},{3,1},{4,6},{6,4},{5,7},{7,5},{8,10},{10,8},{9,1... | collective-permute-start | bytes 786440 | tf_op jit(solution)/shard_map/ppermute | solution.py:25
  141.5 31.0 %collective-permute-start.57 = (bf16[2,64,1024]{2,1,0:T(8,128)(2,1)}, bf16[2,64,1024]{2,1,0:T(8,128)(2,1)S(1)}, u32[]{:S(2)}, u32[]{:S(2)}) collective-permute-start(bf16[2,64,1024]{2,1,0:T(8,128)(2,1)} %get-tuple-element.57), channel_id=1, source_target_pairs={{0,8},{4,12},{8,0},{12,4},{1,9},{5,13},{9,1},{13,5},{2,10},{6,14},... | collective-permute-start | bytes 786440 | tf_op jit(solution)/shard_map/ppermute | solution.py:25
  143.7 28.9 %collective-permute-start.56 = (bf16[2,64,1024]{2,1,0:T(8,128)(2,1)S(1)}, bf16[2,64,1024]{2,1,0:T(8,128)(2,1)}, u32[]{:S(2)}, u32[]{:S(2)}) collective-permute-start(bf16[2,64,1024]{2,1,0:T(8,128)(2,1)S(1)} %get-tuple-element.58), channel_id=1, source_target_pairs={{0,12},{4,0},{8,4},{12,8},{1,13},{5,1},{9,5},{13,9},{2,14},{6,2},{... | collective-permute-start | bytes 786440 | tf_op jit(solution)/shard_map/ppermute | solution.py:25
  145.1 27.5 %collective-permute-start.55 = (bf16[2,64,1024]{2,1,0:T(8,128)(2,1)S(1)}, bf16[2,64,1024]{2,1,0:T(8,128)(2,1)}, u32[]{:S(2)}, u32[]{:S(2)}) collective-permute-start(bf16[2,64,1024]{2,1,0:T(8,128)(2,1)S(1)} %get-tuple-element.56), channel_id=1, source_target_pairs={{0,4},{4,8},{8,12},{12,0},{1,5},{5,9},{9,13},{13,1},{2,6},{6,10},{... | collective-permute-start | bytes 786440 | tf_op jit(solution)/shard_map/ppermute | solution.py:25
  201.3 22.2 %collective-permute-start.44 = (bf16[1024,256]{1,0:T(8,128)(2,1)}, bf16[1024,256]{1,0:T(8,128)(2,1)}, u32[]{:S(2)}, u32[]{:S(2)}) collective-permute-start(bf16[1024,256]{1,0:T(8,128)(2,1)} %get-tuple-element.41), channel_id=1, source_target_pairs={{0,48},{16,0},{32,16},{48,32},{1,49},{17,1},{33,17},{49,33},{2,50}... | collective-permute-start | bytes 1572872 | tf_op jit(solution)/shard_map/ppermute | solution.py:25
  201.4 24.4 %collective-permute-start.41 = (bf16[1024,256]{1,0:T(8,128)(2,1)}, bf16[1024,256]{1,0:T(8,128)(2,1)}, u32[]{:S(2)}, u32[]{:S(2)}) collective-permute-start(bf16[1024,256]{1,0:T(8,128)(2,1)} %get-tuple-element.37), channel_id=1, source_target_pairs={{0,16},{16,32},{32,48},{48,0},{1,17},{17,33},{33,49},{49,1},{2,18}... | collective-permute-start | bytes 1572872 | tf_op jit(solution)/shard_map/ppermute | solution.py:25
  205.1 26.0 %collective-permute-start.60 = (bf16[2,64,1024]{2,1,0:T(8,128)(2,1)S(1)}, bf16[2,64,1024]{2,1,0:T(8,128)(2,1)S(1)}, u32[]{:S(2)}, u32[]{:S(2)}) collective-permute-start(bf16[2,64,1024]{2,1,0:T(8,128)(2,1)S(1)} %pad_maximum_fusion.2), channel_id=1, source_target_pairs={{0,12},{4,0},{8,4},{12,8},{1,13},{5,1},{9,5},{13,9},{2,14},{6,2},{... | collective-permute-start | bytes 786440 | tf_op jit(solution)/shard_map/ppermute | solution.py:25
  214.4 66.5 %collective-permute-start.37 = (bf16[1024,256]{1,0:T(8,128)(2,1)}, bf16[1024,256]{1,0:T(8,128)(2,1)S(1)}, u32[]{:S(2)}, u32[]{:S(2)}) collective-permute-start(bf16[1024,256]{1,0:T(8,128)(2,1)} %get-tuple-element.31), channel_id=1, source_target_pairs={{0,16},{16,32},{32,48},{48,0},{1,17},{17,33},{33,49},{49,1},{2,18}... | collective-permute-start | bytes 1572872 | tf_op jit(solution)/shard_map/ppermute | solution.py:25
  218.9 46.8 %collective-permute-start.43 = (bf16[1024,256]{1,0:T(8,128)(2,1)}, bf16[1024,256]{1,0:T(8,128)(2,1)S(1)}, u32[]{:S(2)}, u32[]{:S(2)}) collective-permute-start(bf16[1024,256]{1,0:T(8,128)(2,1)} %get-tuple-element.39), channel_id=1, source_target_pairs={{0,16},{16,32},{32,48},{48,0},{1,17},{17,33},{33,49},{49,1},{2,18}... | collective-permute-start | bytes 1572872 | tf_op jit(solution)/shard_map/ppermute | solution.py:25
  223.5 48.5 %collective-permute-start.40 = (bf16[1024,256]{1,0:T(8,128)(2,1)S(1)}, bf16[1024,256]{1,0:T(8,128)(2,1)S(1)}, u32[]{:S(2)}, u32[]{:S(2)}) collective-permute-start(bf16[1024,256]{1,0:T(8,128)(2,1)S(1)} %copy-done.21), channel_id=1, source_target_pairs={{0,48},{16,0},{32,16},{48,32},{1,49},{17,1},{33,17},{49,33},{2,50}... | collective-permute-start | bytes 1572872 | tf_op jit(solution)/shard_map/ppermute | solution.py:25
  231.1 20.1 %collective-permute-start.62 = (bf16[2,64,1024]{2,1,0:T(8,128)(2,1)S(1)}, bf16[2,64,1024]{2,1,0:T(8,128)(2,1)S(1)}, u32[]{:S(2)}, u32[]{:S(2)}) collective-permute-start(bf16[2,64,1024]{2,1,0:T(8,128)(2,1)S(1)} %pad_maximum_fusion.2), channel_id=1, source_target_pairs={{0,4},{4,8},{8,12},{12,0},{1,5},{5,9},{9,13},{13,1},{2,6},{6,10},{... | collective-permute-start | bytes 786440 | tf_op jit(solution)/shard_map/ppermute | solution.py:25
  251.2 20.6 %collective-permute-start.45 = (bf16[1024,256]{1,0:T(8,128)(2,1)S(1)}, bf16[1024,256]{1,0:T(8,128)(2,1)S(1)}, u32[]{:S(2)}, u32[]{:S(2)}) collective-permute-start(bf16[1024,256]{1,0:T(8,128)(2,1)S(1)} %add.424), channel_id=1, source_target_pairs={{0,48},{16,0},{32,16},{48,32},{1,49},{17,1},{33,17},{49,33},{2,50}... | collective-permute-start | bytes 1572872 | tf_op jit(solution)/shard_map/ppermute | solution.py:25
  265.8 34.0 %collective-permute-start.34 = (bf16[1024,256]{1,0:T(8,128)(2,1)S(1)}, bf16[1024,256]{1,0:T(8,128)(2,1)S(1)}, u32[]{:S(2)}, u32[]{:S(2)}) collective-permute-start(bf16[1024,256]{1,0:T(8,128)(2,1)S(1)} %copy-done.20), channel_id=1, source_target_pairs={{0,48},{16,0},{32,16},{48,32},{1,49},{17,1},{33,17},{49,33},{2,50}... | collective-permute-start | bytes 1572872 | tf_op jit(solution)/shard_map/ppermute | solution.py:25
  271.8 22.0 %collective-permute-start.39 = (bf16[1024,256]{1,0:T(8,128)(2,1)S(1)}, bf16[1024,256]{1,0:T(8,128)(2,1)S(1)}, u32[]{:S(2)}, u32[]{:S(2)}) collective-permute-start(bf16[1024,256]{1,0:T(8,128)(2,1)S(1)} %add.417), channel_id=1, source_target_pairs={{0,48},{16,0},{32,16},{48,32},{1,49},{17,1},{33,17},{49,33},{2,50}... | collective-permute-start | bytes 1572872 | tf_op jit(solution)/shard_map/ppermute | solution.py:25
  272.0 27.8 %collective-permute-start.36 = (bf16[1024,256]{1,0:T(8,128)(2,1)S(1)}, bf16[1024,256]{1,0:T(8,128)(2,1)S(1)}, u32[]{:S(2)}, u32[]{:S(2)}) collective-permute-start(bf16[1024,256]{1,0:T(8,128)(2,1)S(1)} %add.414), channel_id=1, source_target_pairs={{0,16},{16,32},{32,48},{48,0},{1,17},{17,33},{33,49},{49,1},{2,18}... | collective-permute-start | bytes 1572872 | tf_op jit(solution)/shard_map/ppermute | solution.py:25
  275.6 24.5 %collective-permute-start.66 = (bf16[2,64,1024]{2,1,0:T(8,128)(2,1)S(1)}, bf16[2,64,1024]{2,1,0:T(8,128)(2,1)S(1)}, u32[]{:S(2)}, u32[]{:S(2)}) collective-permute-start(bf16[2,64,1024]{2,1,0:T(8,128)(2,1)S(1)} %pad_maximum_fusion.3), channel_id=1, source_target_pairs={{0,48},{16,0},{32,16},{48,32},{1,49},{17,1},{33,17},{49,33},{2,50}... | collective-permute-start | bytes 786440 | tf_op jit(solution)/shard_map/ppermute | solution.py:25
  299.9 27.1 %collective-permute-start.46 = (bf16[1024,512]{1,0:T(8,128)(2,1)S(1)}, bf16[1024,512]{1,0:T(8,128)(2,1)S(1)}, u32[]{:S(2)}, u32[]{:S(2)}) collective-permute-start(bf16[1024,512]{1,0:T(8,128)(2,1)S(1)} %pad_maximum_fusion), channel_id=1, source_target_pairs={{0,64},{64,0},{1,65},{65,1},{2,66},{66,2},{3,67},{67,3},{4,68},{68... | collective-permute-start | bytes 3145736 | tf_op jit(solution)/shard_map/ppermute | solution.py:25
  (62 other events, 1037.2 us)

commit v2 on v0

v2 whole, which is shorter than its diff:
```python
import functools

import jax
import jax.numpy as jnp
from jax import lax
from jax.experimental import pallas as pl
from jax.experimental.pallas import tpu as pltpu
from jax.sharding import Mesh
from jax.sharding import PartitionSpec as P

BLK = 128
PORD = 8192
PIV = 2048
KH = PIV // 2
OWN = 384
STEP = 6
BF = jnp.bfloat16
F32 = jnp.float32
VMEM_LIMIT = 60 * 2**20
SMEM_SPEC = pl.BlockSpec(memory_space=pltpu.SMEM)
ANY_SPEC = pl.BlockSpec(memory_space=pl.ANY)
SIZE = {"h": 2, "y": 4, "x": 4, "z": 2, "c": 2}
AXES = ("h", "y", "x", "z", "c")
def shift(array, axis, step):
    size = SIZE[axis]
    return lax.ppermute(array, axis, [(i, (i + step) % size) for i in range(size)])


def mirrored(array, axis, step):
    size = SIZE[axis]
    pairs = [
        (i * 2 + core, (i + (step if core == 0 else -step)) % size * 2 + core)
        for i in range(size)
        for core in range(2)
    ]
    return lax.ppermute(array, (axis, "c"), pairs)


def after(value, *earlier):
    return lax.optimization_barrier((value,) + earlier)[0]


def factor_kernel(panel, inverse, out, held, sems):
    width = 512
    for j in range(PIV // width):
        deep = (j + 1) * width
        pltpu.make_async_copy(
            inverse.at[0, pl.ds(0, deep), pl.ds(j * width, width)],
            held.at[pl.ds(0, deep), pl.ds(j * width, width)],
            sems.at[j],
        ).start()
    for j in range(PIV // width):
        deep = (j + 1) * width
        pltpu.make_async_copy(
            inverse.at[0, pl.ds(0, deep), pl.ds(j * width, width)],
            held.at[pl.ds(0, deep), pl.ds(j * width, width)],
            sems.at[j],
        ).wait()
        out[:, j * width : deep] = jnp.dot(
            panel[0, :, :deep], held[:deep, j * width : deep], preferred_element_type=F32
        ).astype(BF)


def factor(panel, inverse):
    vmem = pl.BlockSpec(memory_space=pltpu.VMEM)
    return pl.pallas_call(
        factor_kernel,
        out_shape=jax.ShapeDtypeStruct((OWN, PIV), BF),
        in_specs=[vmem, ANY_SPEC],
        out_specs=vmem,
        scratch_shapes=[pltpu.VMEM((PIV, PIV), BF), pltpu.SemaphoreType.DMA((4,))],
        compiler_params=pltpu.CompilerParams(vmem_limit_bytes=VMEM_LIMIT),
        cost_estimate=pl.CostEstimate(
            flops=2_000_000_000, bytes_accessed=8_000_000, transcendentals=0
        ),
    )(panel, inverse)


def gather_rows(own, ready):
    w = mirrored(own, "x", 1)
    e = mirrored(own, "x", -1)
    z = shift(own, "z", 1)
    w, e, z, ready = lax.optimization_barrier((w, e, z, ready))
    core = shift(after(own, w), "c", 1)
    b = shift(w, "z", 1)
    q = mirrored(w, "x", 1)
    a = mirrored(z, "x", -1)
    core1 = shift(jnp.concatenate([after(w, core), e, z]), "c", 1)
    r = mirrored(b, "x", 1)
    last = [shift(v, "c", 1) for v in (q, a, b, r)]
    pieces, first = [], 0
    for array in (own, w, e, z, q, a, b, r, core, core1, *last):
        pieces.append((array, first, array.shape[0] // BLK))
        first += array.shape[0] // BLK
    return pieces, ready


PLACE = [[0, 3], [2, 5], [4, 7], [1, 6]]


def fetch(ins, pieces, block, dst, sem, first_row=0, count=BLK):
    for ref, (first, blocks) in zip(ins, pieces):

        @pl.when((block >= first) & (block < first + blocks))
        def _(ref=ref, first=first):
            row = pl.multiple_of((block - first) * BLK + first_row, 64)
            pltpu.make_async_copy(ref.at[pl.ds(row, count), :], dst, sem).start()


def fetched(ins, block, dst, sem, count=BLK):
    @pl.when(block < 0)
    def _():
        dst[...] = jnp.zeros((count, PIV), BF)

    @pl.when(block >= 0)
    def _():
        pltpu.make_async_copy(ins[0].at[pl.ds(0, count), :], dst, sem).wait()


def main_kernel(pieces, dest, chosen, *refs):
    n = len(pieces)
    ins, outs = refs[:n], refs[n : n + 16]
    rows, cols, placed, sem_in, sem_sel, sem_out = refs[n + 16 :]

    for m in range(4):
        fetch(ins, pieces, chosen[m], cols.at[pl.ds(m * BLK, BLK), :], sem_sel.at[m])

    def arrival(i):
        first, blocks = pieces[i]
        return pltpu.make_async_copy(
            ins[i], rows.at[pl.ds(first * BLK, blocks * BLK), :], sem_in.at[i]
        )

    for i in range(n):
        arrival(i).start()

    @pl.loop(0, PORD // 256)
    def _(i):
        for half in range(2):
            placed[half, pl.ds(pl.multiple_of(i * 256, 256), 256), :] = jnp.zeros((256, 256), BF)

    for m in range(4):
        fetched(ins, chosen[m], cols.at[pl.ds(m * BLK, BLK), :], sem_sel.at[m])

    def multiply(block, count):
        product = lax.dot_general(
            rows[pl.ds(block * BLK, count * BLK), :],
            cols[...],
            (((1,), (1,)), ((), ())),
            preferred_element_type=F32,
        )
        for b in range(count):
            at = pl.multiple_of(dest[block + b] * BLK, BLK)
            result = (-product[b * BLK : (b + 1) * BLK]).astype(BF)
            placed[0, pl.ds(at, BLK), :] = result[:, :256]
            placed[1, pl.ds(at, BLK), :] = result[:, 256:]

    done, at = 0, 0
    for i in range(n):
        arrival(i).wait()
        done += pieces[i][1]
        if (done - at) % STEP == 0:

            @pl.loop(0, (done - at) // STEP)
            def _(k, at=at):
                multiply(at + k * STEP, STEP)

            at = done

    def leaving(i):
        return pltpu.make_async_copy(
            placed.at[i % 2, pl.ds((i // 2) * 1024, 1024), :], outs[i], sem_out.at[i]
        )

    for i in range(16):
        leaving(i).start()
    for i in range(16):
        leaving(i).wait()


def main_parts(pieces, dest, chosen):
    arrays = [p[0] for p in pieces]
    n = len(arrays)
    outs = pl.pallas_call(
        functools.partial(main_kernel, [p[1:] for p in pieces]),
        out_shape=[jax.ShapeDtypeStruct((1024, 256), BF)] * 16,
        in_specs=[SMEM_SPEC] * 2 + [ANY_SPEC] * n,
        out_specs=[ANY_SPEC] * 16,
        scratch_shapes=[
            pltpu.VMEM((6144, PIV), BF),
            pltpu.VMEM((512, PIV), BF),
            pltpu.VMEM((2, PORD, 256), BF),
            pltpu.SemaphoreType.DMA((n,)),
            pltpu.SemaphoreType.DMA((4,)),
            pltpu.SemaphoreType.DMA((16,)),
        ],
        compiler_params=pltpu.CompilerParams(vmem_limit_bytes=VMEM_LIMIT),
        cost_estimate=pl.CostEstimate(
            flops=20_000_000_000, bytes_accessed=36_000_000, transcendentals=0
        ),
    )(dest, chosen, *arrays)
    return [[[outs[(dh * 4 + dy) * 2 + k] for k in range(2)] for dy in range(4)] for dh in range(2)]


def panel_kernel(pieces, pan_rows, pan_cols, offset, *refs):
    n = len(pieces)
    ins, out = refs[:n], refs[n]
    left, right, sem_left, sem_right = refs[n + 1 :]
    to_left = lambda q: left.at[pl.ds(q * 64, 64), :]
    to_right = lambda q: right.at[pl.ds(q * BLK, BLK), :]
    for q in range(8):
        fetch(ins, pieces, pan_rows[q], to_left(q), sem_left.at[q], offset[0], 64)
        fetch(ins, pieces, pan_cols[q], to_right(q), sem_right.at[q])
    for q in range(8):
        fetched(ins, pan_rows[q], to_left(q), sem_left.at[q], 64)
    for q in range(8):
        fetched(ins, pan_cols[q], to_right(q), sem_right.at[q])

    for part in range(4):
        product = lax.dot_general(
            left[...],
            right[pl.ds(part * 256, 256), :],
            (((1,), (1,)), ((), ())),
            preferred_element_type=F32,
        )
        out[:, part * 256 : (part + 1) * 256] = (-product).astype(BF)


def panel_parts(pieces, pan_rows, pan_cols, offset):
    arrays = [p[0] for p in pieces]
    n = len(arrays)
    return pl.pallas_call(
        functools.partial(panel_kernel, [p[1:] for p in pieces]),
        out_shape=jax.ShapeDtypeStruct((512, 1024), BF),
        in_specs=[SMEM_SPEC] * 3 + [ANY_SPEC] * n,
        out_specs=pl.BlockSpec(memory_space=pltpu.VMEM),
        scratch_shapes=[
            pltpu.VMEM((512, PIV), BF),
            pltpu.VMEM((1024, PIV), BF),
            pltpu.SemaphoreType.DMA((8,)),
            pltpu.SemaphoreType.DMA((8,)),
        ],
        compiler_params=pltpu.CompilerParams(vmem_limit_bytes=VMEM_LIMIT),
        cost_estimate=pl.CostEstimate(
            flops=2_200_000_000, bytes_accessed=8_000_000, transcendentals=0
        ),
    )(pan_rows, pan_cols, offset, *arrays)


def ring_sum(first, second):
    rings = (first, second)
    carried = [parts[3] for parts in rings]
    marks = []
    for k in (2, 1, 0):
        moved = [mirrored(v, "y", 1) for v in carried]
        marks.append(moved)
        carried = [parts[k].astype(F32) + v.astype(F32) for parts, v in zip(rings, moved)]
        if k > 0:
            carried = [v.astype(BF) for v in carried]
    return carried, marks


def pick(bit, when_zero, when_one):
    return jnp.where(bit == 0, when_zero, when_one)


def ordered_pair(bit, own, other):
    return jnp.stack([pick(bit, own, other), pick(bit, other, own)])


def ordered_ring(at, parts):
    twice = jnp.stack(list(parts) + list(parts))
    return lax.dynamic_slice_in_dim(twice, (4 - at) % 4, 4, 0)


def front_kernel(pivots, place, front, keep, send, zeros, sems):
    zeros[...] = jnp.zeros_like(zeros)
    for r in range(8):
        columns = pl.ds(r * BLK, BLK)
        local_block = pivots[r] - place[0] * 4
        mine = (local_block >= 0) & (local_block < 4)
        for k, out in enumerate((keep, send)):

            @pl.when(mine)
            def _(k=k, out=out, columns=columns, r=r):
                pltpu.make_async_copy(
                    front.at[:, place[1] ^ k, :, pl.ds(pl.multiple_of(local_block * BLK, BLK), BLK)],
                    out.at[:, :, columns],
                    sems.at[r, k],
                ).start()

            @pl.when(jnp.logical_not(mine))
            def _(k=k, out=out, columns=columns, r=r):
                pltpu.make_async_copy(zeros, out.at[:, :, columns], sems.at[r, k]).start()

    for r in range(8):
        for k, out in enumerate((keep, send)):
            pltpu.make_async_copy(zeros, out.at[:, :, pl.ds(r * BLK, BLK)], sems.at[r, k]).wait()


def front_pick(pivots, place, front):
    return pl.pallas_call(
        front_kernel,
        out_shape=[jax.ShapeDtypeStruct((8, 64, 1024), BF)] * 2,
        in_specs=[SMEM_SPEC] * 2 + [ANY_SPEC],
        out_specs=[ANY_SPEC] * 2,
        scratch_shapes=[pltpu.VMEM((8, 64, BLK), BF), pltpu.SemaphoreType.DMA((8, 2))],
        compiler_params=pltpu.CompilerParams(vmem_limit_bytes=VMEM_LIMIT),
    )(pivots, place, front.reshape(8, 2, 64, 512))


def local(child_panel, child_inverse, child_map, parent_front, parent_inverse, parent_pivots):
    h, y, x, z, c = (lax.axis_index(a) for a in AXES)
    sec = h * 4 + y
    dev = x * 4 + z * 2 + c

    my_map = lax.dynamic_index_in_dim(child_map, sec, 0, keepdims=False)
    place_table = jnp.array(PLACE, jnp.int32)
    child = jnp.arange(48, dtype=jnp.int32)
    owner = child // 3
    place = place_table[
        (owner // 4 - x) * (1 - 2 * (owner % 2)) % 4, (owner // 2 % 2) ^ z
    ]
    position = ((owner % 2) ^ c) * 24 + place * 3 + child % 3
    parent_row = my_map // 8
    slot = (((parent_row // 4) ^ h) * 4 + (parent_row % 4 - y) * (1 - 2 * c) % 4) * 8 + my_map % 8
    dest = jnp.sum(
        jnp.where(position[None, :] == child[:, None], slot[None, :], 0), axis=1, dtype=jnp.int32
    )

    def find(targets):
        hit = my_map[None, :] == targets[:, None]
        return jnp.sum(jnp.where(hit, position[None, :] + 1, 0), axis=1, dtype=jnp.int32) - 1

    chosen = find(dev * 4 + jnp.arange(4, dtype=jnp.int32))
    pan_rows = find(jnp.arange(8, dtype=jnp.int32) * 8 + dev // 2)
    pan_cols = find(parent_pivots)
    offset = (dev % 2 * 64).astype(jnp.int32).reshape(1)

    keep, send = front_pick(parent_pivots, jnp.stack([dev, c]).astype(jnp.int32), parent_front)
    front = (keep + shift(send, "c", 1)).reshape(4, 2, 64, 1024)
    front_x = [lax.dynamic_index_in_dim(front, (x + k) % 4, 0, keepdims=False) for k in range(4)]

    pieces, ready = gather_rows(
        factor(child_panel, child_inverse), (dest, chosen, pan_rows, pan_cols, offset, front_x)
    )
    dest, chosen, pan_rows, pan_cols, offset, front_x = ready

    pan = panel_parts(pieces, pan_rows, pan_cols, offset)
    arrived = lax.all_to_all(
        pan.reshape(8, 64, 1024), ("h", "y"), split_axis=0, concat_axis=0, tiled=True
    )
    main = main_parts(pieces, dest, chosen)

    front_x = [after(v, pan) for v in front_x]
    front_z = (
        front_x[0]
        + shift(front_x[1], "x", 1)
        + shift(front_x[3], "x", -1)
        + shift(front_x[2], "x", 2)
    )
    front_rows = pick(z, front_z[0], front_z[1]) + shift(pick(z, front_z[1], front_z[0]), "z", 1)

    arrived, main = lax.optimization_barrier((arrived, main))
    pan_rows_f = arrived.astype(F32).sum(axis=0) + front_rows.astype(F32)
    share = jnp.dot(pan_rows_f.astype(BF), parent_inverse, preferred_element_type=F32).astype(BF)

    far_in, near_in = ([[part[k] for part in main[d]] for k in range(2)] for d in (1, 0))
    far, marks = ring_sum(*far_in)
    near_in = [parts[:3] + [after(parts[3], mark)] for parts, mark in zip(near_in, marks[0])]
    far = [shift(v.astype(BF), "h", 1).astype(F32) for v in far]
    near, _ = ring_sum(*near_in)
    near = jnp.concatenate([n + f for n, f in zip(near, far)], axis=1)
    assembled = parent_front.astype(F32) + near

    row_block = sec * 8 + dev // 2
    masked = jnp.where(jnp.any(parent_pivots == row_block), jnp.zeros_like(share), share)
    masked = after(masked, marks[0][0])
    pairs = [(s * 16 + d, (d % 8) * 16 + 2 * s + d // 8) for s in range(8) for d in range(16)]
    moved = lax.ppermute(masked, AXES, pairs)
    ring = ordered_ring(y, [moved, shift(moved, "y", -1), shift(moved, "y", 2), shift(moved, "y", 1)])
    column_factor = ordered_pair(h, ring, shift(ring, "h", 1)).reshape(512, 1024)

    parent_factor = lax.all_gather(share, ("x", "z", "c"), axis=0, tiled=True)

    my_blocks = sec * 8 + jnp.arange(8, dtype=jnp.int32)
    is_pivot = jnp.any(parent_pivots[None, :] == my_blocks[:, None], axis=1)
    row_pivot = jnp.repeat(is_pivot, BLK)
    trailing = jnp.where(row_pivot[:, None], jnp.zeros_like(parent_factor), parent_factor)
    update = lax.dot_general(
        trailing, column_factor, (((1,), (1,)), ((), ())), preferred_element_type=F32
    )
    return assembled - update, parent_factor


def solution(mesh):
    fine = Mesh(mesh.devices.reshape(tuple(SIZE[a] for a in AXES)), AXES)
    sec, dev = ("h", "y"), ("x", "z", "c")
    placed = (P(sec, dev, None), P(sec, None, None), P(), P(sec, dev), P(), P())
    return jax.shard_map(
        local,
        mesh=fine,
        in_specs=placed,
        out_specs=(P(sec, dev), P(sec, None)),
        check_vma=False,
    )
```

time: 537 us -> 285 us (0.53)
  the two profiles are of different devices: /device:TPU:18 before, /device:TPU:37 now
where the time goes in v2:
time: 285 us; the launch traced here: 284 us
  waiting for transfers between devices  117 us (41%)
  starting transfers between devices  85.4 us (30%)
  Pallas kernels  37.9 us (13%)
  other arithmetic  18.6 us (7%)
  between operations  14.5 us (5%)
  matrix products  7 us (2%)
  local copies, waits for them, and re-layouts  3.6 us (1%)
    ppermute x17, waiting for transfers between devices, mirrored(): return lax.ppermute(array, (axis, 'c'), pairs)  58.2 us
    ppermute x19, waiting for transfers between devices, shift(): lax.ppermute(array, axis, [(i, (i + step) % size) for i in range(size)])  57.9 us
    ppermute x19, starting transfers between devices, shift(): lax.ppermute(array, axis, [(i, (i + step) % size) for i in range(size)])  52.8 us
    ppermute x17, starting transfers between devices, mirrored(): return lax.ppermute(array, (axis, 'c'), pairs)  24.3 us
    pallas_call x1, Pallas kernels, main_parts(): pl.pallas_call(functools.partial(main_kernel, [p[1:] for p in pieces]), o...  22.3 us
    pallas_call x1, Pallas kernels, panel_parts(): pl.pallas_call(functools.partial(panel_kernel, [p[1:] for p in pieces]),...  6.98 us
    pallas_call x1, Pallas kernels, factor(): pl.pallas_call(factor_kernel, out_shape=jax.ShapeDtypeStruct((OWN, PIV),...  6.49 us
    all_to_all x1, starting transfers between devices, local(): lax.all_to_all(pan.reshape(8, 64, 1024), ('h', 'y'), split_axis=0, concat...  6.33 us
  transfers between devices with their start and end apart: 39, of which 20 were waited for; matrix products, arithmetic and copies ran while one was open for 8% of the time, Pallas kernels for 9%

profile of v2, /device:TPU:37, one launch (start us, length us, event | category | flops | bytes accessed | tf_op | source)
XLA Modules:
  0.0 284.4 jit_solution(2035065628510132128)
XLA Ops:
  7.2 6.5 %shard_map.86.refs_0_ = bf16[384,2048]{1,0:T(8,128)(2,1)} custom-call(bf16[1,384,2048]{2,1,0:T(8,128)(2,1)} %panel.1, bf16[1,2048,2048]{2,1,0:T(8,128)(2,1)} %inverse.1), custom_call_target="tpu_custom_call" | custom-call | flops 2000000000 | bytes 8000000 | tf_op jit(solution)/shard_map/pallas_call | solution.py:66
  18.0 9.2 %collective-permute-start.3 = (bf16[8,64,1024]{2,1,0:T(8,128)(2,1)}, bf16[8,64,1024]{2,1,0:T(8,128)(2,1)S(1)}, u32[]{:S(2)}, u32[]{:S(2)}) collective-permute-start(bf16[8,64,1024]{2,1,0:T(8,128)(2,1)} %get-tuple-element.59), channel_id=1, source_target_pairs={{0,1},{1,0},{2,3},{3,2},{4,5},{5,4},{6,7},{7,6},{8,9},{9,8},{10,11... | collective-permute-start | bytes 3145736 | tf_op jit(solution)/shard_map/ppermute | solution.py:26
  34.2 13.9 %collective-permute-done.refs_1_ = bf16[384,2048]{1,0:T(8,128)(2,1)} collective-permute-done((bf16[384,2048]{1,0:T(8,128)(2,1)}, bf16[384,2048]{1,0:T(8,128)(2,1)}, u32[]{:S(2)}, u32[]{:S(2)}) %collective-permute-start) | collective-permute-done | bytes 1572896 | tf_op jit(solution)/shard_map/ppermute | solution.py:36
  52.4 3.1 %collective-permute-done.8.refs_8_ = bf16[384,2048]{1,0:T(8,128)(2,1)} collective-permute-done((bf16[384,2048]{1,0:T(8,128)(2,1)S(1)}, bf16[384,2048]{1,0:T(8,128)(2,1)}, u32[]{:S(2)}, u32[]{:S(2)}) %collective-permute-start.8) | collective-permute-done | bytes 1572896 | tf_op jit(solution)/shard_map/ppermute | solution.py:26
  55.5 4.0 %pad_maximum_fusion = bf16[1152,2048]{1,0:T(8,128)(2,1)} fusion(bf16[384,2048]{1,0:T(8,128)(2,1)} %collective-permute-done.2.refs_3_, bf16[384,2048]{1,0:T(8,128)(2,1)} %collective-permute-done.1.refs_2_, bf16[384,2048]{1,0:T(8,128)(2,1)} %collective-permute-done.refs_1_), kind=kLoop, calls=%fused_computation.1 | loop fusion | flops 14155776 | bytes 9437184 | tf_op jit(solution)/shard_map/concatenate | solution.py:88
  62.1 26.6 %collective-permute-done.6.refs_6_ = bf16[384,2048]{1,0:T(8,128)(2,1)} collective-permute-done((bf16[384,2048]{1,0:T(8,128)(2,1)}, bf16[384,2048]{1,0:T(8,128)(2,1)}, u32[]{:S(2)}, u32[]{:S(2)}) %collective-permute-start.6) | collective-permute-done | bytes 1572896 | tf_op jit(solution)/shard_map/ppermute | solution.py:26
  89.0 2.9 %collective-permute-start.12 = (bf16[384,2048]{1,0:T(8,128)(2,1)}, bf16[384,2048]{1,0:T(8,128)(2,1)}, u32[]{:S(2)}, u32[]{:S(2)}) collective-permute-start(bf16[384,2048]{1,0:T(8,128)(2,1)} %collective-permute-done.6.refs_6_), channel_id=1, source_target_pairs={{0,1},{1,0},{2,3},{3,2},{4,5},{5,4},{6,7},{7,6},{8,9},{9,8},{10,11... | collective-permute-start | bytes 4718600 | tf_op jit(solution)/shard_map/ppermute | solution.py:26
  91.9 3.0 %collective-permute-done.4.refs_4_ = bf16[384,2048]{1,0:T(8,128)(2,1)} collective-permute-done((bf16[384,2048]{1,0:T(8,128)(2,1)}, bf16[384,2048]{1,0:T(8,128)(2,1)}, u32[]{:S(2)}, u32[]{:S(2)}) %collective-permute-start.4) | collective-permute-done | bytes 1572896 | tf_op jit(solution)/shard_map/ppermute | solution.py:36
  97.3 2.8 collective-permute-start.11
  100.1 13.7 %collective-permute-done.7.refs_7_ = bf16[384,2048]{1,0:T(8,128)(2,1)} collective-permute-done((bf16[384,2048]{1,0:T(8,128)(2,1)}, bf16[384,2048]{1,0:T(8,128)(2,1)}, u32[]{:S(2)}, u32[]{:S(2)}) %collective-permute-start.7) | collective-permute-done | bytes 1572896 | tf_op jit(solution)/shard_map/ppermute | solution.py:36
  115.1 2.5 collective-permute-done.13.refs_13_
  117.6 7.0 %shard_map.88 = bf16[512,1024]{1,0:T(8,128)(2,1)} custom-call(s32[8]{0:T(128)} %get-tuple-element.60.pan_rows, s32[8]{0:T(128)} %get-tuple-element.61.pan_cols, s32[1]{0:T(128)} %bitcast.3.offset, bf16[384,2048]{1,0:T(8,128)(2,1)} %shard_map.86.refs_0_, bf16[384,2048]{1,0:T(8,128)(2,1)} %collective-permute-done.refs_1_, ...), custom_call_target="tpu_custom_call" | custom-call | flops 2200000000 | bytes 8000000 | tf_op jit(solution)/shard_map/pallas_call | solution.py:232
  124.6 2.6 collective-permute-start.28
  127.2 2.9 %collective-permute-start.30 = (bf16[2,64,1024]{2,1,0:T(8,128)(2,1)S(1)}, bf16[2,64,1024]{2,1,0:T(8,128)(2,1)}, u32[]{:S(2)}, u32[]{:S(2)}) collective-permute-start(bf16[2,64,1024]{2,1,0:T(8,128)(2,1)S(1)} %get-tuple-element.112), channel_id=1, source_target_pairs={{0,8},{4,12},{8,0},{12,4},{1,9},{5,13},{9,1},{13,5},{2,10},{6,14},... | collective-permute-start | bytes 786440 | tf_op jit(solution)/shard_map/ppermute | solution.py:26
  130.1 6.3 %all-to-all-start = ((bf16[8,64,1024]{2,1,0:T(8,128)(2,1)}), bf16[8,64,1024]{2,1,0:T(8,128)(2,1)S(1)}, u32[]{:S(2)}, u32[]{:S(2)}) async-start(bf16[8,64,1024]{2,1,0:T(8,128)(2,1)} %bitcast.51), calls=%async_computation | async-start | bytes 2097152 | tf_op jit(solution)/shard_map/all_to_all | solution.py:350
  136.5 22.3 %shard_map.89 = (bf16[1024,256]{1,0:T(8,128)(2,1)}, bf16[1024,256]{1,0:T(8,128)(2,1)}, bf16[1024,256]{1,0:T(8,128)(2,1)}, bf16[1024,256]{1,0:T(8,128)(2,1)}, bf1...) custom-call(s32[48]{0:T(128)} %select_reduce_fusion.dest, ...), custom_call_target="tpu_custom_call" | custom-call | flops 20000000000 | bytes 36000000 | tf_op jit(solution)/shard_map/pallas_call | solution.py:184
  160.1 7.6 %collective-permute-start.14 = (bf16[1024,256]{1,0:T(8,128)(2,1)}, bf16[1024,256]{1,0:T(8,128)(2,1)}, u32[]{:S(2)}, u32[]{:S(2)}) collective-permute-start(bf16[1024,256]{1,0:T(8,128)(2,1)} %get-tuple-element.90), channel_id=1, source_target_pairs={{0,16},{1,49},{16,32},{17,1},{32,48},{33,17},{48,0},{49,33},{2,18}... | collective-permute-start | bytes 1572872 | tf_op jit(solution)/shard_map/ppermute | solution.py:36
  168.0 3.9 %collective-permute-done.31 = bf16[64,1024]{1,0:T(8,128)(2,1)S(1)} collective-permute-done((bf16[64,1024]{1,0:T(8,128)(2,1)S(1)}, bf16[64,1024]{1,0:T(8,128)(2,1)S(1)}, u32[]{:S(2)}, u32[]{:S(2)}) %collective-permute-start.31) | collective-permute-done | bytes 131104 | tf_op jit(solution)/shard_map/ppermute | solution.py:26
  176.0 3.4 %collective-permute-start.15 = (bf16[1024,256]{1,0:T(8,128)(2,1)}, bf16[1024,256]{1,0:T(8,128)(2,1)S(1)}, u32[]{:S(2)}, u32[]{:S(2)}) collective-permute-start(bf16[1024,256]{1,0:T(8,128)(2,1)} %get-tuple-element.91), channel_id=1, source_target_pairs={{0,16},{1,49},{16,32},{17,1},{32,48},{33,17},{48,0},{49,33},{2,18}... | collective-permute-start | bytes 1572872 | tf_op jit(solution)/shard_map/ppermute | solution.py:36
  185.3 9.4 %collective-permute-start.33 = (bf16[64,1024]{1,0:T(8,128)(2,1)S(1)}, bf16[64,1024]{1,0:T(8,128)(2,1)S(1)}, u32[]{:S(2)}, u32[]{:S(2)}) collective-permute-start(bf16[64,1024]{1,0:T(8,128)(2,1)S(1)} %collective-permute-done.32), channel_id=1, source_target_pairs={{0,48},{16,0},{32,16},{48,32},{1,49},{17,1},{33,17},{49,33},{2,50}... | collective-permute-start | bytes 393224 | tf_op jit(solution)/shard_map/ppermute | solution.py:26
  194.7 12.1 %collective-permute-done.33 = bf16[64,1024]{1,0:T(8,128)(2,1)S(1)} collective-permute-done((bf16[64,1024]{1,0:T(8,128)(2,1)S(1)}, bf16[64,1024]{1,0:T(8,128)(2,1)S(1)}, u32[]{:S(2)}, u32[]{:S(2)}) %collective-permute-start.33) | collective-permute-done | bytes 131104 | tf_op jit(solution)/shard_map/ppermute | solution.py:26
  208.8 4.2 %collective-permute-done.34 = bf16[64,1024]{1,0:T(8,128)(2,1)S(1)} collective-permute-done((bf16[64,1024]{1,0:T(8,128)(2,1)S(1)}, bf16[64,1024]{1,0:T(8,128)(2,1)S(1)}, u32[]{:S(2)}, u32[]{:S(2)}) %collective-permute-start.34) | collective-permute-done | bytes 131104 | tf_op jit(solution)/shard_map/ppermute | solution.py:26
  213.0 5.0 %collective-permute-done.35 = bf16[64,1024]{1,0:T(8,128)(2,1)S(1)} collective-permute-done((bf16[64,1024]{1,0:T(8,128)(2,1)S(1)}, bf16[64,1024]{1,0:T(8,128)(2,1)S(1)}, u32[]{:S(2)}, u32[]{:S(2)}) %collective-permute-start.35) | collective-permute-done | bytes 131104 | tf_op jit(solution)/shard_map/ppermute | solution.py:26
  218.1 15.3 %collective-permute-start.36 = (bf16[4,64,1024]{2,1,0:T(8,128)(2,1)S(1)}, bf16[4,64,1024]{2,1,0:T(8,128)(2,1)S(1)}, u32[]{:S(2)}, u32[]{:S(2)}) collective-permute-start(bf16[4,64,1024]{2,1,0:T(8,128)(2,1)S(1)} %constant_dynamic-slice_fusion), channel_id=1, source_target_pairs={{0,64},{64,0},{1,65},{65,1},{2,66},{66,2},{3,67},{67,3},{4,68},{68... | collective-permute-start | bytes 1572872 | tf_op jit(solution)/shard_map/ppermute | solution.py:26
  235.1 2.7 collective-permute-start.26
  237.9 4.1 %collective-permute-done.16 = bf16[1024,256]{1,0:T(8,128)(2,1)S(1)} collective-permute-done((bf16[1024,256]{1,0:T(8,128)(2,1)S(1)}, bf16[1024,256]{1,0:T(8,128)(2,1)S(1)}, u32[]{:S(2)}, u32[]{:S(2)}) %collective-permute-start.16) | collective-permute-done | bytes 524320 | tf_op jit(solution)/shard_map/ppermute | solution.py:36
  243.8 3.8 %collective-permute-done.19 = bf16[1024,256]{1,0:T(8,128)(2,1)S(1)} collective-permute-done((bf16[1024,256]{1,0:T(8,128)(2,1)S(1)}, bf16[1024,256]{1,0:T(8,128)(2,1)S(1)}, u32[]{:S(2)}, u32[]{:S(2)}) %collective-permute-start.19) | collective-permute-done | bytes 524320 | tf_op jit(solution)/shard_map/ppermute | solution.py:36
  247.9 5.4 %collective-permute-done.23 = bf16[1024,256]{1,0:T(8,128)(2,1)S(1)} collective-permute-done((bf16[1024,256]{1,0:T(8,128)(2,1)S(1)}, bf16[1024,256]{1,0:T(8,128)(2,1)S(1)}, u32[]{:S(2)}, u32[]{:S(2)}) %collective-permute-start.23) | collective-permute-done | bytes 524320 | tf_op jit(solution)/shard_map/ppermute | solution.py:36
  255.1 3.8 %collective-permute-done.26 = bf16[1024,256]{1,0:T(8,128)(2,1)S(1)} collective-permute-done((bf16[1024,256]{1,0:T(8,128)(2,1)S(1)}, bf16[1024,256]{1,0:T(8,128)(2,1)S(1)}, u32[]{:S(2)}, u32[]{:S(2)}) %collective-permute-start.26) | collective-permute-done | bytes 524320 | tf_op jit(solution)/shard_map/ppermute | solution.py:36
  260.3 3.9 %collective-permute-done.17 = bf16[1024,256]{1,0:T(8,128)(2,1)S(1)} collective-permute-done((bf16[1024,256]{1,0:T(8,128)(2,1)S(1)}, bf16[1024,256]{1,0:T(8,128)(2,1)S(1)}, u32[]{:S(2)}, u32[]{:S(2)}) %collective-permute-start.17) | collective-permute-done | bytes 524320 | tf_op jit(solution)/shard_map/ppermute | solution.py:36
  265.3 4.5 %collective-permute-done.24 = bf16[1024,256]{1,0:T(8,128)(2,1)S(1)} collective-permute-done((bf16[1024,256]{1,0:T(8,128)(2,1)S(1)}, bf16[1024,256]{1,0:T(8,128)(2,1)S(1)}, u32[]{:S(2)}, u32[]{:S(2)}) %collective-permute-start.24) | collective-permute-done | bytes 524320 | tf_op jit(solution)/shard_map/ppermute | solution.py:36
  270.9 5.3 %fusion = f32[1024,512]{1,0:T(8,128)} fusion(f32[1024,256]{1,0:T(8,128)} %convert_add_fusion, f32[1024,256]{1,0:T(8,128)} %convert_add_fusion.1, bf16[1024,512]{1,0:T(8,128)(2,1)S(1)} %copy-done.5, bf16[512,1024]{1,0:T(8,128)(2,1)} %bitcast.53, bf16[1024,1024]{1,0:T(8,128)(2,1)} %all-gather.2.cloned.1.call-done, pred[1024]{0:T(1024)(128)(4,1)S(1)} %broadcast_bitcast_fusion), kind=kOutput, calls=%fused_computation.3 | convolution fusion | flops 1076887552 | bytes 8389632 | tf_op jit(solution)/shard_map/dot_general | solution.py:390
  (135 shorter events, 45.9 us)
Async XLA Ops:
  13.7 34.4 %collective-permute-start = (bf16[384,2048]{1,0:T(8,128)(2,1)}, bf16[384,2048]{1,0:T(8,128)(2,1)}, u32[]{:S(2)}, u32[]{:S(2)}) collective-permute-start(bf16[384,2048]{1,0:T(8,128)(2,1)} %shard_map.86.refs_0_), channel_id=1, source_target_pairs={{0,4},{1,13},{4,8},{5,1},{8,12},{9,5},{12,0},{13,9},{2,6},{3,15},{... | collective-permute-start | bytes 4718600 | tf_op jit(solution)/shard_map/ppermute | solution.py:36
  14.0 35.9 %collective-permute-start.1 = (bf16[384,2048]{1,0:T(8,128)(2,1)}, bf16[384,2048]{1,0:T(8,128)(2,1)}, u32[]{:S(2)}, u32[]{:S(2)}) collective-permute-start(bf16[384,2048]{1,0:T(8,128)(2,1)} %shard_map.86.refs_0_), channel_id=1, source_target_pairs={{0,12},{1,5},{4,0},{5,9},{8,4},{9,13},{12,8},{13,1},{2,14},{3,7},{... | collective-permute-start | bytes 4718600 | tf_op jit(solution)/shard_map/ppermute | solution.py:36
  15.2 35.0 %collective-permute-start.2 = (bf16[384,2048]{1,0:T(8,128)(2,1)}, bf16[384,2048]{1,0:T(8,128)(2,1)}, u32[]{:S(2)}, u32[]{:S(2)}) collective-permute-start(bf16[384,2048]{1,0:T(8,128)(2,1)} %shard_map.86.refs_0_), channel_id=1, source_target_pairs={{0,2},{2,0},{1,3},{3,1},{4,6},{6,4},{5,7},{7,5},{8,10},{10,8},{9,1... | collective-permute-start | bytes 4718600 | tf_op jit(solution)/shard_map/ppermute | solution.py:26
  18.0 13.5 %collective-permute-start.3 = (bf16[8,64,1024]{2,1,0:T(8,128)(2,1)}, bf16[8,64,1024]{2,1,0:T(8,128)(2,1)S(1)}, u32[]{:S(2)}, u32[]{:S(2)}) collective-permute-start(bf16[8,64,1024]{2,1,0:T(8,128)(2,1)} %get-tuple-element.59), channel_id=1, source_target_pairs={{0,1},{1,0},{2,3},{3,2},{4,5},{5,4},{6,7},{7,6},{8,9},{9,8},{10,11... | collective-permute-start | bytes 3145736 | tf_op jit(solution)/shard_map/ppermute | solution.py:26
  52.4 36.3 %collective-permute-start.6 = (bf16[384,2048]{1,0:T(8,128)(2,1)}, bf16[384,2048]{1,0:T(8,128)(2,1)}, u32[]{:S(2)}, u32[]{:S(2)}) collective-permute-start(bf16[384,2048]{1,0:T(8,128)(2,1)} %collective-permute-done.refs_1_), channel_id=1, source_target_pairs={{0,2},{2,0},{1,3},{3,1},{4,6},{6,4},{5,7},{7,5},{8,10},{10,8},{9,1... | collective-permute-start | bytes 4718600 | tf_op jit(solution)/shard_map/ppermute | solution.py:26
  59.6 58.1 %collective-permute-start.9 = (bf16[1152,2048]{1,0:T(8,128)(2,1)}, bf16[1152,2048]{1,0:T(8,128)(2,1)}, u32[]{:S(2)}, u32[]{:S(2)}) collective-permute-start(bf16[1152,2048]{1,0:T(8,128)(2,1)} %pad_maximum_fusion), channel_id=1, source_target_pairs={{0,1},{1,0},{2,3},{3,2},{4,5},{5,4},{6,7},{7,6},{8,9},{9,8},{10,11... | collective-permute-start | bytes 14155784 | tf_op jit(solution)/shard_map/ppermute | solution.py:26
  59.9 35.0 %collective-permute-start.4 = (bf16[384,2048]{1,0:T(8,128)(2,1)}, bf16[384,2048]{1,0:T(8,128)(2,1)}, u32[]{:S(2)}, u32[]{:S(2)}) collective-permute-start(bf16[384,2048]{1,0:T(8,128)(2,1)} %collective-permute-done.refs_1_), channel_id=1, source_target_pairs={{0,4},{1,13},{4,8},{5,1},{8,12},{9,5},{12,0},{13,9},{2,6},{3,15},{... | collective-permute-start | bytes 4718600 | tf_op jit(solution)/shard_map/ppermute | solution.py:36
  60.2 37.1 %collective-permute-start.5 = (bf16[384,2048]{1,0:T(8,128)(2,1)}, bf16[384,2048]{1,0:T(8,128)(2,1)}, u32[]{:S(2)}, u32[]{:S(2)}) collective-permute-start(bf16[384,2048]{1,0:T(8,128)(2,1)} %collective-permute-done.2.refs_3_), channel_id=1, source_target_pairs={{0,12},{1,5},{4,0},{5,9},{8,4},{9,13},{12,8},{13,1},{2,14},{3,7},{... | collective-permute-start | bytes 4718600 | tf_op jit(solution)/shard_map/ppermute | solution.py:36
  88.7 25.2 %collective-permute-start.7 = (bf16[384,2048]{1,0:T(8,128)(2,1)}, bf16[384,2048]{1,0:T(8,128)(2,1)}, u32[]{:S(2)}, u32[]{:S(2)}) collective-permute-start(bf16[384,2048]{1,0:T(8,128)(2,1)} %collective-permute-done.6.refs_6_), channel_id=1, source_target_pairs={{0,4},{1,13},{4,8},{5,1},{8,12},{9,5},{12,0},{13,9},{2,6},{3,15},{... | collective-permute-start | bytes 4718600 | tf_op jit(solution)/shard_map/ppermute | solution.py:36
  89.0 26.1 %collective-permute-start.12 = (bf16[384,2048]{1,0:T(8,128)(2,1)}, bf16[384,2048]{1,0:T(8,128)(2,1)}, u32[]{:S(2)}, u32[]{:S(2)}) collective-permute-start(bf16[384,2048]{1,0:T(8,128)(2,1)} %collective-permute-done.6.refs_6_), channel_id=1, source_target_pairs={{0,1},{1,0},{2,3},{3,2},{4,5},{5,4},{6,7},{7,6},{8,9},{9,8},{10,11... | collective-permute-start | bytes 4718600 | tf_op jit(solution)/shard_map/ppermute | solution.py:26
  94.9 20.2 %collective-permute-start.10 = (bf16[384,2048]{1,0:T(8,128)(2,1)}, bf16[384,2048]{1,0:T(8,128)(2,1)}, u32[]{:S(2)}, u32[]{:S(2)}) collective-permute-start(bf16[384,2048]{1,0:T(8,128)(2,1)} %collective-permute-done.4.refs_4_), channel_id=1, source_target_pairs={{0,1},{1,0},{2,3},{3,2},{4,5},{5,4},{6,7},{7,6},{8,9},{9,8},{10,11... | collective-permute-start | bytes 4718600 | tf_op jit(solution)/shard_map/ppermute | solution.py:26
  97.3 17.8 %collective-permute-start.11 = (bf16[384,2048]{1,0:T(8,128)(2,1)}, bf16[384,2048]{1,0:T(8,128)(2,1)}, u32[]{:S(2)}, u32[]{:S(2)}) collective-permute-start(bf16[384,2048]{1,0:T(8,128)(2,1)} %collective-permute-done.5.refs_5_), channel_id=1, source_target_pairs={{0,1},{1,0},{2,3},{3,2},{4,5},{5,4},{6,7},{7,6},{8,9},{9,8},{10,11... | collective-permute-start | bytes 4718600 | tf_op jit(solution)/shard_map/ppermute | solution.py:26
  124.6 34.2 %collective-permute-start.28 = (bf16[2,64,1024]{2,1,0:T(8,128)(2,1)}, bf16[2,64,1024]{2,1,0:T(8,128)(2,1)}, u32[]{:S(2)}, u32[]{:S(2)}) collective-permute-start(bf16[2,64,1024]{2,1,0:T(8,128)(2,1)} %get-tuple-element.108), channel_id=1, source_target_pairs={{0,4},{4,8},{8,12},{12,0},{1,5},{5,9},{9,13},{13,1},{2,6},{6,10},{... | collective-permute-start | bytes 786440 | tf_op jit(solution)/shard_map/ppermute | solution.py:26
  127.2 31.7 %collective-permute-start.29 = (bf16[2,64,1024]{2,1,0:T(8,128)(2,1)}, bf16[2,64,1024]{2,1,0:T(8,128)(2,1)}, u32[]{:S(2)}, u32[]{:S(2)}) collective-permute-start(bf16[2,64,1024]{2,1,0:T(8,128)(2,1)} %get-tuple-element.110), channel_id=1, source_target_pairs={{0,12},{4,0},{8,4},{12,8},{1,13},{5,1},{9,5},{13,9},{2,14},{6,2},{... | collective-permute-start | bytes 786440 | tf_op jit(solution)/shard_map/ppermute | solution.py:26
  127.2 31.7 %collective-permute-start.30 = (bf16[2,64,1024]{2,1,0:T(8,128)(2,1)S(1)}, bf16[2,64,1024]{2,1,0:T(8,128)(2,1)}, u32[]{:S(2)}, u32[]{:S(2)}) collective-permute-start(bf16[2,64,1024]{2,1,0:T(8,128)(2,1)S(1)} %get-tuple-element.112), channel_id=1, source_target_pairs={{0,8},{4,12},{8,0},{12,4},{1,9},{5,13},{9,1},{13,5},{2,10},{6,14},... | collective-permute-start | bytes 786440 | tf_op jit(solution)/shard_map/ppermute | solution.py:26
  130.1 29.9 %all-to-all-start = ((bf16[8,64,1024]{2,1,0:T(8,128)(2,1)}), bf16[8,64,1024]{2,1,0:T(8,128)(2,1)S(1)}, u32[]{:S(2)}, u32[]{:S(2)}) async-start(bf16[8,64,1024]{2,1,0:T(8,128)(2,1)} %bitcast.51), calls=%async_computation | async-start | bytes 2097152 | tf_op jit(solution)/shard_map/all_to_all | solution.py:350
  136.5 134.5 %all-gather.2.cloned.1.call-start = ((), (), s32[]{:S(2)}) async-start(), calls=%async_computation.1 | async-start | bytes 2228224 | tf_op jit(solution)/shard_map/all_gather | solution.py:384
  160.1 14.0 %collective-permute-start.14 = (bf16[1024,256]{1,0:T(8,128)(2,1)}, bf16[1024,256]{1,0:T(8,128)(2,1)}, u32[]{:S(2)}, u32[]{:S(2)}) collective-permute-start(bf16[1024,256]{1,0:T(8,128)(2,1)} %get-tuple-element.90), channel_id=1, source_target_pairs={{0,16},{1,49},{16,32},{17,1},{32,48},{33,17},{48,0},{49,33},{2,18}... | collective-permute-start | bytes 1572872 | tf_op jit(solution)/shard_map/ppermute | solution.py:36
  167.8 13.1 %collective-permute-start.21 = (bf16[1024,256]{1,0:T(8,128)(2,1)}, bf16[1024,256]{1,0:T(8,128)(2,1)}, u32[]{:S(2)}, u32[]{:S(2)}) collective-permute-start(bf16[1024,256]{1,0:T(8,128)(2,1)} %get-tuple-element.99), channel_id=1, source_target_pairs={{0,16},{1,49},{16,32},{17,1},{32,48},{33,17},{48,0},{49,33},{2,18}... | collective-permute-start | bytes 1572872 | tf_op jit(solution)/shard_map/ppermute | solution.py:36
  174.1 11.2 %collective-permute-start.32 = (bf16[64,1024]{1,0:T(8,128)(2,1)S(1)}, bf16[64,1024]{1,0:T(8,128)(2,1)S(1)}, u32[]{:S(2)}, u32[]{:S(2)}) collective-permute-start(bf16[64,1024]{1,0:T(8,128)(2,1)S(1)} %get-tuple-element.113), channel_id=1, source_target_pairs={{0,0},{1,16},{2,32},{3,48},{4,64},{5,80},{6,96},{7,112},{8,1},{9,1... | collective-permute-start | bytes 393224 | tf_op jit(solution)/shard_map/ppermute | solution.py:380
  176.0 57.4 %collective-permute-start.15 = (bf16[1024,256]{1,0:T(8,128)(2,1)}, bf16[1024,256]{1,0:T(8,128)(2,1)S(1)}, u32[]{:S(2)}, u32[]{:S(2)}) collective-permute-start(bf16[1024,256]{1,0:T(8,128)(2,1)} %get-tuple-element.91), channel_id=1, source_target_pairs={{0,16},{1,49},{16,32},{17,1},{32,48},{33,17},{48,0},{49,33},{2,18}... | collective-permute-start | bytes 1572872 | tf_op jit(solution)/shard_map/ppermute | solution.py:36
  180.8 53.5 %collective-permute-start.18 = (bf16[1024,256]{1,0:T(8,128)(2,1)S(1)}, bf16[1024,256]{1,0:T(8,128)(2,1)S(1)}, u32[]{:S(2)}, u32[]{:S(2)}) collective-permute-start(bf16[1024,256]{1,0:T(8,128)(2,1)S(1)} %add_convert_fusion.7), channel_id=1, source_target_pairs={{0,16},{1,49},{16,32},{17,1},{32,48},{33,17},{48,0},{49,33},{2,18}... | collective-permute-start | bytes 1572872 | tf_op jit(solution)/shard_map/ppermute | solution.py:36
  180.9 53.6 %collective-permute-start.22 = (bf16[1024,256]{1,0:T(8,128)(2,1)}, bf16[1024,256]{1,0:T(8,128)(2,1)S(1)}, u32[]{:S(2)}, u32[]{:S(2)}) collective-permute-start(bf16[1024,256]{1,0:T(8,128)(2,1)} %get-tuple-element.100), channel_id=1, source_target_pairs={{0,16},{1,49},{16,32},{17,1},{32,48},{33,17},{48,0},{49,33},{2,18}... | collective-permute-start | bytes 1572872 | tf_op jit(solution)/shard_map/ppermute | solution.py:36
  184.0 51.0 %collective-permute-start.25 = (bf16[1024,256]{1,0:T(8,128)(2,1)S(1)}, bf16[1024,256]{1,0:T(8,128)(2,1)S(1)}, u32[]{:S(2)}, u32[]{:S(2)}) collective-permute-start(bf16[1024,256]{1,0:T(8,128)(2,1)S(1)} %add_convert_fusion.2), channel_id=1, source_target_pairs={{0,16},{1,49},{16,32},{17,1},{32,48},{33,17},{48,0},{49,33},{2,18}... | collective-permute-start | bytes 1572872 | tf_op jit(solution)/shard_map/ppermute | solution.py:36
  185.3 21.6 %collective-permute-start.33 = (bf16[64,1024]{1,0:T(8,128)(2,1)S(1)}, bf16[64,1024]{1,0:T(8,128)(2,1)S(1)}, u32[]{:S(2)}, u32[]{:S(2)}) collective-permute-start(bf16[64,1024]{1,0:T(8,128)(2,1)S(1)} %collective-permute-done.32), channel_id=1, source_target_pairs={{0,48},{16,0},{32,16},{48,32},{1,49},{17,1},{33,17},{49,33},{2,50}... | collective-permute-start | bytes 393224 | tf_op jit(solution)/shard_map/ppermute | solution.py:26
  218.1 41.0 %collective-permute-start.36 = (bf16[4,64,1024]{2,1,0:T(8,128)(2,1)S(1)}, bf16[4,64,1024]{2,1,0:T(8,128)(2,1)S(1)}, u32[]{:S(2)}, u32[]{:S(2)}) collective-permute-start(bf16[4,64,1024]{2,1,0:T(8,128)(2,1)S(1)} %constant_dynamic-slice_fusion), channel_id=1, source_target_pairs={{0,64},{64,0},{1,65},{65,1},{2,66},{66,2},{3,67},{67,3},{4,68},{68... | collective-permute-start | bytes 1572872 | tf_op jit(solution)/shard_map/ppermute | solution.py:26
  234.4 13.2 %collective-permute-start.19 = (bf16[1024,256]{1,0:T(8,128)(2,1)S(1)}, bf16[1024,256]{1,0:T(8,128)(2,1)S(1)}, u32[]{:S(2)}, u32[]{:S(2)}) collective-permute-start(bf16[1024,256]{1,0:T(8,128)(2,1)S(1)} %add_convert_fusion.6), channel_id=1, source_target_pairs={{0,16},{1,49},{16,32},{17,1},{32,48},{33,17},{48,0},{49,33},{2,18}... | collective-permute-start | bytes 1572872 | tf_op jit(solution)/shard_map/ppermute | solution.py:36
  234.6 18.6 %collective-permute-start.23 = (bf16[1024,256]{1,0:T(8,128)(2,1)S(1)}, bf16[1024,256]{1,0:T(8,128)(2,1)S(1)}, u32[]{:S(2)}, u32[]{:S(2)}) collective-permute-start(bf16[1024,256]{1,0:T(8,128)(2,1)S(1)} %add_convert_fusion.4), channel_id=1, source_target_pairs={{0,16},{1,49},{16,32},{17,1},{32,48},{33,17},{48,0},{49,33},{2,18}... | collective-permute-start | bytes 1572872 | tf_op jit(solution)/shard_map/ppermute | solution.py:36
  235.1 23.7 %collective-permute-start.26 = (bf16[1024,256]{1,0:T(8,128)(2,1)S(1)}, bf16[1024,256]{1,0:T(8,128)(2,1)S(1)}, u32[]{:S(2)}, u32[]{:S(2)}) collective-permute-start(bf16[1024,256]{1,0:T(8,128)(2,1)S(1)} %add_convert_fusion.1), channel_id=1, source_target_pairs={{0,16},{1,49},{16,32},{17,1},{32,48},{33,17},{48,0},{49,33},{2,18}... | collective-permute-start | bytes 1572872 | tf_op jit(solution)/shard_map/ppermute | solution.py:36
  242.1 22.0 %collective-permute-start.17 = (bf16[1024,256]{1,0:T(8,128)(2,1)S(1)}, bf16[1024,256]{1,0:T(8,128)(2,1)S(1)}, u32[]{:S(2)}, u32[]{:S(2)}) collective-permute-start(bf16[1024,256]{1,0:T(8,128)(2,1)S(1)} %add_convert_fusion.8), channel_id=1, source_target_pairs={{0,16},{1,49},{16,32},{17,1},{32,48},{33,17},{48,0},{49,33},{2,18}... | collective-permute-start | bytes 1572872 | tf_op jit(solution)/shard_map/ppermute | solution.py:36
  247.7 16.4 %collective-permute-start.20 = (bf16[1024,256]{1,0:T(8,128)(2,1)S(1)}, bf16[1024,256]{1,0:T(8,128)(2,1)S(1)}, u32[]{:S(2)}, u32[]{:S(2)}) collective-permute-start(bf16[1024,256]{1,0:T(8,128)(2,1)S(1)} %add_convert_fusion.5), channel_id=1, source_target_pairs={{0,64},{64,0},{1,65},{65,1},{2,66},{66,2},{3,67},{67,3},{4,68},{68... | collective-permute-start | bytes 1572872 | tf_op jit(solution)/shard_map/ppermute | solution.py:26
  253.4 16.4 %collective-permute-start.24 = (bf16[1024,256]{1,0:T(8,128)(2,1)S(1)}, bf16[1024,256]{1,0:T(8,128)(2,1)S(1)}, u32[]{:S(2)}, u32[]{:S(2)}) collective-permute-start(bf16[1024,256]{1,0:T(8,128)(2,1)S(1)} %add_convert_fusion.3), channel_id=1, source_target_pairs={{0,16},{1,49},{16,32},{17,1},{32,48},{33,17},{48,0},{49,33},{2,18}... | collective-permute-start | bytes 1572872 | tf_op jit(solution)/shard_map/ppermute | solution.py:36
  (25 other events, 515.4 us)
Sparse Core Ops, SparseCore 0:
  173.9 35.4 all-gather.1

commit v3 on v2

--- a/solution.py
+++ b/solution.py
@@ -13,7 +13,7 @@
 PIV = 2048
 KH = PIV // 2
 OWN = 384
-STEP = 6
+STEP = 12
 BF = jnp.bfloat16
 F32 = jnp.float32
 VMEM_LIMIT = 60 * 2**20
@@ -80,16 +80,17 @@
     w = mirrored(own, "x", 1)
     e = mirrored(own, "x", -1)
     z = shift(own, "z", 1)
-    w, e, z, ready = lax.optimization_barrier((w, e, z, ready))
-    core = shift(after(own, w), "c", 1)
+    core = shift(own, "c", 1)
+    w, e, z, core, ready = lax.optimization_barrier((w, e, z, core, ready))
     b = shift(w, "z", 1)
     q = mirrored(w, "x", 1)
     a = mirrored(z, "x", -1)
-    core1 = shift(jnp.concatenate([after(w, core), e, z]), "c", 1)
+    cross = [shift(v, "c", 1) for v in (w, e)]
+    q, a, b, cross = lax.optimization_barrier((q, a, b, cross))
     r = mirrored(b, "x", 1)
-    last = [shift(v, "c", 1) for v in (q, a, b, r)]
+    last = cross + [shift(v, "c", 1) for v in (z, q, a, b, r)]
     pieces, first = [], 0
-    for array in (own, w, e, z, q, a, b, r, core, core1, *last):
+    for array in (own, w, e, z, q, a, b, r, core, *last):
         pieces.append((array, first, array.shape[0] // BLK))
         first += array.shape[0] // BLK
     return pieces, ready
@@ -120,7 +121,7 @@
 def main_kernel(pieces, dest, chosen, *refs):
     n = len(pieces)
     ins, outs = refs[:n], refs[n : n + 16]
-    rows, cols, placed, sem_in, sem_sel, sem_out = refs[n + 16 :]
+    rows, cols, turned, placed, sem_in, sem_sel, sem_out = refs[n + 16 :]
 
     for m in range(4):
         fetch(ins, pieces, chosen[m], cols.at[pl.ds(m * BLK, BLK), :], sem_sel.at[m])
@@ -142,12 +143,11 @@
     for m in range(4):
         fetched(ins, chosen[m], cols.at[pl.ds(m * BLK, BLK), :], sem_sel.at[m])
 
+    turned[...] = cols[...].T
+
     def multiply(block, count):
-        product = lax.dot_general(
-            rows[pl.ds(block * BLK, count * BLK), :],
-            cols[...],
-            (((1,), (1,)), ((), ())),
-            preferred_element_type=F32,
+        product = jnp.dot(
+            rows[pl.ds(block * BLK, count * BLK), :], turned[...], preferred_element_type=F32
         )
         for b in range(count):
             at = pl.multiple_of(dest[block + b] * BLK, BLK)
@@ -189,6 +189,7 @@
         scratch_shapes=[
             pltpu.VMEM((6144, PIV), BF),
             pltpu.VMEM((512, PIV), BF),
+            pltpu.VMEM((PIV, 512), BF),
             pltpu.VMEM((2, PORD, 256), BF),
             pltpu.SemaphoreType.DMA((n,)),
             pltpu.SemaphoreType.DMA((4,)),
@@ -247,17 +248,17 @@
     )(pan_rows, pan_cols, offset, *arrays)
 
 
-def ring_sum(first, second):
-    rings = (first, second)
-    carried = [parts[3] for parts in rings]
-    marks = []
-    for k in (2, 1, 0):
-        moved = [mirrored(v, "y", 1) for v in carried]
-        marks.append(moved)
-        carried = [parts[k].astype(F32) + v.astype(F32) for parts, v in zip(rings, moved)]
-        if k > 0:
-            carried = [v.astype(BF) for v in carried]
-    return carried, marks
+class Ring:
+    def __init__(self, term, gate=None):
+        carried = term(3).astype(BF)
+        if gate is not None:
+            carried = after(carried, gate)
+        self.marks = []
+        for k in (2, 1, 0):
+            moved = mirrored(carried, "y", 1)
+            self.marks.append(moved)
+            self.total = term(k).astype(F32) + moved.astype(F32)
+            carried = self.total.astype(BF)
 
 
 def pick(bit, when_zero, when_one):
@@ -365,23 +366,34 @@
     pan_rows_f = arrived.astype(F32).sum(axis=0) + front_rows.astype(F32)
     share = jnp.dot(pan_rows_f.astype(BF), parent_inverse, preferred_element_type=F32).astype(BF)
 
-    far_in, near_in = ([[part[k] for part in main[d]] for k in range(2)] for d in (1, 0))
-    far, marks = ring_sum(*far_in)
-    near_in = [parts[:3] + [after(parts[3], mark)] for parts, mark in zip(near_in, marks[0])]
-    far = [shift(v.astype(BF), "h", 1).astype(F32) for v in far]
-    near, _ = ring_sum(*near_in)
-    near = jnp.concatenate([n + f for n, f in zip(near, far)], axis=1)
+    rings = []
+    for d in (1, 0):
+        for half in range(2):
+            rings.append(
+                Ring(
+                    lambda k: main[d][k][half],
+                    None if d == 1 else rings[half].marks[0],
+                )
+            )
+    far = [shift(ring.total.astype(BF), "h", 1).astype(F32) for ring in rings[:2]]
+    near = jnp.concatenate([rings[2].total + far[0], rings[3].total + far[1]], axis=1)
     assembled = parent_front.astype(F32) + near
 
     row_block = sec * 8 + dev // 2
     masked = jnp.where(jnp.any(parent_pivots == row_block), jnp.zeros_like(share), share)
-    masked = after(masked, marks[0][0])
+    masked = after(masked, rings[0].marks[0])
     pairs = [(s * 16 + d, (d % 8) * 16 + 2 * s + d // 8) for s in range(8) for d in range(16)]
     moved = lax.ppermute(masked, AXES, pairs)
-    ring = ordered_ring(y, [moved, shift(moved, "y", -1), shift(moved, "y", 2), shift(moved, "y", 1)])
-    column_factor = ordered_pair(h, ring, shift(ring, "h", 1)).reshape(512, 1024)
-
-    parent_factor = lax.all_gather(share, ("x", "z", "c"), axis=0, tiled=True)
+    both = ordered_pair(h, moved, shift(moved, "h", 1))
+    share = after(share, both)
+    both = after(both, rings[1].marks[1])
+    ring = ordered_ring(y, [both, shift(both, "y", -1), shift(both, "y", 2), shift(both, "y", 1)])
+    column_factor = ring.transpose(1, 0, 2, 3).reshape(512, 1024)
+
+    copies = jnp.broadcast_to(share, (16, 64, 1024))
+    parent_factor = lax.all_to_all(
+        copies, ("x", "z", "c"), split_axis=0, concat_axis=0, tiled=True
+    ).reshape(1024, 1024)
 
     my_blocks = sec * 8 + jnp.arange(8, dtype=jnp.int32)
     is_pivot = jnp.any(parent_pivots[None, :] == my_blocks[:, None], axis=1)
@@ -390,6 +402,8 @@
     update = lax.dot_general(
         trailing, column_factor, (((1,), (1,)), ((), ())), preferred_element_type=F32
     )
+    update = lax.optimization_barrier(update)
+    parent_factor = jnp.where(parent_pivots[0] < 0, jnp.zeros_like(parent_factor), parent_factor)
     return assembled - update, parent_factor
 
 

time: 285 us -> 262 us (0.919)
  the two profiles are of different devices: /device:TPU:37 before, /device:TPU:18 now
where the time goes in v3:
time: 262 us; the launch traced here: 260 us
  waiting for transfers between devices  116 us (44%)
  starting transfers between devices  74 us (28%)
  Pallas kernels  41.6 us (16%)
  other arithmetic  19.9 us (8%)
  local copies, waits for them, and re-layouts  5.38 us (2%)
    ppermute x17, waiting for transfers between devices, mirrored(): return lax.ppermute(array, (axis, 'c'), pairs)  80 us
    ppermute x21, waiting for transfers between devices, shift(): lax.ppermute(array, axis, [(i, (i + step) % size) for i in range(size)])  32.8 us
    ppermute x17, starting transfers between devices, mirrored(): return lax.ppermute(array, (axis, 'c'), pairs)  30.7 us
    pallas_call x1, Pallas kernels, main_parts(): pl.pallas_call(functools.partial(main_kernel, [p[1:] for p in pieces]), o...  26.3 us
    ppermute x21, starting transfers between devices, shift(): lax.ppermute(array, axis, [(i, (i + step) % size) for i in range(size)])  22.8 us
    all_to_all x1, starting transfers between devices, local(): lax.all_to_all(pan.reshape(8, 64, 1024), ('h', 'y'), split_axis=0, concat...  7.98 us
    pallas_call x1, Pallas kernels, panel_parts(): pl.pallas_call(functools.partial(panel_kernel, [p[1:] for p in pieces]),...  6.58 us
    pallas_call x1, Pallas kernels, factor(): pl.pallas_call(factor_kernel, out_shape=jax.ShapeDtypeStruct((OWN, PIV),...  6.48 us
  transfers between devices with their start and end apart: 41, of which 18 were waited for; matrix products, arithmetic and copies ran while one was open for 8% of the time, Pallas kernels for 11%

profile of v3, /device:TPU:18, one launch (start us, length us, event | category | flops | bytes accessed | tf_op | source)
XLA Modules:
  0.0 260.4 jit_solution(7947450365581749147)
XLA Ops:
  0.7 6.5 %shard_map.86.refs_0_ = bf16[384,2048]{1,0:T(8,128)(2,1)} custom-call(bf16[1,384,2048]{2,1,0:T(8,128)(2,1)} %panel.1, bf16[1,2048,2048]{2,1,0:T(8,128)(2,1)} %inverse.1), custom_call_target="tpu_custom_call" | custom-call | flops 2000000000 | bytes 8000000 | tf_op jit(solution)/shard_map/pallas_call | solution.py:66
  14.0 7.4 %collective-permute-start.4 = (bf16[8,64,1024]{2,1,0:T(8,128)(2,1)}, bf16[8,64,1024]{2,1,0:T(8,128)(2,1)S(1)}, u32[]{:S(2)}, u32[]{:S(2)}) collective-permute-start(bf16[8,64,1024]{2,1,0:T(8,128)(2,1)} %get-tuple-element.65), channel_id=1, source_target_pairs={{0,1},{1,0},{2,3},{3,2},{4,5},{5,4},{6,7},{7,6},{8,9},{9,8},{10,11... | collective-permute-start | bytes 3145736 | tf_op jit(solution)/shard_map/ppermute | solution.py:26
  28.2 16.3 %collective-permute-done.2.refs_3_ = bf16[384,2048]{1,0:T(8,128)(2,1)} collective-permute-done((bf16[384,2048]{1,0:T(8,128)(2,1)}, bf16[384,2048]{1,0:T(8,128)(2,1)}, u32[]{:S(2)}, u32[]{:S(2)}) %collective-permute-start.2) | collective-permute-done | bytes 1572896 | tf_op jit(solution)/shard_map/ppermute | solution.py:26
  50.6 32.6 %collective-permute-done.6.refs_5_ = bf16[384,2048]{1,0:T(8,128)(2,1)} collective-permute-done((bf16[384,2048]{1,0:T(8,128)(2,1)}, bf16[384,2048]{1,0:T(8,128)(2,1)}, u32[]{:S(2)}, u32[]{:S(2)}) %collective-permute-start.6) | collective-permute-done | bytes 1572896 | tf_op jit(solution)/shard_map/ppermute | solution.py:36
  88.0 18.6 %collective-permute-done.10.refs_7_ = bf16[384,2048]{1,0:T(8,128)(2,1)} collective-permute-done((bf16[384,2048]{1,0:T(8,128)(2,1)}, bf16[384,2048]{1,0:T(8,128)(2,1)}, u32[]{:S(2)}, u32[]{:S(2)}) %collective-permute-start.10) | collective-permute-done | bytes 1572896 | tf_op jit(solution)/shard_map/ppermute | solution.py:36
  107.7 2.6 %collective-permute-done.15.refs_15_ = bf16[384,2048]{1,0:T(8,128)(2,1)} collective-permute-done((bf16[384,2048]{1,0:T(8,128)(2,1)}, bf16[384,2048]{1,0:T(8,128)(2,1)}, u32[]{:S(2)}, u32[]{:S(2)}) %collective-permute-start.15) | collective-permute-done | bytes 1572896 | tf_op jit(solution)/shard_map/ppermute | solution.py:26
  110.3 6.6 %shard_map.88 = bf16[512,1024]{1,0:T(8,128)(2,1)} custom-call(s32[8]{0:T(128)} %get-tuple-element.66.pan_rows, s32[8]{0:T(128)} %get-tuple-element.67.pan_cols, s32[1]{0:T(128)} %bitcast.3.offset, bf16[384,2048]{1,0:T(8,128)(2,1)} %shard_map.86.refs_0_, bf16[384,2048]{1,0:T(8,128)(2,1)} %collective-permute-done.refs_1_, ...), custom_call_target="tpu_custom_call" | custom-call | flops 2200000000 | bytes 8000000 | tf_op jit(solution)/shard_map/pallas_call | solution.py:233
  116.9 8.0 %all-to-all-start = ((bf16[8,64,1024]{2,1,0:T(8,128)(2,1)}), bf16[8,64,1024]{2,1,0:T(8,128)(2,1)S(1)}, u32[]{:S(2)}, u32[]{:S(2)}) async-start(bf16[8,64,1024]{2,1,0:T(8,128)(2,1)} %bitcast.57), calls=%async_computation | async-start | bytes 2097152 | tf_op jit(solution)/shard_map/all_to_all | solution.py:351
  126.1 2.3 collective-permute-start.31
  130.3 26.3 %shard_map.89 = (bf16[1024,256]{1,0:T(8,128)(2,1)}, bf16[1024,256]{1,0:T(8,128)(2,1)}, bf16[1024,256]{1,0:T(8,128)(2,1)}, bf16[1024,256]{1,0:T(8,128)(2,1)}, bf1...) custom-call(s32[48]{0:T(128)} %select_reduce_fusion.dest, ...), custom_call_target="tpu_custom_call" | custom-call | flops 20000000000 | bytes 36000000 | tf_op jit(solution)/shard_map/pallas_call | solution.py:184
  158.5 4.8 %collective-permute-done.33 = bf16[64,1024]{1,0:T(8,128)(2,1)S(1)} collective-permute-done((bf16[64,1024]{1,0:T(8,128)(2,1)S(1)}, bf16[64,1024]{1,0:T(8,128)(2,1)S(1)}, u32[]{:S(2)}, u32[]{:S(2)}) %collective-permute-start.33) | collective-permute-done | bytes 131104 | tf_op jit(solution)/shard_map/ppermute | solution.py:26
  164.3 3.1 %collective-permute-done.16 = bf16[1024,256]{1,0:T(8,128)(2,1)S(1)} collective-permute-done((bf16[1024,256]{1,0:T(8,128)(2,1)}, bf16[1024,256]{1,0:T(8,128)(2,1)S(1)}, u32[]{:S(2)}, u32[]{:S(2)}) %collective-permute-start.16) | collective-permute-done | bytes 524320 | tf_op jit(solution)/shard_map/ppermute | solution.py:36
  167.4 6.3 %collective-permute-start.34 = (bf16[64,1024]{1,0:T(8,128)(2,1)S(1)}, bf16[64,1024]{1,0:T(8,128)(2,1)S(1)}, u32[]{:S(2)}, u32[]{:S(2)}) collective-permute-start(bf16[64,1024]{1,0:T(8,128)(2,1)S(1)} %get-tuple-element.123), channel_id=1, source_target_pairs={{0,0},{1,16},{2,32},{3,48},{4,64},{5,80},{6,96},{7,112},{8,1},{9,1... | collective-permute-start | bytes 393224 | tf_op jit(solution)/shard_map/ppermute | solution.py:386
  174.8 2.3 collective-permute-start.27
  177.0 3.1 %collective-permute-done.34 = bf16[64,1024]{1,0:T(8,128)(2,1)S(1)} collective-permute-done((bf16[64,1024]{1,0:T(8,128)(2,1)S(1)}, bf16[64,1024]{1,0:T(8,128)(2,1)S(1)}, u32[]{:S(2)}, u32[]{:S(2)}) %collective-permute-start.34) | collective-permute-done | bytes 131104 | tf_op jit(solution)/shard_map/ppermute | solution.py:386
  181.1 2.8 %collective-permute-start.20 = (bf16[1024,256]{1,0:T(8,128)(2,1)}, bf16[1024,256]{1,0:T(8,128)(2,1)}, u32[]{:S(2)}, u32[]{:S(2)}) collective-permute-start(bf16[1024,256]{1,0:T(8,128)(2,1)} %add_convert_fusion.7), channel_id=1, source_target_pairs={{0,16},{1,49},{16,32},{17,1},{32,48},{33,17},{48,0},{49,33},{2,18}... | collective-permute-start | bytes 1572872 | tf_op jit(solution)/shard_map/ppermute | solution.py:36
  183.9 5.4 %collective-permute-start.24 = (bf16[1024,256]{1,0:T(8,128)(2,1)}, bf16[1024,256]{1,0:T(8,128)(2,1)}, u32[]{:S(2)}, u32[]{:S(2)}) collective-permute-start(bf16[1024,256]{1,0:T(8,128)(2,1)} %get-tuple-element.110), channel_id=1, source_target_pairs={{0,16},{1,49},{16,32},{17,1},{32,48},{33,17},{48,0},{49,33},{2,18}... | collective-permute-start | bytes 1572872 | tf_op jit(solution)/shard_map/ppermute | solution.py:36
  190.9 6.3 %all-to-all-start.1 = ((bf16[16,64,1024]{2,1,0:T(8,128)(2,1)}), bf16[16,64,1024]{2,1,0:T(8,128)(2,1)}, u32[]{:S(2)}, u32[]{:S(2)}) async-start(bf16[16,64,1024]{2,1,0:T(8,128)(2,1)} %broadcast_in_dim.88), calls=%async_computation.1 | async-start | bytes 4194304 | tf_op jit(solution)/shard_map/all_to_all | solution.py:394
  200.4 2.5 collective-permute-start.36
  204.3 2.5 collective-permute-done.24
  206.8 4.0 %collective-permute-start.21 = (bf16[1024,256]{1,0:T(8,128)(2,1)S(1)}, bf16[1024,256]{1,0:T(8,128)(2,1)S(1)}, u32[]{:S(2)}, u32[]{:S(2)}) collective-permute-start(bf16[1024,256]{1,0:T(8,128)(2,1)S(1)} %add_convert_fusion.6), channel_id=1, source_target_pairs={{0,16},{1,49},{16,32},{17,1},{32,48},{33,17},{48,0},{49,33},{2,18}... | collective-permute-start | bytes 1572872 | tf_op jit(solution)/shard_map/ppermute | solution.py:36
  212.1 2.2 collective-permute-done.36
  217.3 2.3 collective-permute-done.18
  219.7 2.8 %collective-permute-start.19 = (bf16[1024,256]{1,0:T(8,128)(2,1)S(1)}, bf16[1024,256]{1,0:T(8,128)(2,1)S(1)}, u32[]{:S(2)}, u32[]{:S(2)}) collective-permute-start(bf16[1024,256]{1,0:T(8,128)(2,1)S(1)} %add_convert_fusion.8), channel_id=1, source_target_pairs={{0,16},{1,49},{16,32},{17,1},{32,48},{33,17},{48,0},{49,33},{2,18}... | collective-permute-start | bytes 1572872 | tf_op jit(solution)/shard_map/ppermute | solution.py:36
  222.5 2.6 %collective-permute-done.21 = bf16[1024,256]{1,0:T(8,128)(2,1)S(1)} collective-permute-done((bf16[1024,256]{1,0:T(8,128)(2,1)S(1)}, bf16[1024,256]{1,0:T(8,128)(2,1)S(1)}, u32[]{:S(2)}, u32[]{:S(2)}) %collective-permute-start.21) | collective-permute-done | bytes 524320 | tf_op jit(solution)/shard_map/ppermute | solution.py:36
  226.1 4.7 %collective-permute-done.25 = bf16[1024,256]{1,0:T(8,128)(2,1)S(1)} collective-permute-done((bf16[1024,256]{1,0:T(8,128)(2,1)S(1)}, bf16[1024,256]{1,0:T(8,128)(2,1)S(1)}, u32[]{:S(2)}, u32[]{:S(2)}) %collective-permute-start.25) | collective-permute-done | bytes 524320 | tf_op jit(solution)/shard_map/ppermute | solution.py:36
  230.9 2.8 %collective-permute-start.26 = (bf16[1024,256]{1,0:T(8,128)(2,1)S(1)}, bf16[1024,256]{1,0:T(8,128)(2,1)S(1)}, u32[]{:S(2)}, u32[]{:S(2)}) collective-permute-start(bf16[1024,256]{1,0:T(8,128)(2,1)S(1)} %add_convert_fusion.3), channel_id=1, source_target_pairs={{0,16},{1,49},{16,32},{17,1},{32,48},{33,17},{48,0},{49,33},{2,18}... | collective-permute-start | bytes 1572872 | tf_op jit(solution)/shard_map/ppermute | solution.py:36
  233.8 2.6 %collective-permute-done.28 = bf16[1024,256]{1,0:T(8,128)(2,1)S(1)} collective-permute-done((bf16[1024,256]{1,0:T(8,128)(2,1)S(1)}, bf16[1024,256]{1,0:T(8,128)(2,1)S(1)}, u32[]{:S(2)}, u32[]{:S(2)}) %collective-permute-start.28) | collective-permute-done | bytes 524320 | tf_op jit(solution)/shard_map/ppermute | solution.py:36
  238.5 3.5 %collective-permute-done.19 = bf16[1024,256]{1,0:T(8,128)(2,1)S(1)} collective-permute-done((bf16[1024,256]{1,0:T(8,128)(2,1)S(1)}, bf16[1024,256]{1,0:T(8,128)(2,1)S(1)}, u32[]{:S(2)}, u32[]{:S(2)}) %collective-permute-start.19) | collective-permute-done | bytes 524320 | tf_op jit(solution)/shard_map/ppermute | solution.py:36
  242.2 5.4 %collective-permute-done.26 = bf16[1024,256]{1,0:T(8,128)(2,1)S(1)} collective-permute-done((bf16[1024,256]{1,0:T(8,128)(2,1)S(1)}, bf16[1024,256]{1,0:T(8,128)(2,1)S(1)}, u32[]{:S(2)}, u32[]{:S(2)}) %collective-permute-start.26) | collective-permute-done | bytes 524320 | tf_op jit(solution)/shard_map/ppermute | solution.py:36
  247.6 4.9 %collective-permute-done.29 = bf16[1024,256]{1,0:T(8,128)(2,1)S(1)} collective-permute-done((bf16[1024,256]{1,0:T(8,128)(2,1)S(1)}, bf16[1024,256]{1,0:T(8,128)(2,1)S(1)}, u32[]{:S(2)}, u32[]{:S(2)}) %collective-permute-start.29) | collective-permute-done | bytes 524320 | tf_op jit(solution)/shard_map/ppermute | solution.py:26
  253.7 3.3 %broadcast_select_fusion.1 = (bf16[16,64,1024]{2,1,0:T(8,128)(2,1)}, bf16[16,64,1024]{2,1,0:T(8,128)(2,1)S(1)}) fusion(bf16[16,64,1024]{2,1,0:T(8,128)(2,1)} %all-to-all-done.1, pred[]{:T(512)} %bitcast.24, pred[16]{0:T(512)(128)(4,1)S(1)} %broadcast_in_dim.85), kind=kLoop, calls=%fused_computation.5 | loop fusion | flops 2097152 | bytes 6291473 | tf_op jit(solution)/shard_map/jit(_where)/select_n | solution.py:406
  (143 shorter events, 51.4 us)
Async XLA Ops:
  7.2 21.1 %collective-permute-start.3 = (bf16[384,2048]{1,0:T(8,128)(2,1)}, bf16[384,2048]{1,0:T(8,128)(2,1)}, u32[]{:S(2)}, u32[]{:S(2)}) collective-permute-start(bf16[384,2048]{1,0:T(8,128)(2,1)} %shard_map.86.refs_0_), channel_id=1, source_target_pairs={{0,1},{1,0},{2,3},{3,2},{4,5},{5,4},{6,7},{7,6},{8,9},{9,8},{10,11... | collective-permute-start | bytes 4718600 | tf_op jit(solution)/shard_map/ppermute | solution.py:26
  7.3 37.3 %collective-permute-start.2 = (bf16[384,2048]{1,0:T(8,128)(2,1)}, bf16[384,2048]{1,0:T(8,128)(2,1)}, u32[]{:S(2)}, u32[]{:S(2)}) collective-permute-start(bf16[384,2048]{1,0:T(8,128)(2,1)} %shard_map.86.refs_0_), channel_id=1, source_target_pairs={{0,2},{2,0},{1,3},{3,1},{4,6},{6,4},{5,7},{7,5},{8,10},{10,8},{9,1... | collective-permute-start | bytes 4718600 | tf_op jit(solution)/shard_map/ppermute | solution.py:26
  9.2 37.3 %collective-permute-start.1 = (bf16[384,2048]{1,0:T(8,128)(2,1)}, bf16[384,2048]{1,0:T(8,128)(2,1)}, u32[]{:S(2)}, u32[]{:S(2)}) collective-permute-start(bf16[384,2048]{1,0:T(8,128)(2,1)} %shard_map.86.refs_0_), channel_id=1, source_target_pairs={{0,12},{1,5},{4,0},{5,9},{8,4},{9,13},{12,8},{13,1},{2,14},{3,7},{... | collective-permute-start | bytes 4718600 | tf_op jit(solution)/shard_map/ppermute | solution.py:36
  9.8 36.7 %collective-permute-start = (bf16[384,2048]{1,0:T(8,128)(2,1)}, bf16[384,2048]{1,0:T(8,128)(2,1)}, u32[]{:S(2)}, u32[]{:S(2)}) collective-permute-start(bf16[384,2048]{1,0:T(8,128)(2,1)} %shard_map.86.refs_0_), channel_id=1, source_target_pairs={{0,4},{1,13},{4,8},{5,1},{8,12},{9,5},{12,0},{13,9},{2,6},{3,15},{... | collective-permute-start | bytes 4718600 | tf_op jit(solution)/shard_map/ppermute | solution.py:36
  46.7 36.6 %collective-permute-start.6 = (bf16[384,2048]{1,0:T(8,128)(2,1)}, bf16[384,2048]{1,0:T(8,128)(2,1)}, u32[]{:S(2)}, u32[]{:S(2)}) collective-permute-start(bf16[384,2048]{1,0:T(8,128)(2,1)} %collective-permute-done.2.refs_3_), channel_id=1, source_target_pairs={{0,12},{1,5},{4,0},{5,9},{8,4},{9,13},{12,8},{13,1},{2,14},{3,7},{... | collective-permute-start | bytes 4718600 | tf_op jit(solution)/shard_map/ppermute | solution.py:36
  47.8 35.4 %collective-permute-start.8 = (bf16[384,2048]{1,0:T(8,128)(2,1)}, bf16[384,2048]{1,0:T(8,128)(2,1)}, u32[]{:S(2)}, u32[]{:S(2)}) collective-permute-start(bf16[384,2048]{1,0:T(8,128)(2,1)} %collective-permute-done.refs_1_), channel_id=1, source_target_pairs={{0,1},{1,0},{2,3},{3,2},{4,5},{5,4},{6,7},{7,6},{8,9},{9,8},{10,11... | collective-permute-start | bytes 4718600 | tf_op jit(solution)/shard_map/ppermute | solution.py:26
  48.5 36.6 %collective-permute-start.7 = (bf16[384,2048]{1,0:T(8,128)(2,1)}, bf16[384,2048]{1,0:T(8,128)(2,1)}, u32[]{:S(2)}, u32[]{:S(2)}) collective-permute-start(bf16[384,2048]{1,0:T(8,128)(2,1)} %collective-permute-done.refs_1_), channel_id=1, source_target_pairs={{0,2},{2,0},{1,3},{3,1},{4,6},{6,4},{5,7},{7,5},{8,10},{10,8},{9,1... | collective-permute-start | bytes 4718600 | tf_op jit(solution)/shard_map/ppermute | solution.py:26
  48.5 36.6 %collective-permute-start.5 = (bf16[384,2048]{1,0:T(8,128)(2,1)}, bf16[384,2048]{1,0:T(8,128)(2,1)}, u32[]{:S(2)}, u32[]{:S(2)}) collective-permute-start(bf16[384,2048]{1,0:T(8,128)(2,1)} %collective-permute-done.refs_1_), channel_id=1, source_target_pairs={{0,4},{1,13},{4,8},{5,1},{8,12},{9,5},{12,0},{13,9},{2,6},{3,15},{... | collective-permute-start | bytes 4718600 | tf_op jit(solution)/shard_map/ppermute | solution.py:36
  85.1 21.5 %collective-permute-start.10 = (bf16[384,2048]{1,0:T(8,128)(2,1)}, bf16[384,2048]{1,0:T(8,128)(2,1)}, u32[]{:S(2)}, u32[]{:S(2)}) collective-permute-start(bf16[384,2048]{1,0:T(8,128)(2,1)} %collective-permute-done.7.refs_6_), channel_id=1, source_target_pairs={{0,4},{1,13},{4,8},{5,1},{8,12},{9,5},{12,0},{13,9},{2,6},{3,15},{... | collective-permute-start | bytes 4718600 | tf_op jit(solution)/shard_map/ppermute | solution.py:36
  87.0 20.7 %collective-permute-start.11 = (bf16[384,2048]{1,0:T(8,128)(2,1)}, bf16[384,2048]{1,0:T(8,128)(2,1)}, u32[]{:S(2)}, u32[]{:S(2)}) collective-permute-start(bf16[384,2048]{1,0:T(8,128)(2,1)} %collective-permute-done.2.refs_3_), channel_id=1, source_target_pairs={{0,1},{1,0},{2,3},{3,2},{4,5},{5,4},{6,7},{7,6},{8,9},{9,8},{10,11... | collective-permute-start | bytes 4718600 | tf_op jit(solution)/shard_map/ppermute | solution.py:26
  87.3 20.4 %collective-permute-start.14 = (bf16[384,2048]{1,0:T(8,128)(2,1)}, bf16[384,2048]{1,0:T(8,128)(2,1)}, u32[]{:S(2)}, u32[]{:S(2)}) collective-permute-start(bf16[384,2048]{1,0:T(8,128)(2,1)} %collective-permute-done.7.refs_6_), channel_id=1, source_target_pairs={{0,1},{1,0},{2,3},{3,2},{4,5},{5,4},{6,7},{7,6},{8,9},{9,8},{10,11... | collective-permute-start | bytes 4718600 | tf_op jit(solution)/shard_map/ppermute | solution.py:26
  87.5 20.2 %collective-permute-start.12 = (bf16[384,2048]{1,0:T(8,128)(2,1)}, bf16[384,2048]{1,0:T(8,128)(2,1)}, u32[]{:S(2)}, u32[]{:S(2)}) collective-permute-start(bf16[384,2048]{1,0:T(8,128)(2,1)} %collective-permute-done.5.refs_4_), channel_id=1, source_target_pairs={{0,1},{1,0},{2,3},{3,2},{4,5},{5,4},{6,7},{7,6},{8,9},{9,8},{10,11... | collective-permute-start | bytes 4718600 | tf_op jit(solution)/shard_map/ppermute | solution.py:26
  87.8 19.9 %collective-permute-start.13 = (bf16[384,2048]{1,0:T(8,128)(2,1)}, bf16[384,2048]{1,0:T(8,128)(2,1)}, u32[]{:S(2)}, u32[]{:S(2)}) collective-permute-start(bf16[384,2048]{1,0:T(8,128)(2,1)} %collective-permute-done.6.refs_5_), channel_id=1, source_target_pairs={{0,1},{1,0},{2,3},{3,2},{4,5},{5,4},{6,7},{7,6},{8,9},{9,8},{10,11... | collective-permute-start | bytes 4718600 | tf_op jit(solution)/shard_map/ppermute | solution.py:26
  116.9 40.8 %all-to-all-start = ((bf16[8,64,1024]{2,1,0:T(8,128)(2,1)}), bf16[8,64,1024]{2,1,0:T(8,128)(2,1)S(1)}, u32[]{:S(2)}, u32[]{:S(2)}) async-start(bf16[8,64,1024]{2,1,0:T(8,128)(2,1)} %bitcast.57), calls=%async_computation | async-start | bytes 2097152 | tf_op jit(solution)/shard_map/all_to_all | solution.py:351
  124.9 31.7 %collective-permute-start.30 = (bf16[2,64,1024]{2,1,0:T(8,128)(2,1)}, bf16[2,64,1024]{2,1,0:T(8,128)(2,1)S(1)}, u32[]{:S(2)}, u32[]{:S(2)}) collective-permute-start(bf16[2,64,1024]{2,1,0:T(8,128)(2,1)} %get-tuple-element.118), channel_id=1, source_target_pairs={{0,4},{4,8},{8,12},{12,0},{1,5},{5,9},{9,13},{13,1},{2,6},{6,10},{... | collective-permute-start | bytes 786440 | tf_op jit(solution)/shard_map/ppermute | solution.py:26
  126.1 30.5 %collective-permute-start.31 = (bf16[2,64,1024]{2,1,0:T(8,128)(2,1)}, bf16[2,64,1024]{2,1,0:T(8,128)(2,1)}, u32[]{:S(2)}, u32[]{:S(2)}) collective-permute-start(bf16[2,64,1024]{2,1,0:T(8,128)(2,1)} %get-tuple-element.120), channel_id=1, source_target_pairs={{0,12},{4,0},{8,4},{12,8},{1,13},{5,1},{9,5},{13,9},{2,14},{6,2},{... | collective-permute-start | bytes 786440 | tf_op jit(solution)/shard_map/ppermute | solution.py:26
  128.4 28.2 %collective-permute-start.32 = (bf16[2,64,1024]{2,1,0:T(8,128)(2,1)S(1)}, bf16[2,64,1024]{2,1,0:T(8,128)(2,1)}, u32[]{:S(2)}, u32[]{:S(2)}) collective-permute-start(bf16[2,64,1024]{2,1,0:T(8,128)(2,1)S(1)} %get-tuple-element.122), channel_id=1, source_target_pairs={{0,8},{4,12},{8,0},{12,4},{1,9},{5,13},{9,1},{13,5},{2,10},{6,14},... | collective-permute-start | bytes 786440 | tf_op jit(solution)/shard_map/ppermute | solution.py:26
  173.7 26.6 %collective-permute-start.17 = (bf16[1024,256]{1,0:T(8,128)(2,1)}, bf16[1024,256]{1,0:T(8,128)(2,1)S(1)}, u32[]{:S(2)}, u32[]{:S(2)}) collective-permute-start(bf16[1024,256]{1,0:T(8,128)(2,1)} %get-tuple-element.101), channel_id=1, source_target_pairs={{0,16},{1,49},{16,32},{17,1},{32,48},{33,17},{48,0},{49,33},{2,18}... | collective-permute-start | bytes 1572872 | tf_op jit(solution)/shard_map/ppermute | solution.py:36
  174.8 22.5 %collective-permute-start.27 = (bf16[1024,256]{1,0:T(8,128)(2,1)}, bf16[1024,256]{1,0:T(8,128)(2,1)}, u32[]{:S(2)}, u32[]{:S(2)}) collective-permute-start(bf16[1024,256]{1,0:T(8,128)(2,1)} %add_convert_fusion.2), channel_id=1, source_target_pairs={{0,16},{1,49},{16,32},{17,1},{32,48},{33,17},{48,0},{49,33},{2,18}... | collective-permute-start | bytes 1572872 | tf_op jit(solution)/shard_map/ppermute | solution.py:36
  181.1 21.9 %collective-permute-start.20 = (bf16[1024,256]{1,0:T(8,128)(2,1)}, bf16[1024,256]{1,0:T(8,128)(2,1)}, u32[]{:S(2)}, u32[]{:S(2)}) collective-permute-start(bf16[1024,256]{1,0:T(8,128)(2,1)} %add_convert_fusion.7), channel_id=1, source_target_pairs={{0,16},{1,49},{16,32},{17,1},{32,48},{33,17},{48,0},{49,33},{2,18}... | collective-permute-start | bytes 1572872 | tf_op jit(solution)/shard_map/ppermute | solution.py:36
  183.9 22.9 %collective-permute-start.24 = (bf16[1024,256]{1,0:T(8,128)(2,1)}, bf16[1024,256]{1,0:T(8,128)(2,1)}, u32[]{:S(2)}, u32[]{:S(2)}) collective-permute-start(bf16[1024,256]{1,0:T(8,128)(2,1)} %get-tuple-element.110), channel_id=1, source_target_pairs={{0,16},{1,49},{16,32},{17,1},{32,48},{33,17},{48,0},{49,33},{2,18}... | collective-permute-start | bytes 1572872 | tf_op jit(solution)/shard_map/ppermute | solution.py:36
  190.9 62.8 %all-to-all-start.1 = ((bf16[16,64,1024]{2,1,0:T(8,128)(2,1)}), bf16[16,64,1024]{2,1,0:T(8,128)(2,1)}, u32[]{:S(2)}, u32[]{:S(2)}) async-start(bf16[16,64,1024]{2,1,0:T(8,128)(2,1)} %broadcast_in_dim.88), calls=%async_computation.1 | async-start | bytes 4194304 | tf_op jit(solution)/shard_map/all_to_all | solution.py:394
  197.2 19.9 %collective-permute-start.38 = (bf16[2,64,1024]{2,1,0:T(8,128)(2,1)S(1)}, bf16[2,64,1024]{2,1,0:T(8,128)(2,1)S(1)}, u32[]{:S(2)}, u32[]{:S(2)}) collective-permute-start(bf16[2,64,1024]{2,1,0:T(8,128)(2,1)S(1)} %pad_maximum_fusion), channel_id=1, source_target_pairs={{0,16},{16,32},{32,48},{48,0},{1,17},{17,33},{33,49},{49,1},{2,18}... | collective-permute-start | bytes 786440 | tf_op jit(solution)/shard_map/ppermute | solution.py:26
  198.2 17.8 %collective-permute-start.37 = (bf16[2,64,1024]{2,1,0:T(8,128)(2,1)S(1)}, bf16[2,64,1024]{2,1,0:T(8,128)(2,1)S(1)}, u32[]{:S(2)}, u32[]{:S(2)}) collective-permute-start(bf16[2,64,1024]{2,1,0:T(8,128)(2,1)S(1)} %pad_maximum_fusion), channel_id=1, source_target_pairs={{0,32},{16,48},{32,0},{48,16},{1,33},{17,49},{33,1},{49,17},{2,34}... | collective-permute-start | bytes 786440 | tf_op jit(solution)/shard_map/ppermute | solution.py:26
  203.0 16.5 %collective-permute-start.18 = (bf16[1024,256]{1,0:T(8,128)(2,1)S(1)}, bf16[1024,256]{1,0:T(8,128)(2,1)S(1)}, u32[]{:S(2)}, u32[]{:S(2)}) collective-permute-start(bf16[1024,256]{1,0:T(8,128)(2,1)S(1)} %add_convert_fusion.9), channel_id=1, source_target_pairs={{0,16},{1,49},{16,32},{17,1},{32,48},{33,17},{48,0},{49,33},{2,18}... | collective-permute-start | bytes 1572872 | tf_op jit(solution)/shard_map/ppermute | solution.py:36
  206.8 18.3 %collective-permute-start.21 = (bf16[1024,256]{1,0:T(8,128)(2,1)S(1)}, bf16[1024,256]{1,0:T(8,128)(2,1)S(1)}, u32[]{:S(2)}, u32[]{:S(2)}) collective-permute-start(bf16[1024,256]{1,0:T(8,128)(2,1)S(1)} %add_convert_fusion.6), channel_id=1, source_target_pairs={{0,16},{1,49},{16,32},{17,1},{32,48},{33,17},{48,0},{49,33},{2,18}... | collective-permute-start | bytes 1572872 | tf_op jit(solution)/shard_map/ppermute | solution.py:36
  214.3 16.5 %collective-permute-start.25 = (bf16[1024,256]{1,0:T(8,128)(2,1)S(1)}, bf16[1024,256]{1,0:T(8,128)(2,1)S(1)}, u32[]{:S(2)}, u32[]{:S(2)}) collective-permute-start(bf16[1024,256]{1,0:T(8,128)(2,1)S(1)} %add_convert_fusion.4), channel_id=1, source_target_pairs={{0,16},{1,49},{16,32},{17,1},{32,48},{33,17},{48,0},{49,33},{2,18}... | collective-permute-start | bytes 1572872 | tf_op jit(solution)/shard_map/ppermute | solution.py:36
  216.0 20.4 %collective-permute-start.28 = (bf16[1024,256]{1,0:T(8,128)(2,1)S(1)}, bf16[1024,256]{1,0:T(8,128)(2,1)S(1)}, u32[]{:S(2)}, u32[]{:S(2)}) collective-permute-start(bf16[1024,256]{1,0:T(8,128)(2,1)S(1)} %add_convert_fusion.1), channel_id=1, source_target_pairs={{0,16},{1,49},{16,32},{17,1},{32,48},{33,17},{48,0},{49,33},{2,18}... | collective-permute-start | bytes 1572872 | tf_op jit(solution)/shard_map/ppermute | solution.py:36
  219.7 22.3 %collective-permute-start.19 = (bf16[1024,256]{1,0:T(8,128)(2,1)S(1)}, bf16[1024,256]{1,0:T(8,128)(2,1)S(1)}, u32[]{:S(2)}, u32[]{:S(2)}) collective-permute-start(bf16[1024,256]{1,0:T(8,128)(2,1)S(1)} %add_convert_fusion.8), channel_id=1, source_target_pairs={{0,16},{1,49},{16,32},{17,1},{32,48},{33,17},{48,0},{49,33},{2,18}... | collective-permute-start | bytes 1572872 | tf_op jit(solution)/shard_map/ppermute | solution.py:36
  225.3 16.7 %collective-permute-start.22 = (bf16[1024,256]{1,0:T(8,128)(2,1)S(1)}, bf16[1024,256]{1,0:T(8,128)(2,1)S(1)}, u32[]{:S(2)}, u32[]{:S(2)}) collective-permute-start(bf16[1024,256]{1,0:T(8,128)(2,1)S(1)} %add_convert_fusion.5), channel_id=1, source_target_pairs={{0,64},{64,0},{1,65},{65,1},{2,66},{66,2},{3,67},{67,3},{4,68},{68... | collective-permute-start | bytes 1572872 | tf_op jit(solution)/shard_map/ppermute | solution.py:26
  230.9 16.7 %collective-permute-start.26 = (bf16[1024,256]{1,0:T(8,128)(2,1)S(1)}, bf16[1024,256]{1,0:T(8,128)(2,1)S(1)}, u32[]{:S(2)}, u32[]{:S(2)}) collective-permute-start(bf16[1024,256]{1,0:T(8,128)(2,1)S(1)} %add_convert_fusion.3), channel_id=1, source_target_pairs={{0,16},{1,49},{16,32},{17,1},{32,48},{33,17},{48,0},{49,33},{2,18}... | collective-permute-start | bytes 1572872 | tf_op jit(solution)/shard_map/ppermute | solution.py:36
  236.5 16.0 %collective-permute-start.29 = (bf16[1024,256]{1,0:T(8,128)(2,1)S(1)}, bf16[1024,256]{1,0:T(8,128)(2,1)S(1)}, u32[]{:S(2)}, u32[]{:S(2)}) collective-permute-start(bf16[1024,256]{1,0:T(8,128)(2,1)S(1)} %add_convert_fusion), channel_id=1, source_target_pairs={{0,64},{64,0},{1,65},{65,1},{2,66},{66,2},{3,67},{67,3},{4,68},{68... | collective-permute-start | bytes 1572872 | tf_op jit(solution)/shard_map/ppermute | solution.py:26
  (28 other events, 477.5 us)

commit v4 on v3

--- a/solution.py
+++ b/solution.py
@@ -132,7 +132,8 @@
             ins[i], rows.at[pl.ds(first * BLK, blocks * BLK), :], sem_in.at[i]
         )
 
-    for i in range(n):
+    early = 4
+    for i in range(early):
         arrival(i).start()
 
     @pl.loop(0, PORD // 256)
@@ -142,6 +143,8 @@
 
     for m in range(4):
         fetched(ins, chosen[m], cols.at[pl.ds(m * BLK, BLK), :], sem_sel.at[m])
+    for i in range(early, n):
+        arrival(i).start()
 
     turned[...] = cols[...].T
 
@@ -372,7 +375,7 @@
             rings.append(
                 Ring(
                     lambda k: main[d][k][half],
-                    None if d == 1 else rings[half].marks[0],
+                    None if d == 1 or half == 0 else rings[half].marks[0],
                 )
             )
     far = [shift(ring.total.astype(BF), "h", 1).astype(F32) for ring in rings[:2]]

time: 262 us -> 268 us (1.023)
  waiting for transfers between devices: 116 us -> 127 us
  Pallas kernels: 41.6 us -> 36.6 us
  starting transfers between devices: 74 us -> 70.8 us
    ppermute x21, waiting for transfers between devices: 32.8 us -> 47.6 us  [shift(): lax.ppermute(array, axis, [(i, (i + step) % size) for i in range(size)])]
    ppermute x17, waiting for transfers between devices: 80 us -> 72.5 us  [mirrored(): return lax.ppermute(array, (axis, 'c'), pairs)]
    ppermute x21, starting transfers between devices: 22.8 us -> 17.1 us  [shift(): lax.ppermute(array, axis, [(i, (i + step) % size) for i in range(size)])]
    pallas_call x1, Pallas kernels: 26.3 us -> 21.4 us  [main_parts(): pl.pallas_call(functools.partial(main_kernel, [p[1:] for p in pieces]), o...]
    ppermute x1, waiting for transfers between devices: 3.13 us -> 7.02 us  [local(): moved = lax.ppermute(masked, AXES, pairs)]
    all_to_all x1, starting transfers between devices: 6.27 us -> 10 us  [local(): lax.all_to_all(copies, ('x', 'z', 'c'), split_axis=0, concat_axis=0, tile...]
  transfers between devices with their start and end apart: 41 -> 41, of which waited for: 18 -> 17; matrix products, arithmetic and copies ran while one was open for 8% -> 8% of each run, Pallas kernels for 11% -> 9%
where the time goes in v4:
time: 268 us; the launch traced here: 264 us
  waiting for transfers between devices  127 us (47%)
  starting transfers between devices  70.8 us (26%)
  Pallas kernels  36.6 us (14%)
  other arithmetic  20.7 us (8%)
  local copies, waits for them, and re-layouts  5.38 us (2%)
    ppermute x17, waiting for transfers between devices, mirrored(): return lax.ppermute(array, (axis, 'c'), pairs)  72.5 us
    ppermute x21, waiting for transfers between devices, shift(): lax.ppermute(array, axis, [(i, (i + step) % size) for i in range(size)])  47.6 us
    ppermute x17, starting transfers between devices, mirrored(): return lax.ppermute(array, (axis, 'c'), pairs)  29.9 us
    pallas_call x1, Pallas kernels, main_parts(): pl.pallas_call(functools.partial(main_kernel, [p[1:] for p in pieces]), o...  21.4 us
    ppermute x21, starting transfers between devices, shift(): lax.ppermute(array, axis, [(i, (i + step) % size) for i in range(size)])  17.1 us
    all_to_all x1, starting transfers between devices, local(): lax.all_to_all(copies, ('x', 'z', 'c'), split_axis=0, concat_axis=0, tile...  10 us
    all_to_all x1, starting transfers between devices, local(): lax.all_to_all(pan.reshape(8, 64, 1024), ('h', 'y'), split_axis=0, concat...  7.85 us
    ppermute x1, waiting for transfers between devices, local(): moved = lax.ppermute(masked, AXES, pairs)  7.02 us
  transfers between devices with their start and end apart: 41, of which 17 were waited for; matrix products, arithmetic and copies ran while one was open for 8% of the time, Pallas kernels for 9%

profile of v4, /device:TPU:18, one launch (start us, length us, event | category | flops | bytes accessed | tf_op | source)
XLA Modules:
  0.0 264.3 jit_solution(215116693258928776)
XLA Ops:
  0.7 6.5 %shard_map.86.refs_0_ = bf16[384,2048]{1,0:T(8,128)(2,1)} custom-call(bf16[1,384,2048]{2,1,0:T(8,128)(2,1)} %panel.1, bf16[1,2048,2048]{2,1,0:T(8,128)(2,1)} %inverse.1), custom_call_target="tpu_custom_call" | custom-call | flops 2000000000 | bytes 8000000 | tf_op jit(solution)/shard_map/pallas_call | solution.py:66
  7.3 2.0 collective-permute-start.2
  11.9 2.2 shard_map.87
  20.9 23.6 %collective-permute-done.2.refs_3_ = bf16[384,2048]{1,0:T(8,128)(2,1)} collective-permute-done((bf16[384,2048]{1,0:T(8,128)(2,1)}, bf16[384,2048]{1,0:T(8,128)(2,1)}, u32[]{:S(2)}, u32[]{:S(2)}) %collective-permute-start.2) | collective-permute-done | bytes 1572896 | tf_op jit(solution)/shard_map/ppermute | solution.py:26
  44.5 2.0 collective-permute-done.1.refs_2_
  48.5 2.1 collective-permute-start.5
  50.6 32.6 %collective-permute-done.6.refs_5_ = bf16[384,2048]{1,0:T(8,128)(2,1)} collective-permute-done((bf16[384,2048]{1,0:T(8,128)(2,1)}, bf16[384,2048]{1,0:T(8,128)(2,1)}, u32[]{:S(2)}, u32[]{:S(2)}) %collective-permute-start.6) | collective-permute-done | bytes 1572896 | tf_op jit(solution)/shard_map/ppermute | solution.py:36
  88.0 18.6 %collective-permute-done.10.refs_7_ = bf16[384,2048]{1,0:T(8,128)(2,1)} collective-permute-done((bf16[384,2048]{1,0:T(8,128)(2,1)}, bf16[384,2048]{1,0:T(8,128)(2,1)}, u32[]{:S(2)}, u32[]{:S(2)}) %collective-permute-start.10) | collective-permute-done | bytes 1572896 | tf_op jit(solution)/shard_map/ppermute | solution.py:36
  107.7 2.6 collective-permute-done.15.refs_15_
  110.3 6.6 %shard_map.88 = bf16[512,1024]{1,0:T(8,128)(2,1)} custom-call(s32[8]{0:T(128)} %get-tuple-element.65.pan_rows, s32[8]{0:T(128)} %get-tuple-element.66.pan_cols, s32[1]{0:T(128)} %bitcast.3.offset, bf16[384,2048]{1,0:T(8,128)(2,1)} %shard_map.86.refs_0_, bf16[384,2048]{1,0:T(8,128)(2,1)} %collective-permute-done.refs_1_, ...), custom_call_target="tpu_custom_call" | custom-call | flops 2200000000 | bytes 8000000 | tf_op jit(solution)/shard_map/pallas_call | solution.py:236
  116.9 7.9 %all-to-all-start = ((bf16[8,64,1024]{2,1,0:T(8,128)(2,1)}), bf16[8,64,1024]{2,1,0:T(8,128)(2,1)S(1)}, u32[]{:S(2)}, u32[]{:S(2)}) async-start(bf16[8,64,1024]{2,1,0:T(8,128)(2,1)} %bitcast.57), calls=%async_computation | async-start | bytes 2097152 | tf_op jit(solution)/shard_map/all_to_all | solution.py:354
  125.9 2.4 collective-permute-start.31
  130.1 21.4 %shard_map.89 = (bf16[1024,256]{1,0:T(8,128)(2,1)}, bf16[1024,256]{1,0:T(8,128)(2,1)}, bf16[1024,256]{1,0:T(8,128)(2,1)}, bf16[1024,256]{1,0:T(8,128)(2,1)}, bf1...) custom-call(s32[48]{0:T(128)} %select_reduce_fusion.dest, ...), custom_call_target="tpu_custom_call" | custom-call | flops 20000000000 | bytes 36000000 | tf_op jit(solution)/shard_map/pallas_call | solution.py:187
  156.3 3.0 %collective-permute-done.33 = bf16[64,1024]{1,0:T(8,128)(2,1)S(1)} collective-permute-done((bf16[64,1024]{1,0:T(8,128)(2,1)S(1)}, bf16[64,1024]{1,0:T(8,128)(2,1)S(1)}, u32[]{:S(2)}, u32[]{:S(2)}) %collective-permute-start.33) | collective-permute-done | bytes 131104 | tf_op jit(solution)/shard_map/ppermute | solution.py:26
  160.4 1.9 collective-permute-done.16
  164.5 3.4 %collective-permute-done.19 = bf16[1024,256]{1,0:T(8,128)(2,1)S(1)} collective-permute-done((bf16[1024,256]{1,0:T(8,128)(2,1)}, bf16[1024,256]{1,0:T(8,128)(2,1)S(1)}, u32[]{:S(2)}, u32[]{:S(2)}) %collective-permute-start.19) | collective-permute-done | bytes 524320 | tf_op jit(solution)/shard_map/ppermute | solution.py:36
  167.9 5.9 %collective-permute-start.34 = (bf16[64,1024]{1,0:T(8,128)(2,1)S(1)}, bf16[64,1024]{1,0:T(8,128)(2,1)S(1)}, u32[]{:S(2)}, u32[]{:S(2)}) collective-permute-start(bf16[64,1024]{1,0:T(8,128)(2,1)S(1)} %get-tuple-element.121), channel_id=1, source_target_pairs={{0,0},{1,16},{2,32},{3,48},{4,64},{5,80},{6,96},{7,112},{8,1},{9,1... | collective-permute-start | bytes 393224 | tf_op jit(solution)/shard_map/ppermute | solution.py:389
  176.6 7.0 %collective-permute-done.34 = bf16[64,1024]{1,0:T(8,128)(2,1)S(1)} collective-permute-done((bf16[64,1024]{1,0:T(8,128)(2,1)S(1)}, bf16[64,1024]{1,0:T(8,128)(2,1)S(1)}, u32[]{:S(2)}, u32[]{:S(2)}) %collective-permute-start.34) | collective-permute-done | bytes 131104 | tf_op jit(solution)/shard_map/ppermute | solution.py:389
  184.6 5.6 %collective-permute-start.20 = (bf16[1024,256]{1,0:T(8,128)(2,1)}, bf16[1024,256]{1,0:T(8,128)(2,1)}, u32[]{:S(2)}, u32[]{:S(2)}) collective-permute-start(bf16[1024,256]{1,0:T(8,128)(2,1)} %add_convert_fusion.7), channel_id=1, source_target_pairs={{0,16},{1,49},{16,32},{17,1},{32,48},{33,17},{48,0},{49,33},{2,18}... | collective-permute-start | bytes 1572872 | tf_op jit(solution)/shard_map/ppermute | solution.py:36
  190.1 2.6 collective-permute-start.24
  194.4 10.0 %all-to-all-start.1 = ((bf16[16,64,1024]{2,1,0:T(8,128)(2,1)}), bf16[16,64,1024]{2,1,0:T(8,128)(2,1)}, u32[]{:S(2)}, u32[]{:S(2)}) async-start(bf16[16,64,1024]{2,1,0:T(8,128)(2,1)} %broadcast_in_dim.88), calls=%async_computation.1 | async-start | bytes 4194304 | tf_op jit(solution)/shard_map/all_to_all | solution.py:397
  204.5 2.0 collective-permute-start.38
  211.4 3.3 %collective-permute-start.21 = (bf16[1024,256]{1,0:T(8,128)(2,1)S(1)}, bf16[1024,256]{1,0:T(8,128)(2,1)S(1)}, u32[]{:S(2)}, u32[]{:S(2)}) collective-permute-start(bf16[1024,256]{1,0:T(8,128)(2,1)S(1)} %add_convert_fusion.6), channel_id=1, source_target_pairs={{0,16},{1,49},{16,32},{17,1},{32,48},{33,17},{48,0},{49,33},{2,18}... | collective-permute-start | bytes 1572872 | tf_op jit(solution)/shard_map/ppermute | solution.py:36
  215.9 5.6 %collective-permute-done.36 = bf16[2,64,1024]{2,1,0:T(8,128)(2,1)S(1)} collective-permute-done((bf16[2,64,1024]{2,1,0:T(8,128)(2,1)S(1)}, bf16[2,64,1024]{2,1,0:T(8,128)(2,1)S(1)}, u32[]{:S(2)}, u32[]{:S(2)}) %collective-permute-start.36) | collective-permute-done | bytes 262176 | tf_op jit(solution)/shard_map/ppermute | solution.py:26
  223.7 6.1 %collective-permute-done.21 = bf16[1024,256]{1,0:T(8,128)(2,1)S(1)} collective-permute-done((bf16[1024,256]{1,0:T(8,128)(2,1)S(1)}, bf16[1024,256]{1,0:T(8,128)(2,1)S(1)}, u32[]{:S(2)}, u32[]{:S(2)}) %collective-permute-start.21) | collective-permute-done | bytes 524320 | tf_op jit(solution)/shard_map/ppermute | solution.py:36
  229.9 2.0 collective-permute-start.22
  231.9 3.5 %collective-permute-done.25 = bf16[1024,256]{1,0:T(8,128)(2,1)S(1)} collective-permute-done((bf16[1024,256]{1,0:T(8,128)(2,1)S(1)}, bf16[1024,256]{1,0:T(8,128)(2,1)S(1)}, u32[]{:S(2)}, u32[]{:S(2)}) %collective-permute-start.25) | collective-permute-done | bytes 524320 | tf_op jit(solution)/shard_map/ppermute | solution.py:36
  235.5 2.0 collective-permute-start.26
  237.5 3.5 %collective-permute-done.28 = bf16[1024,256]{1,0:T(8,128)(2,1)S(1)} collective-permute-done((bf16[1024,256]{1,0:T(8,128)(2,1)S(1)}, bf16[1024,256]{1,0:T(8,128)(2,1)S(1)}, u32[]{:S(2)}, u32[]{:S(2)}) %collective-permute-start.28) | collective-permute-done | bytes 524320 | tf_op jit(solution)/shard_map/ppermute | solution.py:36
  241.1 2.0 collective-permute-start.29
  246.6 9.9 %collective-permute-done.29 = bf16[1024,256]{1,0:T(8,128)(2,1)S(1)} collective-permute-done((bf16[1024,256]{1,0:T(8,128)(2,1)S(1)}, bf16[1024,256]{1,0:T(8,128)(2,1)S(1)}, u32[]{:S(2)}, u32[]{:S(2)}) %collective-permute-start.29) | collective-permute-done | bytes 524320 | tf_op jit(solution)/shard_map/ppermute | solution.py:26
  257.7 3.3 %broadcast_select_fusion.1 = (bf16[16,64,1024]{2,1,0:T(8,128)(2,1)}, bf16[16,64,1024]{2,1,0:T(8,128)(2,1)S(1)}) fusion(bf16[16,64,1024]{2,1,0:T(8,128)(2,1)} %all-to-all-done.1, pred[]{:T(512)} %bitcast.24, pred[16]{0:T(512)(128)(4,1)S(1)} %broadcast_in_dim.85), kind=kLoop, calls=%fused_computation.5 | loop fusion | flops 2097152 | bytes 6291473 | tf_op jit(solution)/shard_map/jit(_where)/select_n | solution.py:409
  (143 shorter events, 50.2 us)
Async XLA Ops:
  7.2 13.8 %collective-permute-start.3 = (bf16[384,2048]{1,0:T(8,128)(2,1)}, bf16[384,2048]{1,0:T(8,128)(2,1)}, u32[]{:S(2)}, u32[]{:S(2)}) collective-permute-start(bf16[384,2048]{1,0:T(8,128)(2,1)} %shard_map.86.refs_0_), channel_id=1, source_target_pairs={{0,1},{1,0},{2,3},{3,2},{4,5},{5,4},{6,7},{7,6},{8,9},{9,8},{10,11... | collective-permute-start | bytes 4718600 | tf_op jit(solution)/shard_map/ppermute | solution.py:26
  7.3 37.3 %collective-permute-start.2 = (bf16[384,2048]{1,0:T(8,128)(2,1)}, bf16[384,2048]{1,0:T(8,128)(2,1)}, u32[]{:S(2)}, u32[]{:S(2)}) collective-permute-start(bf16[384,2048]{1,0:T(8,128)(2,1)} %shard_map.86.refs_0_), channel_id=1, source_target_pairs={{0,2},{2,0},{1,3},{3,1},{4,6},{6,4},{5,7},{7,5},{8,10},{10,8},{9,1... | collective-permute-start | bytes 4718600 | tf_op jit(solution)/shard_map/ppermute | solution.py:26
  9.2 37.3 %collective-permute-start.1 = (bf16[384,2048]{1,0:T(8,128)(2,1)}, bf16[384,2048]{1,0:T(8,128)(2,1)}, u32[]{:S(2)}, u32[]{:S(2)}) collective-permute-start(bf16[384,2048]{1,0:T(8,128)(2,1)} %shard_map.86.refs_0_), channel_id=1, source_target_pairs={{0,12},{1,5},{4,0},{5,9},{8,4},{9,13},{12,8},{13,1},{2,14},{3,7},{... | collective-permute-start | bytes 4718600 | tf_op jit(solution)/shard_map/ppermute | solution.py:36
  9.8 36.7 %collective-permute-start = (bf16[384,2048]{1,0:T(8,128)(2,1)}, bf16[384,2048]{1,0:T(8,128)(2,1)}, u32[]{:S(2)}, u32[]{:S(2)}) collective-permute-start(bf16[384,2048]{1,0:T(8,128)(2,1)} %shard_map.86.refs_0_), channel_id=1, source_target_pairs={{0,4},{1,13},{4,8},{5,1},{8,12},{9,5},{12,0},{13,9},{2,6},{3,15},{... | collective-permute-start | bytes 4718600 | tf_op jit(solution)/shard_map/ppermute | solution.py:36
  46.7 36.6 %collective-permute-start.6 = (bf16[384,2048]{1,0:T(8,128)(2,1)}, bf16[384,2048]{1,0:T(8,128)(2,1)}, u32[]{:S(2)}, u32[]{:S(2)}) collective-permute-start(bf16[384,2048]{1,0:T(8,128)(2,1)} %collective-permute-done.2.refs_3_), channel_id=1, source_target_pairs={{0,12},{1,5},{4,0},{5,9},{8,4},{9,13},{12,8},{13,1},{2,14},{3,7},{... | collective-permute-start | bytes 4718600 | tf_op jit(solution)/shard_map/ppermute | solution.py:36
  47.8 35.4 %collective-permute-start.8 = (bf16[384,2048]{1,0:T(8,128)(2,1)}, bf16[384,2048]{1,0:T(8,128)(2,1)}, u32[]{:S(2)}, u32[]{:S(2)}) collective-permute-start(bf16[384,2048]{1,0:T(8,128)(2,1)} %collective-permute-done.refs_1_), channel_id=1, source_target_pairs={{0,1},{1,0},{2,3},{3,2},{4,5},{5,4},{6,7},{7,6},{8,9},{9,8},{10,11... | collective-permute-start | bytes 4718600 | tf_op jit(solution)/shard_map/ppermute | solution.py:26
  48.5 36.6 %collective-permute-start.7 = (bf16[384,2048]{1,0:T(8,128)(2,1)}, bf16[384,2048]{1,0:T(8,128)(2,1)}, u32[]{:S(2)}, u32[]{:S(2)}) collective-permute-start(bf16[384,2048]{1,0:T(8,128)(2,1)} %collective-permute-done.refs_1_), channel_id=1, source_target_pairs={{0,2},{2,0},{1,3},{3,1},{4,6},{6,4},{5,7},{7,5},{8,10},{10,8},{9,1... | collective-permute-start | bytes 4718600 | tf_op jit(solution)/shard_map/ppermute | solution.py:26
  48.5 36.6 %collective-permute-start.5 = (bf16[384,2048]{1,0:T(8,128)(2,1)}, bf16[384,2048]{1,0:T(8,128)(2,1)}, u32[]{:S(2)}, u32[]{:S(2)}) collective-permute-start(bf16[384,2048]{1,0:T(8,128)(2,1)} %collective-permute-done.refs_1_), channel_id=1, source_target_pairs={{0,4},{1,13},{4,8},{5,1},{8,12},{9,5},{12,0},{13,9},{2,6},{3,15},{... | collective-permute-start | bytes 4718600 | tf_op jit(solution)/shard_map/ppermute | solution.py:36
  85.1 21.5 %collective-permute-start.10 = (bf16[384,2048]{1,0:T(8,128)(2,1)}, bf16[384,2048]{1,0:T(8,128)(2,1)}, u32[]{:S(2)}, u32[]{:S(2)}) collective-permute-start(bf16[384,2048]{1,0:T(8,128)(2,1)} %collective-permute-done.7.refs_6_), channel_id=1, source_target_pairs={{0,4},{1,13},{4,8},{5,1},{8,12},{9,5},{12,0},{13,9},{2,6},{3,15},{... | collective-permute-start | bytes 4718600 | tf_op jit(solution)/shard_map/ppermute | solution.py:36
  87.0 20.7 %collective-permute-start.11 = (bf16[384,2048]{1,0:T(8,128)(2,1)}, bf16[384,2048]{1,0:T(8,128)(2,1)}, u32[]{:S(2)}, u32[]{:S(2)}) collective-permute-start(bf16[384,2048]{1,0:T(8,128)(2,1)} %collective-permute-done.2.refs_3_), channel_id=1, source_target_pairs={{0,1},{1,0},{2,3},{3,2},{4,5},{5,4},{6,7},{7,6},{8,9},{9,8},{10,11... | collective-permute-start | bytes 4718600 | tf_op jit(solution)/shard_map/ppermute | solution.py:26
  87.3 20.4 %collective-permute-start.14 = (bf16[384,2048]{1,0:T(8,128)(2,1)}, bf16[384,2048]{1,0:T(8,128)(2,1)}, u32[]{:S(2)}, u32[]{:S(2)}) collective-permute-start(bf16[384,2048]{1,0:T(8,128)(2,1)} %collective-permute-done.7.refs_6_), channel_id=1, source_target_pairs={{0,1},{1,0},{2,3},{3,2},{4,5},{5,4},{6,7},{7,6},{8,9},{9,8},{10,11... | collective-permute-start | bytes 4718600 | tf_op jit(solution)/shard_map/ppermute | solution.py:26
  87.5 20.2 %collective-permute-start.12 = (bf16[384,2048]{1,0:T(8,128)(2,1)}, bf16[384,2048]{1,0:T(8,128)(2,1)}, u32[]{:S(2)}, u32[]{:S(2)}) collective-permute-start(bf16[384,2048]{1,0:T(8,128)(2,1)} %collective-permute-done.5.refs_4_), channel_id=1, source_target_pairs={{0,1},{1,0},{2,3},{3,2},{4,5},{5,4},{6,7},{7,6},{8,9},{9,8},{10,11... | collective-permute-start | bytes 4718600 | tf_op jit(solution)/shard_map/ppermute | solution.py:26
  87.8 19.9 %collective-permute-start.13 = (bf16[384,2048]{1,0:T(8,128)(2,1)}, bf16[384,2048]{1,0:T(8,128)(2,1)}, u32[]{:S(2)}, u32[]{:S(2)}) collective-permute-start(bf16[384,2048]{1,0:T(8,128)(2,1)} %collective-permute-done.6.refs_5_), channel_id=1, source_target_pairs={{0,1},{1,0},{2,3},{3,2},{4,5},{5,4},{6,7},{7,6},{8,9},{9,8},{10,11... | collective-permute-start | bytes 4718600 | tf_op jit(solution)/shard_map/ppermute | solution.py:26
  116.9 35.7 %all-to-all-start = ((bf16[8,64,1024]{2,1,0:T(8,128)(2,1)}), bf16[8,64,1024]{2,1,0:T(8,128)(2,1)S(1)}, u32[]{:S(2)}, u32[]{:S(2)}) async-start(bf16[8,64,1024]{2,1,0:T(8,128)(2,1)} %bitcast.57), calls=%async_computation | async-start | bytes 2097152 | tf_op jit(solution)/shard_map/all_to_all | solution.py:354
  124.8 26.7 %collective-permute-start.30 = (bf16[2,64,1024]{2,1,0:T(8,128)(2,1)}, bf16[2,64,1024]{2,1,0:T(8,128)(2,1)S(1)}, u32[]{:S(2)}, u32[]{:S(2)}) collective-permute-start(bf16[2,64,1024]{2,1,0:T(8,128)(2,1)} %get-tuple-element.116), channel_id=1, source_target_pairs={{0,4},{4,8},{8,12},{12,0},{1,5},{5,9},{9,13},{13,1},{2,6},{6,10},{... | collective-permute-start | bytes 786440 | tf_op jit(solution)/shard_map/ppermute | solution.py:26
  125.9 25.6 %collective-permute-start.31 = (bf16[2,64,1024]{2,1,0:T(8,128)(2,1)}, bf16[2,64,1024]{2,1,0:T(8,128)(2,1)}, u32[]{:S(2)}, u32[]{:S(2)}) collective-permute-start(bf16[2,64,1024]{2,1,0:T(8,128)(2,1)} %get-tuple-element.118), channel_id=1, source_target_pairs={{0,12},{4,0},{8,4},{12,8},{1,13},{5,1},{9,5},{13,9},{2,14},{6,2},{... | collective-permute-start | bytes 786440 | tf_op jit(solution)/shard_map/ppermute | solution.py:26
  128.3 23.2 %collective-permute-start.32 = (bf16[2,64,1024]{2,1,0:T(8,128)(2,1)S(1)}, bf16[2,64,1024]{2,1,0:T(8,128)(2,1)}, u32[]{:S(2)}, u32[]{:S(2)}) collective-permute-start(bf16[2,64,1024]{2,1,0:T(8,128)(2,1)S(1)} %get-tuple-element.120), channel_id=1, source_target_pairs={{0,8},{4,12},{8,0},{12,4},{1,9},{5,13},{9,1},{13,5},{2,10},{6,14},... | collective-permute-start | bytes 786440 | tf_op jit(solution)/shard_map/ppermute | solution.py:26
  154.4 19.4 %collective-permute-start.23 = (bf16[1024,256]{1,0:T(8,128)(2,1)}, bf16[1024,256]{1,0:T(8,128)(2,1)S(1)}, u32[]{:S(2)}, u32[]{:S(2)}) collective-permute-start(bf16[1024,256]{1,0:T(8,128)(2,1)} %get-tuple-element.107), channel_id=1, source_target_pairs={{0,16},{1,49},{16,32},{17,1},{32,48},{33,17},{48,0},{49,33},{2,18}... | collective-permute-start | bytes 1572872 | tf_op jit(solution)/shard_map/ppermute | solution.py:36
  163.2 44.5 %collective-permute-start.17 = (bf16[1024,256]{1,0:T(8,128)(2,1)}, bf16[1024,256]{1,0:T(8,128)(2,1)S(1)}, u32[]{:S(2)}, u32[]{:S(2)}) collective-permute-start(bf16[1024,256]{1,0:T(8,128)(2,1)} %add_convert_fusion.9), channel_id=1, source_target_pairs={{0,16},{1,49},{16,32},{17,1},{32,48},{33,17},{48,0},{49,33},{2,18}... | collective-permute-start | bytes 1572872 | tf_op jit(solution)/shard_map/ppermute | solution.py:36
  167.9 15.7 %collective-permute-start.34 = (bf16[64,1024]{1,0:T(8,128)(2,1)S(1)}, bf16[64,1024]{1,0:T(8,128)(2,1)S(1)}, u32[]{:S(2)}, u32[]{:S(2)}) collective-permute-start(bf16[64,1024]{1,0:T(8,128)(2,1)S(1)} %get-tuple-element.121), channel_id=1, source_target_pairs={{0,0},{1,16},{2,32},{3,48},{4,64},{5,80},{6,96},{7,112},{8,1},{9,1... | collective-permute-start | bytes 393224 | tf_op jit(solution)/shard_map/ppermute | solution.py:389
  174.8 29.7 %collective-permute-start.27 = (bf16[1024,256]{1,0:T(8,128)(2,1)}, bf16[1024,256]{1,0:T(8,128)(2,1)}, u32[]{:S(2)}, u32[]{:S(2)}) collective-permute-start(bf16[1024,256]{1,0:T(8,128)(2,1)} %add_convert_fusion.2), channel_id=1, source_target_pairs={{0,16},{1,49},{16,32},{17,1},{32,48},{33,17},{48,0},{49,33},{2,18}... | collective-permute-start | bytes 1572872 | tf_op jit(solution)/shard_map/ppermute | solution.py:36
  184.6 24.9 %collective-permute-start.20 = (bf16[1024,256]{1,0:T(8,128)(2,1)}, bf16[1024,256]{1,0:T(8,128)(2,1)}, u32[]{:S(2)}, u32[]{:S(2)}) collective-permute-start(bf16[1024,256]{1,0:T(8,128)(2,1)} %add_convert_fusion.7), channel_id=1, source_target_pairs={{0,16},{1,49},{16,32},{17,1},{32,48},{33,17},{48,0},{49,33},{2,18}... | collective-permute-start | bytes 1572872 | tf_op jit(solution)/shard_map/ppermute | solution.py:36
  190.1 21.3 %collective-permute-start.24 = (bf16[1024,256]{1,0:T(8,128)(2,1)}, bf16[1024,256]{1,0:T(8,128)(2,1)}, u32[]{:S(2)}, u32[]{:S(2)}) collective-permute-start(bf16[1024,256]{1,0:T(8,128)(2,1)} %get-tuple-element.108), channel_id=1, source_target_pairs={{0,16},{1,49},{16,32},{17,1},{32,48},{33,17},{48,0},{49,33},{2,18}... | collective-permute-start | bytes 1572872 | tf_op jit(solution)/shard_map/ppermute | solution.py:36
  194.4 63.3 %all-to-all-start.1 = ((bf16[16,64,1024]{2,1,0:T(8,128)(2,1)}), bf16[16,64,1024]{2,1,0:T(8,128)(2,1)}, u32[]{:S(2)}, u32[]{:S(2)}) async-start(bf16[16,64,1024]{2,1,0:T(8,128)(2,1)} %broadcast_in_dim.88), calls=%async_computation.1 | async-start | bytes 4194304 | tf_op jit(solution)/shard_map/all_to_all | solution.py:397
  204.5 19.1 %collective-permute-start.38 = (bf16[2,64,1024]{2,1,0:T(8,128)(2,1)S(1)}, bf16[2,64,1024]{2,1,0:T(8,128)(2,1)S(1)}, u32[]{:S(2)}, u32[]{:S(2)}) collective-permute-start(bf16[2,64,1024]{2,1,0:T(8,128)(2,1)S(1)} %pad_maximum_fusion), channel_id=1, source_target_pairs={{0,16},{16,32},{32,48},{48,0},{1,17},{17,33},{33,49},{49,1},{2,18}... | collective-permute-start | bytes 786440 | tf_op jit(solution)/shard_map/ppermute | solution.py:26
  206.4 15.7 %collective-permute-start.37 = (bf16[2,64,1024]{2,1,0:T(8,128)(2,1)S(1)}, bf16[2,64,1024]{2,1,0:T(8,128)(2,1)S(1)}, u32[]{:S(2)}, u32[]{:S(2)}) collective-permute-start(bf16[2,64,1024]{2,1,0:T(8,128)(2,1)S(1)} %pad_maximum_fusion), channel_id=1, source_target_pairs={{0,32},{16,48},{32,0},{48,16},{1,33},{17,49},{33,1},{49,17},{2,34}... | collective-permute-start | bytes 786440 | tf_op jit(solution)/shard_map/ppermute | solution.py:26
  209.5 34.8 %collective-permute-start.18 = (bf16[1024,256]{1,0:T(8,128)(2,1)S(1)}, bf16[1024,256]{1,0:T(8,128)(2,1)S(1)}, u32[]{:S(2)}, u32[]{:S(2)}) collective-permute-start(bf16[1024,256]{1,0:T(8,128)(2,1)S(1)} %add_convert_fusion.8), channel_id=1, source_target_pairs={{0,16},{1,49},{16,32},{17,1},{32,48},{33,17},{48,0},{49,33},{2,18}... | collective-permute-start | bytes 1572872 | tf_op jit(solution)/shard_map/ppermute | solution.py:36
  211.4 18.3 %collective-permute-start.21 = (bf16[1024,256]{1,0:T(8,128)(2,1)S(1)}, bf16[1024,256]{1,0:T(8,128)(2,1)S(1)}, u32[]{:S(2)}, u32[]{:S(2)}) collective-permute-start(bf16[1024,256]{1,0:T(8,128)(2,1)S(1)} %add_convert_fusion.6), channel_id=1, source_target_pairs={{0,16},{1,49},{16,32},{17,1},{32,48},{33,17},{48,0},{49,33},{2,18}... | collective-permute-start | bytes 1572872 | tf_op jit(solution)/shard_map/ppermute | solution.py:36
  221.4 13.9 %collective-permute-start.25 = (bf16[1024,256]{1,0:T(8,128)(2,1)S(1)}, bf16[1024,256]{1,0:T(8,128)(2,1)S(1)}, u32[]{:S(2)}, u32[]{:S(2)}) collective-permute-start(bf16[1024,256]{1,0:T(8,128)(2,1)S(1)} %add_convert_fusion.4), channel_id=1, source_target_pairs={{0,16},{1,49},{16,32},{17,1},{32,48},{33,17},{48,0},{49,33},{2,18}... | collective-permute-start | bytes 1572872 | tf_op jit(solution)/shard_map/ppermute | solution.py:36
  222.2 18.8 %collective-permute-start.28 = (bf16[1024,256]{1,0:T(8,128)(2,1)S(1)}, bf16[1024,256]{1,0:T(8,128)(2,1)S(1)}, u32[]{:S(2)}, u32[]{:S(2)}) collective-permute-start(bf16[1024,256]{1,0:T(8,128)(2,1)S(1)} %add_convert_fusion.1), channel_id=1, source_target_pairs={{0,16},{1,49},{16,32},{17,1},{32,48},{33,17},{48,0},{49,33},{2,18}... | collective-permute-start | bytes 1572872 | tf_op jit(solution)/shard_map/ppermute | solution.py:36
  229.9 15.4 %collective-permute-start.22 = (bf16[1024,256]{1,0:T(8,128)(2,1)S(1)}, bf16[1024,256]{1,0:T(8,128)(2,1)S(1)}, u32[]{:S(2)}, u32[]{:S(2)}) collective-permute-start(bf16[1024,256]{1,0:T(8,128)(2,1)S(1)} %add_convert_fusion.5), channel_id=1, source_target_pairs={{0,64},{64,0},{1,65},{65,1},{2,66},{66,2},{3,67},{67,3},{4,68},{68... | collective-permute-start | bytes 1572872 | tf_op jit(solution)/shard_map/ppermute | solution.py:26
  241.1 15.4 %collective-permute-start.29 = (bf16[1024,256]{1,0:T(8,128)(2,1)S(1)}, bf16[1024,256]{1,0:T(8,128)(2,1)S(1)}, u32[]{:S(2)}, u32[]{:S(2)}) collective-permute-start(bf16[1024,256]{1,0:T(8,128)(2,1)S(1)} %add_convert_fusion), channel_id=1, source_target_pairs={{0,64},{64,0},{1,65},{65,1},{2,66},{66,2},{3,67},{67,3},{4,68},{68... | collective-permute-start | bytes 1572872 | tf_op jit(solution)/shard_map/ppermute | solution.py:26
  (28 other events, 440.8 us)

commit v5 on v4

--- a/solution.py
+++ b/solution.py
@@ -375,7 +375,7 @@
             rings.append(
                 Ring(
                     lambda k: main[d][k][half],
-                    None if d == 1 or half == 0 else rings[half].marks[0],
+                    None if d == 1 else rings[half].marks[0],
                 )
             )
     far = [shift(ring.total.astype(BF), "h", 1).astype(F32) for ring in rings[:2]]

time: 268 us -> 259 us (0.966)
  waiting for transfers between devices: 127 us -> 113 us
  starting transfers between devices: 70.8 us -> 77.6 us
    ppermute x17, starting transfers between devices: 29.9 us -> 40.7 us  [mirrored(): return lax.ppermute(array, (axis, 'c'), pairs)]
    ppermute x21, waiting for transfers between devices: 47.6 us -> 38.1 us  [shift(): lax.ppermute(array, axis, [(i, (i + step) % size) for i in range(size)])]
    ppermute x1, waiting for transfers between devices: 7.02 us -> 0.01 us  [local(): moved = lax.ppermute(masked, AXES, pairs)]
    all_to_all x1, starting transfers between devices: 10 us -> 5.63 us  [local(): lax.all_to_all(copies, ('x', 'z', 'c'), split_axis=0, concat_axis=0, tile...]
where the time goes in v5:
time: 259 us; the launch traced here: 256 us
  waiting for transfers between devices  113 us (44%)
  starting transfers between devices  77.6 us (30%)
  Pallas kernels  36.5 us (14%)
  other arithmetic  19.9 us (8%)
  local copies, waits for them, and re-layouts  5.38 us (2%)
    ppermute x17, waiting for transfers between devices, mirrored(): return lax.ppermute(array, (axis, 'c'), pairs)  74.6 us
    ppermute x17, starting transfers between devices, mirrored(): return lax.ppermute(array, (axis, 'c'), pairs)  40.7 us
    ppermute x21, waiting for transfers between devices, shift(): lax.ppermute(array, axis, [(i, (i + step) % size) for i in range(size)])  38.1 us
    pallas_call x1, Pallas kernels, main_parts(): pl.pallas_call(functools.partial(main_kernel, [p[1:] for p in pieces]), o...  21.2 us
    ppermute x21, starting transfers between devices, shift(): lax.ppermute(array, axis, [(i, (i + step) % size) for i in range(size)])  16 us
    all_to_all x1, starting transfers between devices, local(): lax.all_to_all(pan.reshape(8, 64, 1024), ('h', 'y'), split_axis=0, concat...  8 us
    ppermute x1, starting transfers between devices, local(): moved = lax.ppermute(masked, AXES, pairs)  7.16 us
    pallas_call x1, Pallas kernels, panel_parts(): pl.pallas_call(functools.partial(panel_kernel, [p[1:] for p in pieces]),...  6.72 us
  transfers between devices with their start and end apart: 41, of which 17 were waited for; matrix products, arithmetic and copies ran while one was open for 8% of the time, Pallas kernels for 9%

profile of v5, /device:TPU:18, one launch (start us, length us, event | category | flops | bytes accessed | tf_op | source)
XLA Modules:
  0.0 255.8 jit_solution(16774955153212601798)
XLA Ops:
  0.7 6.5 %shard_map.86.refs_0_ = bf16[384,2048]{1,0:T(8,128)(2,1)} custom-call(bf16[1,384,2048]{2,1,0:T(8,128)(2,1)} %panel.1, bf16[1,2048,2048]{2,1,0:T(8,128)(2,1)} %inverse.1), custom_call_target="tpu_custom_call" | custom-call | flops 2000000000 | bytes 8000000 | tf_op jit(solution)/shard_map/pallas_call | solution.py:66
  7.3 2.0 collective-permute-start.2
  11.9 2.2 shard_map.87
  20.9 23.6 %collective-permute-done.2.refs_3_ = bf16[384,2048]{1,0:T(8,128)(2,1)} collective-permute-done((bf16[384,2048]{1,0:T(8,128)(2,1)}, bf16[384,2048]{1,0:T(8,128)(2,1)}, u32[]{:S(2)}, u32[]{:S(2)}) %collective-permute-start.2) | collective-permute-done | bytes 1572896 | tf_op jit(solution)/shard_map/ppermute | solution.py:26
  48.5 2.1 collective-permute-start.5
  50.6 32.6 %collective-permute-done.6.refs_5_ = bf16[384,2048]{1,0:T(8,128)(2,1)} collective-permute-done((bf16[384,2048]{1,0:T(8,128)(2,1)}, bf16[384,2048]{1,0:T(8,128)(2,1)}, u32[]{:S(2)}, u32[]{:S(2)}) %collective-permute-start.6) | collective-permute-done | bytes 1572896 | tf_op jit(solution)/shard_map/ppermute | solution.py:36
  88.0 18.6 %collective-permute-done.10.refs_7_ = bf16[384,2048]{1,0:T(8,128)(2,1)} collective-permute-done((bf16[384,2048]{1,0:T(8,128)(2,1)}, bf16[384,2048]{1,0:T(8,128)(2,1)}, u32[]{:S(2)}, u32[]{:S(2)}) %collective-permute-start.10) | collective-permute-done | bytes 1572896 | tf_op jit(solution)/shard_map/ppermute | solution.py:36
  107.7 2.6 %collective-permute-done.15.refs_15_ = bf16[384,2048]{1,0:T(8,128)(2,1)} collective-permute-done((bf16[384,2048]{1,0:T(8,128)(2,1)}, bf16[384,2048]{1,0:T(8,128)(2,1)}, u32[]{:S(2)}, u32[]{:S(2)}) %collective-permute-start.15) | collective-permute-done | bytes 1572896 | tf_op jit(solution)/shard_map/ppermute | solution.py:26
  110.3 6.7 %shard_map.88 = bf16[512,1024]{1,0:T(8,128)(2,1)} custom-call(s32[8]{0:T(128)} %get-tuple-element.66.pan_rows, s32[8]{0:T(128)} %get-tuple-element.67.pan_cols, s32[1]{0:T(128)} %bitcast.3.offset, bf16[384,2048]{1,0:T(8,128)(2,1)} %shard_map.86.refs_0_, bf16[384,2048]{1,0:T(8,128)(2,1)} %collective-permute-done.refs_1_, ...), custom_call_target="tpu_custom_call" | custom-call | flops 2200000000 | bytes 8000000 | tf_op jit(solution)/shard_map/pallas_call | solution.py:236
  117.0 8.0 %all-to-all-start = ((bf16[8,64,1024]{2,1,0:T(8,128)(2,1)}), bf16[8,64,1024]{2,1,0:T(8,128)(2,1)S(1)}, u32[]{:S(2)}, u32[]{:S(2)}) async-start(bf16[8,64,1024]{2,1,0:T(8,128)(2,1)} %bitcast.57), calls=%async_computation | async-start | bytes 2097152 | tf_op jit(solution)/shard_map/all_to_all | solution.py:354
  126.1 2.5 collective-permute-start.31
  130.4 21.2 %shard_map.89 = (bf16[1024,256]{1,0:T(8,128)(2,1)}, bf16[1024,256]{1,0:T(8,128)(2,1)}, bf16[1024,256]{1,0:T(8,128)(2,1)}, bf16[1024,256]{1,0:T(8,128)(2,1)}, bf1...) custom-call(s32[48]{0:T(128)} %select_reduce_fusion.dest, ...), custom_call_target="tpu_custom_call" | custom-call | flops 20000000000 | bytes 36000000 | tf_op jit(solution)/shard_map/pallas_call | solution.py:187
  154.5 2.1 collective-permute-start.23
  156.9 4.8 %collective-permute-done.33 = bf16[64,1024]{1,0:T(8,128)(2,1)S(1)} collective-permute-done((bf16[64,1024]{1,0:T(8,128)(2,1)S(1)}, bf16[64,1024]{1,0:T(8,128)(2,1)S(1)}, u32[]{:S(2)}, u32[]{:S(2)}) %collective-permute-start.33) | collective-permute-done | bytes 131104 | tf_op jit(solution)/shard_map/ppermute | solution.py:26
  162.8 7.2 %collective-permute-start.34 = (bf16[64,1024]{1,0:T(8,128)(2,1)S(1)}, bf16[64,1024]{1,0:T(8,128)(2,1)S(1)}, u32[]{:S(2)}, u32[]{:S(2)}) collective-permute-start(bf16[64,1024]{1,0:T(8,128)(2,1)S(1)} %get-tuple-element.123), channel_id=1, source_target_pairs={{0,0},{1,16},{2,32},{3,48},{4,64},{5,80},{6,96},{7,112},{8,1},{9,1... | collective-permute-start | bytes 393224 | tf_op jit(solution)/shard_map/ppermute | solution.py:389
  171.0 9.0 %collective-permute-start.27 = (bf16[1024,256]{1,0:T(8,128)(2,1)}, bf16[1024,256]{1,0:T(8,128)(2,1)}, u32[]{:S(2)}, u32[]{:S(2)}) collective-permute-start(bf16[1024,256]{1,0:T(8,128)(2,1)} %add_convert_fusion.2), channel_id=1, source_target_pairs={{0,16},{1,49},{16,32},{17,1},{32,48},{33,17},{48,0},{49,33},{2,18}... | collective-permute-start | bytes 1572872 | tf_op jit(solution)/shard_map/ppermute | solution.py:36
  180.9 3.6 %collective-permute-start.20 = (bf16[1024,256]{1,0:T(8,128)(2,1)}, bf16[1024,256]{1,0:T(8,128)(2,1)}, u32[]{:S(2)}, u32[]{:S(2)}) collective-permute-start(bf16[1024,256]{1,0:T(8,128)(2,1)} %add_convert_fusion.7), channel_id=1, source_target_pairs={{0,16},{1,49},{16,32},{17,1},{32,48},{33,17},{48,0},{49,33},{2,18}... | collective-permute-start | bytes 1572872 | tf_op jit(solution)/shard_map/ppermute | solution.py:36
  188.1 5.6 %all-to-all-start.1 = ((bf16[16,64,1024]{2,1,0:T(8,128)(2,1)}), bf16[16,64,1024]{2,1,0:T(8,128)(2,1)}, u32[]{:S(2)}, u32[]{:S(2)}) async-start(bf16[16,64,1024]{2,1,0:T(8,128)(2,1)} %broadcast_in_dim.88), calls=%async_computation.1 | async-start | bytes 4194304 | tf_op jit(solution)/shard_map/all_to_all | solution.py:397
  193.8 2.5 collective-permute-start.38
  201.0 2.2 collective-permute-done.24
  203.2 5.2 %collective-permute-start.21 = (bf16[1024,256]{1,0:T(8,128)(2,1)S(1)}, bf16[1024,256]{1,0:T(8,128)(2,1)S(1)}, u32[]{:S(2)}, u32[]{:S(2)}) collective-permute-start(bf16[1024,256]{1,0:T(8,128)(2,1)S(1)} %add_convert_fusion.6), channel_id=1, source_target_pairs={{0,16},{1,49},{16,32},{17,1},{32,48},{33,17},{48,0},{49,33},{2,18}... | collective-permute-start | bytes 1572872 | tf_op jit(solution)/shard_map/ppermute | solution.py:36
  210.7 2.8 %collective-permute-start.25 = (bf16[1024,256]{1,0:T(8,128)(2,1)S(1)}, bf16[1024,256]{1,0:T(8,128)(2,1)S(1)}, u32[]{:S(2)}, u32[]{:S(2)}) collective-permute-start(bf16[1024,256]{1,0:T(8,128)(2,1)S(1)} %add_convert_fusion.4), channel_id=1, source_target_pairs={{0,16},{1,49},{16,32},{17,1},{32,48},{33,17},{48,0},{49,33},{2,18}... | collective-permute-start | bytes 1572872 | tf_op jit(solution)/shard_map/ppermute | solution.py:36
  213.8 2.5 collective-permute-done.18
  216.4 3.4 %collective-permute-start.19 = (bf16[1024,256]{1,0:T(8,128)(2,1)S(1)}, bf16[1024,256]{1,0:T(8,128)(2,1)S(1)}, u32[]{:S(2)}, u32[]{:S(2)}) collective-permute-start(bf16[1024,256]{1,0:T(8,128)(2,1)S(1)} %add_convert_fusion.8), channel_id=1, source_target_pairs={{0,16},{1,49},{16,32},{17,1},{32,48},{33,17},{48,0},{49,33},{2,18}... | collective-permute-start | bytes 1572872 | tf_op jit(solution)/shard_map/ppermute | solution.py:36
  219.9 2.0 collective-permute-done.21
  223.3 4.2 %collective-permute-done.25 = bf16[1024,256]{1,0:T(8,128)(2,1)S(1)} collective-permute-done((bf16[1024,256]{1,0:T(8,128)(2,1)S(1)}, bf16[1024,256]{1,0:T(8,128)(2,1)S(1)}, u32[]{:S(2)}, u32[]{:S(2)}) %collective-permute-start.25) | collective-permute-done | bytes 524320 | tf_op jit(solution)/shard_map/ppermute | solution.py:36
  227.7 3.4 %collective-permute-start.26 = (bf16[1024,256]{1,0:T(8,128)(2,1)S(1)}, bf16[1024,256]{1,0:T(8,128)(2,1)S(1)}, u32[]{:S(2)}, u32[]{:S(2)}) collective-permute-start(bf16[1024,256]{1,0:T(8,128)(2,1)S(1)} %add_convert_fusion.3), channel_id=1, source_target_pairs={{0,16},{1,49},{16,32},{17,1},{32,48},{33,17},{48,0},{49,33},{2,18}... | collective-permute-start | bytes 1572872 | tf_op jit(solution)/shard_map/ppermute | solution.py:36
  231.1 2.0 collective-permute-done.28
  235.7 3.0 %collective-permute-done.19 = bf16[1024,256]{1,0:T(8,128)(2,1)S(1)} collective-permute-done((bf16[1024,256]{1,0:T(8,128)(2,1)S(1)}, bf16[1024,256]{1,0:T(8,128)(2,1)S(1)}, u32[]{:S(2)}, u32[]{:S(2)}) %collective-permute-start.19) | collective-permute-done | bytes 524320 | tf_op jit(solution)/shard_map/ppermute | solution.py:36
  238.9 5.4 %collective-permute-done.26 = bf16[1024,256]{1,0:T(8,128)(2,1)S(1)} collective-permute-done((bf16[1024,256]{1,0:T(8,128)(2,1)S(1)}, bf16[1024,256]{1,0:T(8,128)(2,1)S(1)}, u32[]{:S(2)}, u32[]{:S(2)}) %collective-permute-start.26) | collective-permute-done | bytes 524320 | tf_op jit(solution)/shard_map/ppermute | solution.py:36
  244.4 3.7 %collective-permute-done.29 = bf16[1024,256]{1,0:T(8,128)(2,1)S(1)} collective-permute-done((bf16[1024,256]{1,0:T(8,128)(2,1)S(1)}, bf16[1024,256]{1,0:T(8,128)(2,1)S(1)}, u32[]{:S(2)}, u32[]{:S(2)}) %collective-permute-start.29) | collective-permute-done | bytes 524320 | tf_op jit(solution)/shard_map/ppermute | solution.py:26
  249.2 3.3 %broadcast_select_fusion.1 = (bf16[16,64,1024]{2,1,0:T(8,128)(2,1)}, bf16[16,64,1024]{2,1,0:T(8,128)(2,1)S(1)}) fusion(bf16[16,64,1024]{2,1,0:T(8,128)(2,1)} %all-to-all-done.1, pred[]{:T(512)} %bitcast.24, pred[16]{0:T(512)(128)(4,1)S(1)} %broadcast_in_dim.85), kind=kLoop, calls=%fused_computation.5 | loop fusion | flops 2097152 | bytes 6291473 | tf_op jit(solution)/shard_map/jit(_where)/select_n | solution.py:409
  (143 shorter events, 48.0 us)
Async XLA Ops:
  7.3 37.3 %collective-permute-start.2 = (bf16[384,2048]{1,0:T(8,128)(2,1)}, bf16[384,2048]{1,0:T(8,128)(2,1)}, u32[]{:S(2)}, u32[]{:S(2)}) collective-permute-start(bf16[384,2048]{1,0:T(8,128)(2,1)} %shard_map.86.refs_0_), channel_id=1, source_target_pairs={{0,2},{2,0},{1,3},{3,1},{4,6},{6,4},{5,7},{7,5},{8,10},{10,8},{9,1... | collective-permute-start | bytes 4718600 | tf_op jit(solution)/shard_map/ppermute | solution.py:26
  9.2 37.3 %collective-permute-start.1 = (bf16[384,2048]{1,0:T(8,128)(2,1)}, bf16[384,2048]{1,0:T(8,128)(2,1)}, u32[]{:S(2)}, u32[]{:S(2)}) collective-permute-start(bf16[384,2048]{1,0:T(8,128)(2,1)} %shard_map.86.refs_0_), channel_id=1, source_target_pairs={{0,12},{1,5},{4,0},{5,9},{8,4},{9,13},{12,8},{13,1},{2,14},{3,7},{... | collective-permute-start | bytes 4718600 | tf_op jit(solution)/shard_map/ppermute | solution.py:36
  9.8 36.7 %collective-permute-start = (bf16[384,2048]{1,0:T(8,128)(2,1)}, bf16[384,2048]{1,0:T(8,128)(2,1)}, u32[]{:S(2)}, u32[]{:S(2)}) collective-permute-start(bf16[384,2048]{1,0:T(8,128)(2,1)} %shard_map.86.refs_0_), channel_id=1, source_target_pairs={{0,4},{1,13},{4,8},{5,1},{8,12},{9,5},{12,0},{13,9},{2,6},{3,15},{... | collective-permute-start | bytes 4718600 | tf_op jit(solution)/shard_map/ppermute | solution.py:36
  46.7 36.6 %collective-permute-start.6 = (bf16[384,2048]{1,0:T(8,128)(2,1)}, bf16[384,2048]{1,0:T(8,128)(2,1)}, u32[]{:S(2)}, u32[]{:S(2)}) collective-permute-start(bf16[384,2048]{1,0:T(8,128)(2,1)} %collective-permute-done.2.refs_3_), channel_id=1, source_target_pairs={{0,12},{1,5},{4,0},{5,9},{8,4},{9,13},{12,8},{13,1},{2,14},{3,7},{... | collective-permute-start | bytes 4718600 | tf_op jit(solution)/shard_map/ppermute | solution.py:36
  47.8 35.4 %collective-permute-start.8 = (bf16[384,2048]{1,0:T(8,128)(2,1)}, bf16[384,2048]{1,0:T(8,128)(2,1)}, u32[]{:S(2)}, u32[]{:S(2)}) collective-permute-start(bf16[384,2048]{1,0:T(8,128)(2,1)} %collective-permute-done.refs_1_), channel_id=1, source_target_pairs={{0,1},{1,0},{2,3},{3,2},{4,5},{5,4},{6,7},{7,6},{8,9},{9,8},{10,11... | collective-permute-start | bytes 4718600 | tf_op jit(solution)/shard_map/ppermute | solution.py:26
  48.5 36.6 %collective-permute-start.7 = (bf16[384,2048]{1,0:T(8,128)(2,1)}, bf16[384,2048]{1,0:T(8,128)(2,1)}, u32[]{:S(2)}, u32[]{:S(2)}) collective-permute-start(bf16[384,2048]{1,0:T(8,128)(2,1)} %collective-permute-done.refs_1_), channel_id=1, source_target_pairs={{0,2},{2,0},{1,3},{3,1},{4,6},{6,4},{5,7},{7,5},{8,10},{10,8},{9,1... | collective-permute-start | bytes 4718600 | tf_op jit(solution)/shard_map/ppermute | solution.py:26
  48.5 36.6 %collective-permute-start.5 = (bf16[384,2048]{1,0:T(8,128)(2,1)}, bf16[384,2048]{1,0:T(8,128)(2,1)}, u32[]{:S(2)}, u32[]{:S(2)}) collective-permute-start(bf16[384,2048]{1,0:T(8,128)(2,1)} %collective-permute-done.refs_1_), channel_id=1, source_target_pairs={{0,4},{1,13},{4,8},{5,1},{8,12},{9,5},{12,0},{13,9},{2,6},{3,15},{... | collective-permute-start | bytes 4718600 | tf_op jit(solution)/shard_map/ppermute | solution.py:36
  85.1 21.5 %collective-permute-start.10 = (bf16[384,2048]{1,0:T(8,128)(2,1)}, bf16[384,2048]{1,0:T(8,128)(2,1)}, u32[]{:S(2)}, u32[]{:S(2)}) collective-permute-start(bf16[384,2048]{1,0:T(8,128)(2,1)} %collective-permute-done.7.refs_6_), channel_id=1, source_target_pairs={{0,4},{1,13},{4,8},{5,1},{8,12},{9,5},{12,0},{13,9},{2,6},{3,15},{... | collective-permute-start | bytes 4718600 | tf_op jit(solution)/shard_map/ppermute | solution.py:36
  87.0 20.7 %collective-permute-start.11 = (bf16[384,2048]{1,0:T(8,128)(2,1)}, bf16[384,2048]{1,0:T(8,128)(2,1)}, u32[]{:S(2)}, u32[]{:S(2)}) collective-permute-start(bf16[384,2048]{1,0:T(8,128)(2,1)} %collective-permute-done.2.refs_3_), channel_id=1, source_target_pairs={{0,1},{1,0},{2,3},{3,2},{4,5},{5,4},{6,7},{7,6},{8,9},{9,8},{10,11... | collective-permute-start | bytes 4718600 | tf_op jit(solution)/shard_map/ppermute | solution.py:26
  87.3 20.4 %collective-permute-start.14 = (bf16[384,2048]{1,0:T(8,128)(2,1)}, bf16[384,2048]{1,0:T(8,128)(2,1)}, u32[]{:S(2)}, u32[]{:S(2)}) collective-permute-start(bf16[384,2048]{1,0:T(8,128)(2,1)} %collective-permute-done.7.refs_6_), channel_id=1, source_target_pairs={{0,1},{1,0},{2,3},{3,2},{4,5},{5,4},{6,7},{7,6},{8,9},{9,8},{10,11... | collective-permute-start | bytes 4718600 | tf_op jit(solution)/shard_map/ppermute | solution.py:26
  87.5 20.2 %collective-permute-start.12 = (bf16[384,2048]{1,0:T(8,128)(2,1)}, bf16[384,2048]{1,0:T(8,128)(2,1)}, u32[]{:S(2)}, u32[]{:S(2)}) collective-permute-start(bf16[384,2048]{1,0:T(8,128)(2,1)} %collective-permute-done.5.refs_4_), channel_id=1, source_target_pairs={{0,1},{1,0},{2,3},{3,2},{4,5},{5,4},{6,7},{7,6},{8,9},{9,8},{10,11... | collective-permute-start | bytes 4718600 | tf_op jit(solution)/shard_map/ppermute | solution.py:26
  87.8 19.9 %collective-permute-start.13 = (bf16[384,2048]{1,0:T(8,128)(2,1)}, bf16[384,2048]{1,0:T(8,128)(2,1)}, u32[]{:S(2)}, u32[]{:S(2)}) collective-permute-start(bf16[384,2048]{1,0:T(8,128)(2,1)} %collective-permute-done.6.refs_5_), channel_id=1, source_target_pairs={{0,1},{1,0},{2,3},{3,2},{4,5},{5,4},{6,7},{7,6},{8,9},{9,8},{10,11... | collective-permute-start | bytes 4718600 | tf_op jit(solution)/shard_map/ppermute | solution.py:26
  117.0 35.6 %all-to-all-start = ((bf16[8,64,1024]{2,1,0:T(8,128)(2,1)}), bf16[8,64,1024]{2,1,0:T(8,128)(2,1)S(1)}, u32[]{:S(2)}, u32[]{:S(2)}) async-start(bf16[8,64,1024]{2,1,0:T(8,128)(2,1)} %bitcast.57), calls=%async_computation | async-start | bytes 2097152 | tf_op jit(solution)/shard_map/all_to_all | solution.py:354
  125.1 26.5 %collective-permute-start.30 = (bf16[2,64,1024]{2,1,0:T(8,128)(2,1)}, bf16[2,64,1024]{2,1,0:T(8,128)(2,1)S(1)}, u32[]{:S(2)}, u32[]{:S(2)}) collective-permute-start(bf16[2,64,1024]{2,1,0:T(8,128)(2,1)} %get-tuple-element.118), channel_id=1, source_target_pairs={{0,4},{4,8},{8,12},{12,0},{1,5},{5,9},{9,13},{13,1},{2,6},{6,10},{... | collective-permute-start | bytes 786440 | tf_op jit(solution)/shard_map/ppermute | solution.py:26
  126.1 25.5 %collective-permute-start.31 = (bf16[2,64,1024]{2,1,0:T(8,128)(2,1)}, bf16[2,64,1024]{2,1,0:T(8,128)(2,1)}, u32[]{:S(2)}, u32[]{:S(2)}) collective-permute-start(bf16[2,64,1024]{2,1,0:T(8,128)(2,1)} %get-tuple-element.120), channel_id=1, source_target_pairs={{0,12},{4,0},{8,4},{12,8},{1,13},{5,1},{9,5},{13,9},{2,14},{6,2},{... | collective-permute-start | bytes 786440 | tf_op jit(solution)/shard_map/ppermute | solution.py:26
  128.6 23.0 %collective-permute-start.32 = (bf16[2,64,1024]{2,1,0:T(8,128)(2,1)S(1)}, bf16[2,64,1024]{2,1,0:T(8,128)(2,1)}, u32[]{:S(2)}, u32[]{:S(2)}) collective-permute-start(bf16[2,64,1024]{2,1,0:T(8,128)(2,1)S(1)} %get-tuple-element.122), channel_id=1, source_target_pairs={{0,8},{4,12},{8,0},{12,4},{1,9},{5,13},{9,1},{13,5},{2,10},{6,14},... | collective-permute-start | bytes 786440 | tf_op jit(solution)/shard_map/ppermute | solution.py:26
  154.5 15.5 %collective-permute-start.23 = (bf16[1024,256]{1,0:T(8,128)(2,1)}, bf16[1024,256]{1,0:T(8,128)(2,1)S(1)}, u32[]{:S(2)}, u32[]{:S(2)}) collective-permute-start(bf16[1024,256]{1,0:T(8,128)(2,1)} %get-tuple-element.109), channel_id=1, source_target_pairs={{0,16},{1,49},{16,32},{17,1},{32,48},{33,17},{48,0},{49,33},{2,18}... | collective-permute-start | bytes 1572872 | tf_op jit(solution)/shard_map/ppermute | solution.py:36
  162.8 17.2 %collective-permute-start.34 = (bf16[64,1024]{1,0:T(8,128)(2,1)S(1)}, bf16[64,1024]{1,0:T(8,128)(2,1)S(1)}, u32[]{:S(2)}, u32[]{:S(2)}) collective-permute-start(bf16[64,1024]{1,0:T(8,128)(2,1)S(1)} %get-tuple-element.123), channel_id=1, source_target_pairs={{0,0},{1,16},{2,32},{3,48},{4,64},{5,80},{6,96},{7,112},{8,1},{9,1... | collective-permute-start | bytes 393224 | tf_op jit(solution)/shard_map/ppermute | solution.py:389
  170.0 27.6 %collective-permute-start.17 = (bf16[1024,256]{1,0:T(8,128)(2,1)}, bf16[1024,256]{1,0:T(8,128)(2,1)S(1)}, u32[]{:S(2)}, u32[]{:S(2)}) collective-permute-start(bf16[1024,256]{1,0:T(8,128)(2,1)} %get-tuple-element.101), channel_id=1, source_target_pairs={{0,16},{1,49},{16,32},{17,1},{32,48},{33,17},{48,0},{49,33},{2,18}... | collective-permute-start | bytes 1572872 | tf_op jit(solution)/shard_map/ppermute | solution.py:36
  171.0 22.8 %collective-permute-start.27 = (bf16[1024,256]{1,0:T(8,128)(2,1)}, bf16[1024,256]{1,0:T(8,128)(2,1)}, u32[]{:S(2)}, u32[]{:S(2)}) collective-permute-start(bf16[1024,256]{1,0:T(8,128)(2,1)} %add_convert_fusion.2), channel_id=1, source_target_pairs={{0,16},{1,49},{16,32},{17,1},{32,48},{33,17},{48,0},{49,33},{2,18}... | collective-permute-start | bytes 1572872 | tf_op jit(solution)/shard_map/ppermute | solution.py:36
  180.9 18.4 %collective-permute-start.20 = (bf16[1024,256]{1,0:T(8,128)(2,1)}, bf16[1024,256]{1,0:T(8,128)(2,1)}, u32[]{:S(2)}, u32[]{:S(2)}) collective-permute-start(bf16[1024,256]{1,0:T(8,128)(2,1)} %add_convert_fusion.7), channel_id=1, source_target_pairs={{0,16},{1,49},{16,32},{17,1},{32,48},{33,17},{48,0},{49,33},{2,18}... | collective-permute-start | bytes 1572872 | tf_op jit(solution)/shard_map/ppermute | solution.py:36
  184.5 18.7 %collective-permute-start.24 = (bf16[1024,256]{1,0:T(8,128)(2,1)}, bf16[1024,256]{1,0:T(8,128)(2,1)}, u32[]{:S(2)}, u32[]{:S(2)}) collective-permute-start(bf16[1024,256]{1,0:T(8,128)(2,1)} %get-tuple-element.110), channel_id=1, source_target_pairs={{0,16},{1,49},{16,32},{17,1},{32,48},{33,17},{48,0},{49,33},{2,18}... | collective-permute-start | bytes 1572872 | tf_op jit(solution)/shard_map/ppermute | solution.py:36
  188.1 61.1 %all-to-all-start.1 = ((bf16[16,64,1024]{2,1,0:T(8,128)(2,1)}), bf16[16,64,1024]{2,1,0:T(8,128)(2,1)}, u32[]{:S(2)}, u32[]{:S(2)}) async-start(bf16[16,64,1024]{2,1,0:T(8,128)(2,1)} %broadcast_in_dim.88), calls=%async_computation.1 | async-start | bytes 4194304 | tf_op jit(solution)/shard_map/all_to_all | solution.py:397
  193.8 19.9 %collective-permute-start.38 = (bf16[2,64,1024]{2,1,0:T(8,128)(2,1)S(1)}, bf16[2,64,1024]{2,1,0:T(8,128)(2,1)S(1)}, u32[]{:S(2)}, u32[]{:S(2)}) collective-permute-start(bf16[2,64,1024]{2,1,0:T(8,128)(2,1)S(1)} %pad_maximum_fusion), channel_id=1, source_target_pairs={{0,16},{16,32},{32,48},{48,0},{1,17},{17,33},{33,49},{49,1},{2,18}... | collective-permute-start | bytes 786440 | tf_op jit(solution)/shard_map/ppermute | solution.py:26
  196.3 17.3 %collective-permute-start.37 = (bf16[2,64,1024]{2,1,0:T(8,128)(2,1)S(1)}, bf16[2,64,1024]{2,1,0:T(8,128)(2,1)S(1)}, u32[]{:S(2)}, u32[]{:S(2)}) collective-permute-start(bf16[2,64,1024]{2,1,0:T(8,128)(2,1)S(1)} %pad_maximum_fusion), channel_id=1, source_target_pairs={{0,32},{16,48},{32,0},{48,16},{1,33},{17,49},{33,1},{49,17},{2,34}... | collective-permute-start | bytes 786440 | tf_op jit(solution)/shard_map/ppermute | solution.py:26
  199.3 17.0 %collective-permute-start.18 = (bf16[1024,256]{1,0:T(8,128)(2,1)S(1)}, bf16[1024,256]{1,0:T(8,128)(2,1)S(1)}, u32[]{:S(2)}, u32[]{:S(2)}) collective-permute-start(bf16[1024,256]{1,0:T(8,128)(2,1)S(1)} %add_convert_fusion.9), channel_id=1, source_target_pairs={{0,16},{1,49},{16,32},{17,1},{32,48},{33,17},{48,0},{49,33},{2,18}... | collective-permute-start | bytes 1572872 | tf_op jit(solution)/shard_map/ppermute | solution.py:36
  203.2 18.7 %collective-permute-start.21 = (bf16[1024,256]{1,0:T(8,128)(2,1)S(1)}, bf16[1024,256]{1,0:T(8,128)(2,1)S(1)}, u32[]{:S(2)}, u32[]{:S(2)}) collective-permute-start(bf16[1024,256]{1,0:T(8,128)(2,1)S(1)} %add_convert_fusion.6), channel_id=1, source_target_pairs={{0,16},{1,49},{16,32},{17,1},{32,48},{33,17},{48,0},{49,33},{2,18}... | collective-permute-start | bytes 1572872 | tf_op jit(solution)/shard_map/ppermute | solution.py:36
  210.7 16.8 %collective-permute-start.25 = (bf16[1024,256]{1,0:T(8,128)(2,1)S(1)}, bf16[1024,256]{1,0:T(8,128)(2,1)S(1)}, u32[]{:S(2)}, u32[]{:S(2)}) collective-permute-start(bf16[1024,256]{1,0:T(8,128)(2,1)S(1)} %add_convert_fusion.4), channel_id=1, source_target_pairs={{0,16},{1,49},{16,32},{17,1},{32,48},{33,17},{48,0},{49,33},{2,18}... | collective-permute-start | bytes 1572872 | tf_op jit(solution)/shard_map/ppermute | solution.py:36
  213.5 19.6 %collective-permute-start.28 = (bf16[1024,256]{1,0:T(8,128)(2,1)S(1)}, bf16[1024,256]{1,0:T(8,128)(2,1)S(1)}, u32[]{:S(2)}, u32[]{:S(2)}) collective-permute-start(bf16[1024,256]{1,0:T(8,128)(2,1)S(1)} %add_convert_fusion.1), channel_id=1, source_target_pairs={{0,16},{1,49},{16,32},{17,1},{32,48},{33,17},{48,0},{49,33},{2,18}... | collective-permute-start | bytes 1572872 | tf_op jit(solution)/shard_map/ppermute | solution.py:36
  216.4 22.3 %collective-permute-start.19 = (bf16[1024,256]{1,0:T(8,128)(2,1)S(1)}, bf16[1024,256]{1,0:T(8,128)(2,1)S(1)}, u32[]{:S(2)}, u32[]{:S(2)}) collective-permute-start(bf16[1024,256]{1,0:T(8,128)(2,1)S(1)} %add_convert_fusion.8), channel_id=1, source_target_pairs={{0,16},{1,49},{16,32},{17,1},{32,48},{33,17},{48,0},{49,33},{2,18}... | collective-permute-start | bytes 1572872 | tf_op jit(solution)/shard_map/ppermute | solution.py:36
  222.0 16.7 %collective-permute-start.22 = (bf16[1024,256]{1,0:T(8,128)(2,1)S(1)}, bf16[1024,256]{1,0:T(8,128)(2,1)S(1)}, u32[]{:S(2)}, u32[]{:S(2)}) collective-permute-start(bf16[1024,256]{1,0:T(8,128)(2,1)S(1)} %add_convert_fusion.5), channel_id=1, source_target_pairs={{0,64},{64,0},{1,65},{65,1},{2,66},{66,2},{3,67},{67,3},{4,68},{68... | collective-permute-start | bytes 1572872 | tf_op jit(solution)/shard_map/ppermute | solution.py:26
  227.7 16.7 %collective-permute-start.26 = (bf16[1024,256]{1,0:T(8,128)(2,1)S(1)}, bf16[1024,256]{1,0:T(8,128)(2,1)S(1)}, u32[]{:S(2)}, u32[]{:S(2)}) collective-permute-start(bf16[1024,256]{1,0:T(8,128)(2,1)S(1)} %add_convert_fusion.3), channel_id=1, source_target_pairs={{0,16},{1,49},{16,32},{17,1},{32,48},{33,17},{48,0},{49,33},{2,18}... | collective-permute-start | bytes 1572872 | tf_op jit(solution)/shard_map/ppermute | solution.py:36
  (28 other events, 442.8 us)

commit v6 on v5

--- a/solution.py
+++ b/solution.py
@@ -389,7 +389,7 @@
     moved = lax.ppermute(masked, AXES, pairs)
     both = ordered_pair(h, moved, shift(moved, "h", 1))
     share = after(share, both)
-    both = after(both, rings[1].marks[1])
+    both = after(both, rings[1].marks[2])
     ring = ordered_ring(y, [both, shift(both, "y", -1), shift(both, "y", 2), shift(both, "y", 1)])
     column_factor = ring.transpose(1, 0, 2, 3).reshape(512, 1024)
 

time: 259 us -> 265 us (1.023)
  Pallas kernels: 36.5 us -> 44.1 us
  starting transfers between devices: 77.6 us -> 72.7 us
  waiting for transfers between devices: 113 us -> 116 us
    ppermute x17, waiting for transfers between devices: 74.6 us -> 62.7 us  [mirrored(): return lax.ppermute(array, (axis, 'c'), pairs)]
    ppermute x17, starting transfers between devices: 40.7 us -> 29.8 us  [mirrored(): return lax.ppermute(array, (axis, 'c'), pairs)]
    ppermute x21, waiting for transfers between devices: 38.1 us -> 47.7 us  [shift(): lax.ppermute(array, axis, [(i, (i + step) % size) for i in range(size)])]
    pallas_call x1, Pallas kernels: 2.15 us -> 9.91 us  [front_pick(): pl.pallas_call(front_kernel, out_shape=[jax.ShapeDtypeStruct((8, 64, 1024...]
    ppermute x21, starting transfers between devices: 16 us -> 21.4 us  [shift(): lax.ppermute(array, axis, [(i, (i + step) % size) for i in range(size)])]
    ppermute x1, waiting for transfers between devices: 0.01 us -> 5.19 us  [local(): moved = lax.ppermute(masked, AXES, pairs)]
  transfers between devices with their start and end apart: 41 -> 41, of which waited for: 17 -> 19; matrix products, arithmetic and copies ran while one was open for 8% -> 8% of each run, Pallas kernels for 9% -> 12%
where the time goes in v6:
time: 265 us; the launch traced here: 263 us
  waiting for transfers between devices  116 us (44%)
  starting transfers between devices  72.7 us (27%)
  Pallas kernels  44.1 us (17%)
  other arithmetic  21 us (8%)
  local copies, waits for them, and re-layouts  5.38 us (2%)
    ppermute x17, waiting for transfers between devices, mirrored(): return lax.ppermute(array, (axis, 'c'), pairs)  62.7 us
    ppermute x21, waiting for transfers between devices, shift(): lax.ppermute(array, axis, [(i, (i + step) % size) for i in range(size)])  47.7 us
    ppermute x17, starting transfers between devices, mirrored(): return lax.ppermute(array, (axis, 'c'), pairs)  29.8 us
    ppermute x21, starting transfers between devices, shift(): lax.ppermute(array, axis, [(i, (i + step) % size) for i in range(size)])  21.4 us
    pallas_call x1, Pallas kernels, main_parts(): pl.pallas_call(functools.partial(main_kernel, [p[1:] for p in pieces]), o...  21.4 us
    pallas_call x1, Pallas kernels, front_pick(): pl.pallas_call(front_kernel, out_shape=[jax.ShapeDtypeStruct((8, 64, 1024...  9.91 us
    all_to_all x1, starting transfers between devices, local(): lax.all_to_all(pan.reshape(8, 64, 1024), ('h', 'y'), split_axis=0, concat...  8.01 us
    all_to_all x1, starting transfers between devices, local(): lax.all_to_all(copies, ('x', 'z', 'c'), split_axis=0, concat_axis=0, tile...  7.6 us
  transfers between devices with their start and end apart: 41, of which 19 were waited for; matrix products, arithmetic and copies ran while one was open for 8% of the time, Pallas kernels for 12%

profile of v6, /device:TPU:18, one launch (start us, length us, event | category | flops | bytes accessed | tf_op | source)
XLA Modules:
  0.0 262.6 jit_solution(10307550843862979567)
XLA Ops:
  0.7 6.5 %shard_map.86.refs_0_ = bf16[384,2048]{1,0:T(8,128)(2,1)} custom-call(bf16[1,384,2048]{2,1,0:T(8,128)(2,1)} %panel.1, bf16[1,2048,2048]{2,1,0:T(8,128)(2,1)} %inverse.1), custom_call_target="tpu_custom_call" | custom-call | flops 2000000000 | bytes 8000000 | tf_op jit(solution)/shard_map/pallas_call | solution.py:66
  11.9 9.9 %shard_map.87 = (bf16[8,64,1024]{2,1,0:T(8,128)(2,1)}, bf16[8,64,1024]{2,1,0:T(8,128)(2,1)}) custom-call(s32[8]{0:T(128)} %pivots.1, s32[2]{0:T(128)} %pad_add_fusion.place, bf16[8,2,64,512]{3,2,1,0:T(8,128)(2,1)} %bitcast.56), custom_call_target="tpu_custom_call" | custom-call | tf_op jit(solution)/shard_map/pallas_call | solution.py:306
  28.7 15.8 %collective-permute-done.2.refs_3_ = bf16[384,2048]{1,0:T(8,128)(2,1)} collective-permute-done((bf16[384,2048]{1,0:T(8,128)(2,1)}, bf16[384,2048]{1,0:T(8,128)(2,1)}, u32[]{:S(2)}, u32[]{:S(2)}) %collective-permute-start.2) | collective-permute-done | bytes 1572896 | tf_op jit(solution)/shard_map/ppermute | solution.py:26
  48.5 2.1 collective-permute-start.5
  50.6 32.6 %collective-permute-done.6.refs_5_ = bf16[384,2048]{1,0:T(8,128)(2,1)} collective-permute-done((bf16[384,2048]{1,0:T(8,128)(2,1)}, bf16[384,2048]{1,0:T(8,128)(2,1)}, u32[]{:S(2)}, u32[]{:S(2)}) %collective-permute-start.6) | collective-permute-done | bytes 1572896 | tf_op jit(solution)/shard_map/ppermute | solution.py:36
  88.0 18.6 %collective-permute-done.10.refs_7_ = bf16[384,2048]{1,0:T(8,128)(2,1)} collective-permute-done((bf16[384,2048]{1,0:T(8,128)(2,1)}, bf16[384,2048]{1,0:T(8,128)(2,1)}, u32[]{:S(2)}, u32[]{:S(2)}) %collective-permute-start.10) | collective-permute-done | bytes 1572896 | tf_op jit(solution)/shard_map/ppermute | solution.py:36
  107.7 2.6 %collective-permute-done.15.refs_15_ = bf16[384,2048]{1,0:T(8,128)(2,1)} collective-permute-done((bf16[384,2048]{1,0:T(8,128)(2,1)}, bf16[384,2048]{1,0:T(8,128)(2,1)}, u32[]{:S(2)}, u32[]{:S(2)}) %collective-permute-start.15) | collective-permute-done | bytes 1572896 | tf_op jit(solution)/shard_map/ppermute | solution.py:26
  110.3 6.4 %shard_map.88 = bf16[512,1024]{1,0:T(8,128)(2,1)} custom-call(s32[8]{0:T(128)} %get-tuple-element.66.pan_rows, s32[8]{0:T(128)} %get-tuple-element.67.pan_cols, s32[1]{0:T(128)} %bitcast.3.offset, bf16[384,2048]{1,0:T(8,128)(2,1)} %shard_map.86.refs_0_, bf16[384,2048]{1,0:T(8,128)(2,1)} %collective-permute-done.refs_1_, ...), custom_call_target="tpu_custom_call" | custom-call | flops 2200000000 | bytes 8000000 | tf_op jit(solution)/shard_map/pallas_call | solution.py:236
  116.7 8.0 %all-to-all-start = ((bf16[8,64,1024]{2,1,0:T(8,128)(2,1)}), bf16[8,64,1024]{2,1,0:T(8,128)(2,1)S(1)}, u32[]{:S(2)}, u32[]{:S(2)}) async-start(bf16[8,64,1024]{2,1,0:T(8,128)(2,1)} %bitcast.57), calls=%async_computation | async-start | bytes 2097152 | tf_op jit(solution)/shard_map/all_to_all | solution.py:354
  125.9 2.6 collective-permute-start.31
  130.2 21.4 %shard_map.89 = (bf16[1024,256]{1,0:T(8,128)(2,1)}, bf16[1024,256]{1,0:T(8,128)(2,1)}, bf16[1024,256]{1,0:T(8,128)(2,1)}, bf16[1024,256]{1,0:T(8,128)(2,1)}, bf1...) custom-call(s32[48]{0:T(128)} %select_reduce_fusion.dest, ...), custom_call_target="tpu_custom_call" | custom-call | flops 20000000000 | bytes 36000000 | tf_op jit(solution)/shard_map/pallas_call | solution.py:187
  152.8 2.5 collective-permute-start.16
  156.8 3.5 %collective-permute-done.33 = bf16[64,1024]{1,0:T(8,128)(2,1)S(1)} collective-permute-done((bf16[64,1024]{1,0:T(8,128)(2,1)S(1)}, bf16[64,1024]{1,0:T(8,128)(2,1)S(1)}, u32[]{:S(2)}, u32[]{:S(2)}) %collective-permute-start.33) | collective-permute-done | bytes 131104 | tf_op jit(solution)/shard_map/ppermute | solution.py:26
  162.4 6.0 %collective-permute-start.34 = (bf16[64,1024]{1,0:T(8,128)(2,1)S(1)}, bf16[64,1024]{1,0:T(8,128)(2,1)S(1)}, u32[]{:S(2)}, u32[]{:S(2)}) collective-permute-start(bf16[64,1024]{1,0:T(8,128)(2,1)S(1)} %get-tuple-element.123), channel_id=1, source_target_pairs={{0,0},{1,16},{2,32},{3,48},{4,64},{5,80},{6,96},{7,112},{8,1},{9,1... | collective-permute-start | bytes 393224 | tf_op jit(solution)/shard_map/ppermute | solution.py:389
  169.6 2.4 collective-permute-start.20
  172.2 5.2 %collective-permute-done.34 = bf16[64,1024]{1,0:T(8,128)(2,1)S(1)} collective-permute-done((bf16[64,1024]{1,0:T(8,128)(2,1)S(1)}, bf16[64,1024]{1,0:T(8,128)(2,1)S(1)}, u32[]{:S(2)}, u32[]{:S(2)}) %collective-permute-start.34) | collective-permute-done | bytes 131104 | tf_op jit(solution)/shard_map/ppermute | solution.py:389
  178.4 2.8 %collective-permute-start.27 = (bf16[1024,256]{1,0:T(8,128)(2,1)}, bf16[1024,256]{1,0:T(8,128)(2,1)}, u32[]{:S(2)}, u32[]{:S(2)}) collective-permute-start(bf16[1024,256]{1,0:T(8,128)(2,1)} %add_convert_fusion.2), channel_id=1, source_target_pairs={{0,16},{1,49},{16,32},{17,1},{32,48},{33,17},{48,0},{49,33},{2,18}... | collective-permute-start | bytes 1572872 | tf_op jit(solution)/shard_map/ppermute | solution.py:36
  181.1 3.0 %collective-permute-done.35 = bf16[64,1024]{1,0:T(8,128)(2,1)S(1)} collective-permute-done((bf16[64,1024]{1,0:T(8,128)(2,1)S(1)}, bf16[64,1024]{1,0:T(8,128)(2,1)S(1)}, u32[]{:S(2)}, u32[]{:S(2)}) %collective-permute-start.35) | collective-permute-done | bytes 131104 | tf_op jit(solution)/shard_map/ppermute | solution.py:26
  185.8 7.6 %all-to-all-start.1 = ((bf16[16,64,1024]{2,1,0:T(8,128)(2,1)}), bf16[16,64,1024]{2,1,0:T(8,128)(2,1)}, u32[]{:S(2)}, u32[]{:S(2)}) async-start(bf16[16,64,1024]{2,1,0:T(8,128)(2,1)} %broadcast_in_dim.88), calls=%async_computation.1 | async-start | bytes 4194304 | tf_op jit(solution)/shard_map/all_to_all | solution.py:397
  196.6 3.4 %collective-permute-done.27 = bf16[1024,256]{1,0:T(8,128)(2,1)} collective-permute-done((bf16[1024,256]{1,0:T(8,128)(2,1)}, bf16[1024,256]{1,0:T(8,128)(2,1)}, u32[]{:S(2)}, u32[]{:S(2)}) %collective-permute-start.27) | collective-permute-done | bytes 524320 | tf_op jit(solution)/shard_map/ppermute | solution.py:36
  201.2 2.8 %collective-permute-start.28 = (bf16[1024,256]{1,0:T(8,128)(2,1)S(1)}, bf16[1024,256]{1,0:T(8,128)(2,1)S(1)}, u32[]{:S(2)}, u32[]{:S(2)}) collective-permute-start(bf16[1024,256]{1,0:T(8,128)(2,1)S(1)} %add_convert_fusion.1), channel_id=1, source_target_pairs={{0,16},{1,49},{16,32},{17,1},{32,48},{33,17},{48,0},{49,33},{2,18}... | collective-permute-start | bytes 1572872 | tf_op jit(solution)/shard_map/ppermute | solution.py:36
  205.2 3.8 %collective-permute-start.21 = (bf16[1024,256]{1,0:T(8,128)(2,1)S(1)}, bf16[1024,256]{1,0:T(8,128)(2,1)S(1)}, u32[]{:S(2)}, u32[]{:S(2)}) collective-permute-start(bf16[1024,256]{1,0:T(8,128)(2,1)S(1)} %add_convert_fusion.6), channel_id=1, source_target_pairs={{0,16},{1,49},{16,32},{17,1},{32,48},{33,17},{48,0},{49,33},{2,18}... | collective-permute-start | bytes 1572872 | tf_op jit(solution)/shard_map/ppermute | solution.py:36
  211.1 5.2 %collective-permute-start.38 = (bf16[2,64,1024]{2,1,0:T(8,128)(2,1)S(1)}, bf16[2,64,1024]{2,1,0:T(8,128)(2,1)S(1)}, u32[]{:S(2)}, u32[]{:S(2)}) collective-permute-start(bf16[2,64,1024]{2,1,0:T(8,128)(2,1)S(1)} %pad_maximum_fusion), channel_id=1, source_target_pairs={{0,16},{16,32},{32,48},{48,0},{1,17},{17,33},{33,49},{49,1},{2,18}... | collective-permute-start | bytes 786440 | tf_op jit(solution)/shard_map/ppermute | solution.py:26
  216.4 2.5 collective-permute-start.37
  219.1 2.7 %collective-permute-start.36 = (bf16[2,64,1024]{2,1,0:T(8,128)(2,1)S(1)}, bf16[2,64,1024]{2,1,0:T(8,128)(2,1)S(1)}, u32[]{:S(2)}, u32[]{:S(2)}) collective-permute-start(bf16[2,64,1024]{2,1,0:T(8,128)(2,1)S(1)} %pad_maximum_fusion), channel_id=1, source_target_pairs={{0,48},{16,0},{32,16},{48,32},{1,49},{17,1},{33,17},{49,33},{2,50}... | collective-permute-start | bytes 786440 | tf_op jit(solution)/shard_map/ppermute | solution.py:26
  221.9 3.7 %collective-permute-start.19 = (bf16[1024,256]{1,0:T(8,128)(2,1)S(1)}, bf16[1024,256]{1,0:T(8,128)(2,1)S(1)}, u32[]{:S(2)}, u32[]{:S(2)}) collective-permute-start(bf16[1024,256]{1,0:T(8,128)(2,1)S(1)} %add_convert_fusion.8), channel_id=1, source_target_pairs={{0,16},{1,49},{16,32},{17,1},{32,48},{33,17},{48,0},{49,33},{2,18}... | collective-permute-start | bytes 1572872 | tf_op jit(solution)/shard_map/ppermute | solution.py:36
  225.8 2.2 collective-permute-done.25
  229.4 3.5 %collective-permute-done.36 = bf16[2,64,1024]{2,1,0:T(8,128)(2,1)S(1)} collective-permute-done((bf16[2,64,1024]{2,1,0:T(8,128)(2,1)S(1)}, bf16[2,64,1024]{2,1,0:T(8,128)(2,1)S(1)}, u32[]{:S(2)}, u32[]{:S(2)}) %collective-permute-start.36) | collective-permute-done | bytes 262176 | tf_op jit(solution)/shard_map/ppermute | solution.py:26
  233.8 2.4 collective-permute-done.37
  239.3 5.0 %collective-permute-done.22 = bf16[1024,256]{1,0:T(8,128)(2,1)S(1)} collective-permute-done((bf16[1024,256]{1,0:T(8,128)(2,1)S(1)}, bf16[1024,256]{1,0:T(8,128)(2,1)S(1)}, u32[]{:S(2)}, u32[]{:S(2)}) %collective-permute-start.22) | collective-permute-done | bytes 524320 | tf_op jit(solution)/shard_map/ppermute | solution.py:26
  244.9 9.9 %collective-permute-done.29 = bf16[1024,256]{1,0:T(8,128)(2,1)S(1)} collective-permute-done((bf16[1024,256]{1,0:T(8,128)(2,1)S(1)}, bf16[1024,256]{1,0:T(8,128)(2,1)S(1)}, u32[]{:S(2)}, u32[]{:S(2)}) %collective-permute-start.29) | collective-permute-done | bytes 524320 | tf_op jit(solution)/shard_map/ppermute | solution.py:26
  255.9 3.3 %broadcast_select_fusion.1 = (bf16[16,64,1024]{2,1,0:T(8,128)(2,1)}, bf16[16,64,1024]{2,1,0:T(8,128)(2,1)S(1)}) fusion(bf16[16,64,1024]{2,1,0:T(8,128)(2,1)} %all-to-all-done.1, pred[]{:T(512)} %bitcast.24, pred[16]{0:T(512)(128)(4,1)S(1)} %broadcast_in_dim.85), kind=kLoop, calls=%fused_computation.5 | loop fusion | flops 2097152 | bytes 6291473 | tf_op jit(solution)/shard_map/jit(_where)/select_n | solution.py:409
  (143 shorter events, 51.3 us)
Async XLA Ops:
  7.2 21.5 %collective-permute-start.3 = (bf16[384,2048]{1,0:T(8,128)(2,1)}, bf16[384,2048]{1,0:T(8,128)(2,1)}, u32[]{:S(2)}, u32[]{:S(2)}) collective-permute-start(bf16[384,2048]{1,0:T(8,128)(2,1)} %shard_map.86.refs_0_), channel_id=1, source_target_pairs={{0,1},{1,0},{2,3},{3,2},{4,5},{5,4},{6,7},{7,6},{8,9},{9,8},{10,11... | collective-permute-start | bytes 4718600 | tf_op jit(solution)/shard_map/ppermute | solution.py:26
  7.3 37.3 %collective-permute-start.2 = (bf16[384,2048]{1,0:T(8,128)(2,1)}, bf16[384,2048]{1,0:T(8,128)(2,1)}, u32[]{:S(2)}, u32[]{:S(2)}) collective-permute-start(bf16[384,2048]{1,0:T(8,128)(2,1)} %shard_map.86.refs_0_), channel_id=1, source_target_pairs={{0,2},{2,0},{1,3},{3,1},{4,6},{6,4},{5,7},{7,5},{8,10},{10,8},{9,1... | collective-permute-start | bytes 4718600 | tf_op jit(solution)/shard_map/ppermute | solution.py:26
  9.2 37.3 %collective-permute-start.1 = (bf16[384,2048]{1,0:T(8,128)(2,1)}, bf16[384,2048]{1,0:T(8,128)(2,1)}, u32[]{:S(2)}, u32[]{:S(2)}) collective-permute-start(bf16[384,2048]{1,0:T(8,128)(2,1)} %shard_map.86.refs_0_), channel_id=1, source_target_pairs={{0,12},{1,5},{4,0},{5,9},{8,4},{9,13},{12,8},{13,1},{2,14},{3,7},{... | collective-permute-start | bytes 4718600 | tf_op jit(solution)/shard_map/ppermute | solution.py:36
  9.8 36.7 %collective-permute-start = (bf16[384,2048]{1,0:T(8,128)(2,1)}, bf16[384,2048]{1,0:T(8,128)(2,1)}, u32[]{:S(2)}, u32[]{:S(2)}) collective-permute-start(bf16[384,2048]{1,0:T(8,128)(2,1)} %shard_map.86.refs_0_), channel_id=1, source_target_pairs={{0,4},{1,13},{4,8},{5,1},{8,12},{9,5},{12,0},{13,9},{2,6},{3,15},{... | collective-permute-start | bytes 4718600 | tf_op jit(solution)/shard_map/ppermute | solution.py:36
  46.7 36.6 %collective-permute-start.6 = (bf16[384,2048]{1,0:T(8,128)(2,1)}, bf16[384,2048]{1,0:T(8,128)(2,1)}, u32[]{:S(2)}, u32[]{:S(2)}) collective-permute-start(bf16[384,2048]{1,0:T(8,128)(2,1)} %collective-permute-done.2.refs_3_), channel_id=1, source_target_pairs={{0,12},{1,5},{4,0},{5,9},{8,4},{9,13},{12,8},{13,1},{2,14},{3,7},{... | collective-permute-start | bytes 4718600 | tf_op jit(solution)/shard_map/ppermute | solution.py:36
  47.8 35.4 %collective-permute-start.8 = (bf16[384,2048]{1,0:T(8,128)(2,1)}, bf16[384,2048]{1,0:T(8,128)(2,1)}, u32[]{:S(2)}, u32[]{:S(2)}) collective-permute-start(bf16[384,2048]{1,0:T(8,128)(2,1)} %collective-permute-done.refs_1_), channel_id=1, source_target_pairs={{0,1},{1,0},{2,3},{3,2},{4,5},{5,4},{6,7},{7,6},{8,9},{9,8},{10,11... | collective-permute-start | bytes 4718600 | tf_op jit(solution)/shard_map/ppermute | solution.py:26
  48.5 36.6 %collective-permute-start.7 = (bf16[384,2048]{1,0:T(8,128)(2,1)}, bf16[384,2048]{1,0:T(8,128)(2,1)}, u32[]{:S(2)}, u32[]{:S(2)}) collective-permute-start(bf16[384,2048]{1,0:T(8,128)(2,1)} %collective-permute-done.refs_1_), channel_id=1, source_target_pairs={{0,2},{2,0},{1,3},{3,1},{4,6},{6,4},{5,7},{7,5},{8,10},{10,8},{9,1... | collective-permute-start | bytes 4718600 | tf_op jit(solution)/shard_map/ppermute | solution.py:26
  48.5 36.6 %collective-permute-start.5 = (bf16[384,2048]{1,0:T(8,128)(2,1)}, bf16[384,2048]{1,0:T(8,128)(2,1)}, u32[]{:S(2)}, u32[]{:S(2)}) collective-permute-start(bf16[384,2048]{1,0:T(8,128)(2,1)} %collective-permute-done.refs_1_), channel_id=1, source_target_pairs={{0,4},{1,13},{4,8},{5,1},{8,12},{9,5},{12,0},{13,9},{2,6},{3,15},{... | collective-permute-start | bytes 4718600 | tf_op jit(solution)/shard_map/ppermute | solution.py:36
  85.1 21.5 %collective-permute-start.10 = (bf16[384,2048]{1,0:T(8,128)(2,1)}, bf16[384,2048]{1,0:T(8,128)(2,1)}, u32[]{:S(2)}, u32[]{:S(2)}) collective-permute-start(bf16[384,2048]{1,0:T(8,128)(2,1)} %collective-permute-done.7.refs_6_), channel_id=1, source_target_pairs={{0,4},{1,13},{4,8},{5,1},{8,12},{9,5},{12,0},{13,9},{2,6},{3,15},{... | collective-permute-start | bytes 4718600 | tf_op jit(solution)/shard_map/ppermute | solution.py:36
  87.0 20.7 %collective-permute-start.11 = (bf16[384,2048]{1,0:T(8,128)(2,1)}, bf16[384,2048]{1,0:T(8,128)(2,1)}, u32[]{:S(2)}, u32[]{:S(2)}) collective-permute-start(bf16[384,2048]{1,0:T(8,128)(2,1)} %collective-permute-done.2.refs_3_), channel_id=1, source_target_pairs={{0,1},{1,0},{2,3},{3,2},{4,5},{5,4},{6,7},{7,6},{8,9},{9,8},{10,11... | collective-permute-start | bytes 4718600 | tf_op jit(solution)/shard_map/ppermute | solution.py:26
  87.3 20.4 %collective-permute-start.14 = (bf16[384,2048]{1,0:T(8,128)(2,1)}, bf16[384,2048]{1,0:T(8,128)(2,1)}, u32[]{:S(2)}, u32[]{:S(2)}) collective-permute-start(bf16[384,2048]{1,0:T(8,128)(2,1)} %collective-permute-done.7.refs_6_), channel_id=1, source_target_pairs={{0,1},{1,0},{2,3},{3,2},{4,5},{5,4},{6,7},{7,6},{8,9},{9,8},{10,11... | collective-permute-start | bytes 4718600 | tf_op jit(solution)/shard_map/ppermute | solution.py:26
  87.5 20.2 %collective-permute-start.12 = (bf16[384,2048]{1,0:T(8,128)(2,1)}, bf16[384,2048]{1,0:T(8,128)(2,1)}, u32[]{:S(2)}, u32[]{:S(2)}) collective-permute-start(bf16[384,2048]{1,0:T(8,128)(2,1)} %collective-permute-done.5.refs_4_), channel_id=1, source_target_pairs={{0,1},{1,0},{2,3},{3,2},{4,5},{5,4},{6,7},{7,6},{8,9},{9,8},{10,11... | collective-permute-start | bytes 4718600 | tf_op jit(solution)/shard_map/ppermute | solution.py:26
  87.8 19.9 %collective-permute-start.13 = (bf16[384,2048]{1,0:T(8,128)(2,1)}, bf16[384,2048]{1,0:T(8,128)(2,1)}, u32[]{:S(2)}, u32[]{:S(2)}) collective-permute-start(bf16[384,2048]{1,0:T(8,128)(2,1)} %collective-permute-done.6.refs_5_), channel_id=1, source_target_pairs={{0,1},{1,0},{2,3},{3,2},{4,5},{5,4},{6,7},{7,6},{8,9},{9,8},{10,11... | collective-permute-start | bytes 4718600 | tf_op jit(solution)/shard_map/ppermute | solution.py:26
  116.7 36.0 %all-to-all-start = ((bf16[8,64,1024]{2,1,0:T(8,128)(2,1)}), bf16[8,64,1024]{2,1,0:T(8,128)(2,1)S(1)}, u32[]{:S(2)}, u32[]{:S(2)}) async-start(bf16[8,64,1024]{2,1,0:T(8,128)(2,1)} %bitcast.57), calls=%async_computation | async-start | bytes 2097152 | tf_op jit(solution)/shard_map/all_to_all | solution.py:354
  124.7 26.9 %collective-permute-start.30 = (bf16[2,64,1024]{2,1,0:T(8,128)(2,1)}, bf16[2,64,1024]{2,1,0:T(8,128)(2,1)S(1)}, u32[]{:S(2)}, u32[]{:S(2)}) collective-permute-start(bf16[2,64,1024]{2,1,0:T(8,128)(2,1)} %get-tuple-element.118), channel_id=1, source_target_pairs={{0,4},{4,8},{8,12},{12,0},{1,5},{5,9},{9,13},{13,1},{2,6},{6,10},{... | collective-permute-start | bytes 786440 | tf_op jit(solution)/shard_map/ppermute | solution.py:26
  125.9 25.8 %collective-permute-start.31 = (bf16[2,64,1024]{2,1,0:T(8,128)(2,1)}, bf16[2,64,1024]{2,1,0:T(8,128)(2,1)}, u32[]{:S(2)}, u32[]{:S(2)}) collective-permute-start(bf16[2,64,1024]{2,1,0:T(8,128)(2,1)} %get-tuple-element.120), channel_id=1, source_target_pairs={{0,12},{4,0},{8,4},{12,8},{1,13},{5,1},{9,5},{13,9},{2,14},{6,2},{... | collective-permute-start | bytes 786440 | tf_op jit(solution)/shard_map/ppermute | solution.py:26
  128.4 23.2 %collective-permute-start.32 = (bf16[2,64,1024]{2,1,0:T(8,128)(2,1)S(1)}, bf16[2,64,1024]{2,1,0:T(8,128)(2,1)}, u32[]{:S(2)}, u32[]{:S(2)}) collective-permute-start(bf16[2,64,1024]{2,1,0:T(8,128)(2,1)S(1)} %get-tuple-element.122), channel_id=1, source_target_pairs={{0,8},{4,12},{8,0},{12,4},{1,9},{5,13},{9,1},{13,5},{2,10},{6,14},... | collective-permute-start | bytes 786440 | tf_op jit(solution)/shard_map/ppermute | solution.py:26
  155.4 16.6 %collective-permute-start.23 = (bf16[1024,256]{1,0:T(8,128)(2,1)}, bf16[1024,256]{1,0:T(8,128)(2,1)S(1)}, u32[]{:S(2)}, u32[]{:S(2)}) collective-permute-start(bf16[1024,256]{1,0:T(8,128)(2,1)} %get-tuple-element.109), channel_id=1, source_target_pairs={{0,16},{1,49},{16,32},{17,1},{32,48},{33,17},{48,0},{49,33},{2,18}... | collective-permute-start | bytes 1572872 | tf_op jit(solution)/shard_map/ppermute | solution.py:36
  162.4 15.0 %collective-permute-start.34 = (bf16[64,1024]{1,0:T(8,128)(2,1)S(1)}, bf16[64,1024]{1,0:T(8,128)(2,1)S(1)}, u32[]{:S(2)}, u32[]{:S(2)}) collective-permute-start(bf16[64,1024]{1,0:T(8,128)(2,1)S(1)} %get-tuple-element.123), channel_id=1, source_target_pairs={{0,0},{1,16},{2,32},{3,48},{4,64},{5,80},{6,96},{7,112},{8,1},{9,1... | collective-permute-start | bytes 393224 | tf_op jit(solution)/shard_map/ppermute | solution.py:389
  168.4 25.0 %collective-permute-start.17 = (bf16[1024,256]{1,0:T(8,128)(2,1)}, bf16[1024,256]{1,0:T(8,128)(2,1)}, u32[]{:S(2)}, u32[]{:S(2)}) collective-permute-start(bf16[1024,256]{1,0:T(8,128)(2,1)} %get-tuple-element.101), channel_id=1, source_target_pairs={{0,16},{1,49},{16,32},{17,1},{32,48},{33,17},{48,0},{49,33},{2,18}... | collective-permute-start | bytes 1572872 | tf_op jit(solution)/shard_map/ppermute | solution.py:36
  169.6 34.5 %collective-permute-start.20 = (bf16[1024,256]{1,0:T(8,128)(2,1)}, bf16[1024,256]{1,0:T(8,128)(2,1)}, u32[]{:S(2)}, u32[]{:S(2)}) collective-permute-start(bf16[1024,256]{1,0:T(8,128)(2,1)} %add_convert_fusion.7), channel_id=1, source_target_pairs={{0,16},{1,49},{16,32},{17,1},{32,48},{33,17},{48,0},{49,33},{2,18}... | collective-permute-start | bytes 1572872 | tf_op jit(solution)/shard_map/ppermute | solution.py:36
  172.0 37.0 %collective-permute-start.24 = (bf16[1024,256]{1,0:T(8,128)(2,1)}, bf16[1024,256]{1,0:T(8,128)(2,1)}, u32[]{:S(2)}, u32[]{:S(2)}) collective-permute-start(bf16[1024,256]{1,0:T(8,128)(2,1)} %get-tuple-element.110), channel_id=1, source_target_pairs={{0,16},{1,49},{16,32},{17,1},{32,48},{33,17},{48,0},{49,33},{2,18}... | collective-permute-start | bytes 1572872 | tf_op jit(solution)/shard_map/ppermute | solution.py:36
  178.4 21.6 %collective-permute-start.27 = (bf16[1024,256]{1,0:T(8,128)(2,1)}, bf16[1024,256]{1,0:T(8,128)(2,1)}, u32[]{:S(2)}, u32[]{:S(2)}) collective-permute-start(bf16[1024,256]{1,0:T(8,128)(2,1)} %add_convert_fusion.2), channel_id=1, source_target_pairs={{0,16},{1,49},{16,32},{17,1},{32,48},{33,17},{48,0},{49,33},{2,18}... | collective-permute-start | bytes 1572872 | tf_op jit(solution)/shard_map/ppermute | solution.py:36
  185.8 70.1 %all-to-all-start.1 = ((bf16[16,64,1024]{2,1,0:T(8,128)(2,1)}), bf16[16,64,1024]{2,1,0:T(8,128)(2,1)}, u32[]{:S(2)}, u32[]{:S(2)}) async-start(bf16[16,64,1024]{2,1,0:T(8,128)(2,1)} %broadcast_in_dim.88), calls=%async_computation.1 | async-start | bytes 4194304 | tf_op jit(solution)/shard_map/all_to_all | solution.py:397
  194.7 24.4 %collective-permute-start.18 = (bf16[1024,256]{1,0:T(8,128)(2,1)S(1)}, bf16[1024,256]{1,0:T(8,128)(2,1)S(1)}, u32[]{:S(2)}, u32[]{:S(2)}) collective-permute-start(bf16[1024,256]{1,0:T(8,128)(2,1)S(1)} %add_convert_fusion.9), channel_id=1, source_target_pairs={{0,16},{1,49},{16,32},{17,1},{32,48},{33,17},{48,0},{49,33},{2,18}... | collective-permute-start | bytes 1572872 | tf_op jit(solution)/shard_map/ppermute | solution.py:36
  205.2 16.7 %collective-permute-start.21 = (bf16[1024,256]{1,0:T(8,128)(2,1)S(1)}, bf16[1024,256]{1,0:T(8,128)(2,1)S(1)}, u32[]{:S(2)}, u32[]{:S(2)}) collective-permute-start(bf16[1024,256]{1,0:T(8,128)(2,1)S(1)} %add_convert_fusion.6), channel_id=1, source_target_pairs={{0,16},{1,49},{16,32},{17,1},{32,48},{33,17},{48,0},{49,33},{2,18}... | collective-permute-start | bytes 1572872 | tf_op jit(solution)/shard_map/ppermute | solution.py:36
  210.2 17.8 %collective-permute-start.25 = (bf16[1024,256]{1,0:T(8,128)(2,1)S(1)}, bf16[1024,256]{1,0:T(8,128)(2,1)S(1)}, u32[]{:S(2)}, u32[]{:S(2)}) collective-permute-start(bf16[1024,256]{1,0:T(8,128)(2,1)S(1)} %add_convert_fusion.4), channel_id=1, source_target_pairs={{0,16},{1,49},{16,32},{17,1},{32,48},{33,17},{48,0},{49,33},{2,18}... | collective-permute-start | bytes 1572872 | tf_op jit(solution)/shard_map/ppermute | solution.py:36
  211.1 25.2 %collective-permute-start.38 = (bf16[2,64,1024]{2,1,0:T(8,128)(2,1)S(1)}, bf16[2,64,1024]{2,1,0:T(8,128)(2,1)S(1)}, u32[]{:S(2)}, u32[]{:S(2)}) collective-permute-start(bf16[2,64,1024]{2,1,0:T(8,128)(2,1)S(1)} %pad_maximum_fusion), channel_id=1, source_target_pairs={{0,16},{16,32},{32,48},{48,0},{1,17},{17,33},{33,49},{49,1},{2,18}... | collective-permute-start | bytes 786440 | tf_op jit(solution)/shard_map/ppermute | solution.py:26
  216.4 19.9 %collective-permute-start.37 = (bf16[2,64,1024]{2,1,0:T(8,128)(2,1)S(1)}, bf16[2,64,1024]{2,1,0:T(8,128)(2,1)S(1)}, u32[]{:S(2)}, u32[]{:S(2)}) collective-permute-start(bf16[2,64,1024]{2,1,0:T(8,128)(2,1)S(1)} %pad_maximum_fusion), channel_id=1, source_target_pairs={{0,32},{16,48},{32,0},{48,16},{1,33},{17,49},{33,1},{49,17},{2,34}... | collective-permute-start | bytes 786440 | tf_op jit(solution)/shard_map/ppermute | solution.py:26
  221.9 17.4 %collective-permute-start.19 = (bf16[1024,256]{1,0:T(8,128)(2,1)S(1)}, bf16[1024,256]{1,0:T(8,128)(2,1)S(1)}, u32[]{:S(2)}, u32[]{:S(2)}) collective-permute-start(bf16[1024,256]{1,0:T(8,128)(2,1)S(1)} %add_convert_fusion.8), channel_id=1, source_target_pairs={{0,16},{1,49},{16,32},{17,1},{32,48},{33,17},{48,0},{49,33},{2,18}... | collective-permute-start | bytes 1572872 | tf_op jit(solution)/shard_map/ppermute | solution.py:36
  228.0 16.3 %collective-permute-start.22 = (bf16[1024,256]{1,0:T(8,128)(2,1)S(1)}, bf16[1024,256]{1,0:T(8,128)(2,1)S(1)}, u32[]{:S(2)}, u32[]{:S(2)}) collective-permute-start(bf16[1024,256]{1,0:T(8,128)(2,1)S(1)} %add_convert_fusion.5), channel_id=1, source_target_pairs={{0,64},{64,0},{1,65},{65,1},{2,66},{66,2},{3,67},{67,3},{4,68},{68... | collective-permute-start | bytes 1572872 | tf_op jit(solution)/shard_map/ppermute | solution.py:26
  236.3 18.5 %collective-permute-start.29 = (bf16[1024,256]{1,0:T(8,128)(2,1)S(1)}, bf16[1024,256]{1,0:T(8,128)(2,1)S(1)}, u32[]{:S(2)}, u32[]{:S(2)}) collective-permute-start(bf16[1024,256]{1,0:T(8,128)(2,1)S(1)} %add_convert_fusion), channel_id=1, source_target_pairs={{0,64},{64,0},{1,65},{65,1},{2,66},{66,2},{3,67},{67,3},{4,68},{68... | collective-permute-start | bytes 1572872 | tf_op jit(solution)/shard_map/ppermute | solution.py:26
  (28 other events, 476.7 us)
